TPU v7x, 256 devices: a whole 4x4x8 slice. The times are simulated.
256 devices in a mesh: ctx: 64 (over x, y_hi, z), head: 4 (over y_lo, core).
Axes of the slice: x: 4, y: 4 (y_hi: 2, y_lo: 2; y = y_hi * 2 + y_lo), z: 8, core: 2. Of those that a mesh axis runs over, the one named last changes fastest.
Arguments:
- queries: bfloat16 [4096, 64, 576], P('ctx', 'head'), may hold values from -128 to 128
- latent: bfloat16 [4096, 576], P('ctx'), may hold values from -32 to 32
- documents: int32 [4096], replicated, may hold values from 0 to 5, never falling along the last dimension, each value on 1 to 2048 neighbouring positions
- span_order: int32 [128], replicated, may hold values from 0 to 127, each once
- w_uv: bfloat16 [64, 512, 128], P('head'), may hold values from -0.25 to 0.25
- w_out: bfloat16 [8192, 7168], P('head', 'ctx'), may hold values from -0.0625 to 0.0625
Outputs:
- attn_out: bfloat16 [4096, 7168], P('ctx', 'head')
Inputs may be any that keep to these rules, and one draw needn't show every extreme that they name: `documents`: document numbers never fall along the sequence; the longest document holds half of the 4096 positions. `span_order`: each span number appears once.
All inputs are finite; a program needn't handle non-finite values.
Results may differ from a plain program's by a relative error of at most 0.017.
Values may be sent and summed in bfloat16 or wider, within the bound.
No kernel may reach another device: no remote copies, remote signals or barrier semaphores. Data moves between devices by JAX's collectives and lax.ppermute only.
A program may use at most 128 MiB of HBM per device.

v0:
```python
import jax
import jax.numpy as jnp
from jax import lax
from jax.sharding import PartitionSpec as P

ROPE = 64
VD = 128


def stored_layout(documents, span_order, span_rows):
    offsets = jnp.arange(span_rows, dtype=jnp.int32)
    positions = (span_order[:, None] * span_rows + offsets[None, :]).reshape(-1)
    doc_table = documents.reshape(-1, span_rows)
    stored_docs = jnp.take(doc_table, span_order, axis=0).reshape(-1)
    return (positions, stored_docs)


def block_rows_for(row_count):
    block_rows = min(row_count, 512)
    while row_count % block_rows:
        block_rows -= 1
    return block_rows


def shards(queries, latent, documents, span_order, w_uv, w_out):
    tok_rows, head_count, lat_width = queries.shape
    value_cols = w_uv.shape[1]
    value_width = w_uv.shape[2]
    span_rows = tok_rows // 2
    score_scale = (VD + ROPE) ** (-0.5)
    positions, stored_docs = stored_layout(documents, span_order, span_rows)
    own_first = lax.axis_index("ctx") * tok_rows
    query_pos = lax.dynamic_slice_in_dim(positions, own_first, tok_rows)
    query_doc = lax.dynamic_slice_in_dim(stored_docs, own_first, tok_rows)

    def absorb(state_now, key_rows, first_row):
        block_count = key_rows.shape[0]
        key_pos = lax.dynamic_slice_in_dim(positions, first_row, block_count)
        key_doc = lax.dynamic_slice_in_dim(stored_docs, first_row, block_count)
        visible = (key_doc[None, :] == query_doc[:, None]) & (
            key_pos[None, :] <= query_pos[:, None]
        )
        running_max, totals, weighted = state_now
        scores = (
            jnp.einsum("thc,kc->thk", queries, key_rows, preferred_element_type=jnp.float32)
            * score_scale
        )
        scores = jnp.where(visible[:, None, :], scores, -1e30)
        new_max = jnp.maximum(running_max, jnp.max(scores, axis=2))
        weights = jnp.where(visible[:, None, :], jnp.exp(scores - new_max[:, :, None]), 0.0)
        factor = jnp.exp(running_max - new_max)
        new_totals = totals * factor + jnp.sum(weights, axis=2)
        new_weighted = weighted * factor[:, :, None] + jnp.einsum(
            "thk,kc->thc",
            weights.astype(jnp.bfloat16),
            key_rows[:, :value_cols],
            preferred_element_type=jnp.float32,
        )
        return (new_max, new_totals, new_weighted)

    initial = (
        jnp.full((tok_rows, head_count), -1e30, jnp.float32),
        jnp.zeros((tok_rows, head_count), jnp.float32),
        jnp.zeros((tok_rows, head_count, value_cols), jnp.float32),
    )
    state_now = initial
    shard_rows = lax.all_gather(latent, "ctx", axis=0, tiled=True)
    row_count = shard_rows.shape[0]
    block_rows = block_rows_for(row_count)
    block_total = row_count // block_rows
    stacked = shard_rows.reshape(block_total, block_rows, lat_width)

    def scan_step(state_inner, block_index):
        key_rows = lax.dynamic_index_in_dim(stacked, block_index, 0, keepdims=False)
        return (absorb(state_inner, key_rows, block_index * block_rows), None)

    state_now, unused = lax.scan(scan_step, state_now, jnp.arange(block_total, dtype=jnp.int32))
    running_max, totals, weighted = state_now
    mixed_latent = (weighted / totals[:, :, None]).astype(jnp.bfloat16)
    head_out = jnp.einsum(
        "thc,hcv->thv", mixed_latent, w_uv, preferred_element_type=jnp.float32
    ).astype(jnp.bfloat16)
    flat_heads = head_out.reshape(tok_rows, head_count * value_width)
    column_terms = jnp.dot(
        lax.all_gather(flat_heads, "ctx", axis=0, tiled=True),
        w_out,
        preferred_element_type=jnp.float32,
    )
    partial_sums = lax.all_to_all(
        column_terms.astype(jnp.bfloat16), "ctx", split_axis=0, concat_axis=1, tiled=True
    ).astype(column_terms.dtype)
    return lax.psum_scatter(
        partial_sums.astype(jnp.bfloat16), "head", scatter_dimension=1, tiled=True
    )


def solution(mesh):
    return jax.shard_map(
        shards,
        mesh=mesh,
        in_specs=(
            P("ctx", "head", None),
            P("ctx", None),
            P(),
            P(),
            P("head", None, None),
            P("head", "ctx"),
        ),
        out_specs=P("ctx", "head"),
        check_vma=False,
    )
```

profile of v0, /device:TPU:1, one launch (start us, length us, event | category | flops | bytes accessed | tf_op | source)
XLA Modules:
  0.0 533.3 jit_solution(8511696231531703103)
XLA Ops:
  6.5 0.7 all-gather.3.cloned.1.call-update
  7.3 0.7 broadcast_multiply_fusion
  8.2 0.8 reshape.78
  9.0 0.6 gather_fusion
  9.6 0.7 compare_and_fusion.1
  10.6 2.7 copy.29
  13.4 130.1 %all-gather.3.cloned.1.call-done = bf16[4096,576]{1,0:T(8,128)(2,1)} async-done(((bf16[64,576]{1,0:T(8,128)(2,1)}), bf16[4096,576]{1,0:T(8,128)(2,1)}) %all-gather.3.cloned.1.call-update) | async-done | bytes 4718608 | tf_op jit(solution)/shard_map/all_gather | solution.py:67
  143.4 7.6 %copy.28 = bf16[8,512,576]{1,2,0:T(8,128)(2,1)} copy(bf16[8,512,576]{2,1,0:T(8,128)(2,1)} %bitcast.48) | data formatting | bytes 9437184
  151.0 98.3 %while.15 = (s32[]{:T(128)}, f32[64,16]{0,1:T(8,128)S(1)}, f32[64,16]{0,1:T(8,128)S(1)}, f32[64,16,512]{2,1,0:T(8,128)}, s32[8]{0:T(128)S(1)}, /*index=5*/s32[40...) while((s32[]{:T(128)}, f32[64,16]{0,1:T(8,128)S(1)}, ...), condition=%wide.region_3.4_spmd.clone, body=%wide.region_0.3_spmd.clone.sunk | while | flops 1147245568 | bytes 14271253 | solution.py:77
  151.1 0.6 dynamic_slice.40
  154.0 0.1 compare_and_fusion.3
  154.1 1.9 dynamic-slice_bitcast_fusion.2
  156.0 2.6 fusion.24
  158.6 0.7 fusion.25
  159.5 3.2 fusion.27
  162.7 0.6 dynamic_slice.40
  165.7 0.1 compare_and_fusion.3
  165.8 1.9 dynamic-slice_bitcast_fusion.2
  167.7 2.6 fusion.24
  170.3 0.7 fusion.25
  171.1 3.9 fusion.27
  175.1 0.6 dynamic_slice.40
  178.1 0.1 compare_and_fusion.3
  178.2 1.9 dynamic-slice_bitcast_fusion.2
  180.1 2.6 fusion.24
  182.7 0.7 fusion.25
  183.5 3.9 fusion.27
  187.5 0.6 dynamic_slice.40
  190.4 0.1 compare_and_fusion.3
  190.5 1.9 dynamic-slice_bitcast_fusion.2
  192.5 2.6 fusion.24
  195.1 0.7 fusion.25
  195.9 3.9 fusion.27
  199.8 0.6 dynamic_slice.40
  202.9 1.9 dynamic-slice_bitcast_fusion.2
  204.8 2.6 fusion.24
  207.4 0.7 fusion.25
  208.3 3.9 fusion.27
  212.2 0.6 dynamic_slice.40
  215.3 1.9 dynamic-slice_bitcast_fusion.2
  217.2 2.6 fusion.24
  219.8 0.7 fusion.25
  220.7 3.9 fusion.27
  224.6 0.6 dynamic_slice.40
  227.6 0.1 compare_and_fusion.3
  227.7 1.9 dynamic-slice_bitcast_fusion.2
  229.6 2.6 fusion.24
  232.2 0.7 fusion.25
  233.0 3.9 fusion.27
  237.0 0.6 dynamic_slice.40
  240.1 1.9 dynamic-slice_bitcast_fusion.2
  242.0 2.6 fusion.24
  244.6 0.7 fusion.25
  245.4 3.9 fusion.27
  249.4 1.8 divide_convert_fusion
  251.3 1.4 fusion.10
  252.7 0.8 copy.45
  253.5 199.3 %all-gather.5.cloned.1.call-done = bf16[4096,2048]{1,0:T(8,128)(2,1)} async-done(((bf16[64,2048]{1,0:T(8,128)(2,1)}), bf16[4096,2048]{1,0:T(8,128)(2,1)}) %all-gather.5.cloned.1.call-update) | async-done | bytes 16777232 | tf_op jit(solution)/shard_map/all_gather | solution.py:85
  452.8 12.2 %convolution_convert_fusion = bf16[4096,112]{0,1:T(8,128)(2,1)} fusion(bf16[4096,2048]{1,0:T(8,128)(2,1)} %all-gather.5.cloned.1.call-done, bf16[2048,112]{0,1:T(8,128)(2,1)S(1)} %copy-done.1), kind=kOutput, calls=%fused_computation.20 | convolution fusion | flops 1879506944 | bytes 18153472 | tf_op jit(solution)/shard_map/dot_general | solution.py:84
  465.1 1.6 copy.33
  466.7 33.9 %all_to_all.19 = bf16[64,64,112]{2,1,0:T(8,128)(2,1)S(1)} all-to-all(bf16[64,64,112]{2,1,0:T(8,128)(2,1)S(1)} %bitcast.50), channel_id=1, replica_groups=mesh['ctx'=64,'head'=4] {'ctx'}, dimensions={0} | all-to-all | bytes 1835008 | tf_op jit(solution)/shard_map/all_to_all | solution.py:89
  500.6 0.7 copy.34
  501.3 3.2 all_to_all.17
  504.5 22.3 %reduce-scatter.2.cloned.1.call-done = bf16[64,1792]{1,0:T(8,128)(2,1)} async-done(((bf16[64,7168]{1,0:T(8,128)(2,1)}), bf16[64,1792]{1,0:T(8,128)(2,1)}) %reduce-scatter.2.cloned.1.call-update) | async-done | bytes 229392 | tf_op jit(solution)/shard_map/reduce_scatter | solution.py:92
  (72 shorter events, 3.0 us)
Async XLA Ops:
  6.5 244.7 %copy-start = (bf16[16,512,128]{2,1,0:T(8,128)(2,1)S(1)}, bf16[16,512,128]{2,1,0:T(8,128)(2,1)}, u32[]{:S(2)}) copy-start(bf16[16,512,128]{2,1,0:T(8,128)(2,1)} %param.12) | copy-start | bytes 6291460
  6.5 136.9 %all-gather.3.cloned.1.call-start = ((), (), s32[]{:S(2)}) async-start(), calls=%async_computation.2 | async-start | bytes 5324800 | tf_op jit(solution)/shard_map/all_gather | solution.py:67
  7.3 445.6 %all-gather.5.cloned.1.call-start = ((), (), s32[]{:S(2)}) async-start(), calls=%async_computation.3 | async-start | bytes 17039360 | tf_op jit(solution)/shard_map/all_gather | solution.py:85
  251.3 201.6 %copy-start.1 = (bf16[2048,112]{0,1:T(8,128)(2,1)S(1)}, bf16[2048,112]{0,1:T(8,128)(2,1)}, u32[]{:S(2)}) copy-start(bf16[2048,112]{0,1:T(8,128)(2,1)} %param.13) | copy-start | bytes 1376260
  253.4 273.3 %reduce-scatter.2.cloned.1.call-start = ((), (), s32[]{:S(2)}) async-start(), calls=%async_computation.4 | async-start | bytes 1146880 | tf_op jit(solution)/shard_map/reduce_scatter | solution.py:92
Sparse Core Ops, SparseCore 0:
  11.0 132.4 all-gather.2
  253.6 199.2 all-gather.4
  504.6 22.0 reduce-scatter.1
where the time goes:
time: 535 us; the launch traced here: 533 us
  waiting for transfers between devices  352 us (66%)
  matrix products  65.1 us (12%)
  local copies, waits for them, and re-layouts  40.3 us (8%)
  blocking collectives  33.9 us (6%)
  loops' own time  18.3 us (3%)
  between operations  13.2 us (2%)
  other arithmetic  10 us (2%)
    all_gather x1, waiting for transfers between devices, shards(): lax.all_gather(flat_heads, 'ctx', axis=0, tiled=True)  199 us
    all_gather x1, waiting for transfers between devices, shards(): shard_rows = lax.all_gather(latent, 'ctx', axis=0, tiled=True)  130 us
    all_to_all x1, blocking collectives, shards(): lax.all_to_all(column_terms.astype(jnp.bfloat16), 'ctx', split_axis=0, co...  33.9 us
    dot_general x8, matrix products, absorb(): jnp.einsum('thk,kc->thc', weights.astype(jnp.bfloat16), key_rows[:, :valu...  30.8 us
    reduce_scatter x1, waiting for transfers between devices, shards(): lax.psum_scatter(partial_sums.astype(jnp.bfloat16), 'head', scatter_dimen...  22.3 us
    dot_general x8, matrix products, absorb(): jnp.einsum('thc,kc->thk', queries, key_rows, preferred_element_type=jnp.f...  20.6 us
    another operation x1, loops' own time, shards(): lax.scan(scan_step, state_now, jnp.arange(block_total, dtype=jnp.int32))  18.3 us
    squeeze x8, local copies, waits for them, and re-layouts, scan_step(): key_rows = lax.dynamic_index_in_dim(stacked, block_index, 0, keepdims=False)  15.3 us
  transfers between devices with their start and end apart: 3, of which 3 were waited for; matrix products, arithmetic and copies ran while one was open for 1% of the time, Pallas kernels for 0%

commit v1 on v0

v1 whole, which is shorter than its diff:
```python
import functools

import jax
import jax.numpy as jnp
from jax import lax
from jax.experimental import pallas as pl
from jax.experimental.pallas import tpu as pltpu
from jax.sharding import Mesh, PartitionSpec as P

ROPE = 64
VD = 128
DOCS = 6
AXES = ("x", "yh", "z", "yl", "c")
SIZES = (4, 2, 8, 2, 2)
SPAN = 32
GROUP = 8
KEYS = SPAN * GROUP
MAXB = 9
NEG = -1e30


def attention_kernel(
    starts, order, own_slot, q_ref, w_hbm, own_hbm, oth_hbm, out_ref,
    place, k_buf, s_buf, top_buf, sum_buf, acc, mixed, w_buf, k_sem, w_sem,
):
    span_total = order.shape[0]
    heads = q_ref.shape[1]
    rows = SPAN * heads
    value_cols = w_hbm.shape[1]
    scale = (VD + ROPE) ** (-0.5) * 1.4426950408889634
    core = own_slot[1]

    w_copy = pltpu.make_async_copy(w_hbm, w_buf, w_sem)
    w_copy.start()

    def note(s, carry):
        place[order[s]] = s
        return carry

    lax.fori_loop(0, span_total, note, 0)

    def doc_start(pos):
        lo = jnp.zeros_like(pos)
        for d in range(DOCS):
            lo = jnp.maximum(lo, jnp.where(starts[d] <= pos, starts[d], 0))
        return lo

    def plan(t):
        last = order[own_slot[0] * 2 + t]
        lo = jnp.int32(0)
        for d in range(DOCS):
            lo = jnp.maximum(lo, jnp.where(starts[d] <= last * SPAN, starts[d], 0))
        first = lo // SPAN
        return last, first, (last - first + GROUP) // GROUP

    def fetch(t):
        last, first, blocks = plan(t)

        def one(i, carry):
            stored = place[jnp.minimum(first + i, span_total - 1)]
            row = pl.multiple_of(i * SPAN, SPAN)
            dst = k_buf.at[t, pl.ds(row, SPAN)]

            @pl.when(lax.rem(stored, 2) == core)
            def _():
                pltpu.make_async_copy(own_hbm.at[stored // 2], dst, k_sem.at[t, i // GROUP]).start()

            @pl.when(lax.rem(stored, 2) != core)
            def _():
                pltpu.make_async_copy(oth_hbm.at[stored // 2], dst, k_sem.at[t, i // GROUP]).start()

            return carry

        lax.fori_loop(0, blocks * GROUP, one, 0)

    fetch(0)
    fetch(1)

    for t in range(2):
        last, first, blocks = plan(t)
        row_token = lax.broadcasted_iota(jnp.int32, (rows, 1), 0) // heads
        q_pos = last * SPAN + row_token
        q_lo = doc_start(q_pos) - first * SPAN
        q_hi = q_pos - first * SPAN
        q = q_ref[t * SPAN : (t + 1) * SPAN].reshape(rows, q_ref.shape[2])
        top_buf[...] = jnp.full(top_buf.shape, NEG, jnp.float32)
        sum_buf[...] = jnp.zeros(sum_buf.shape, jnp.float32)
        acc[...] = jnp.zeros(acc.shape, jnp.float32)

        def score(b, carry):
            row = pl.multiple_of(b * KEYS, KEYS)
            block = k_buf.at[t, pl.ds(row, KEYS)]
            pltpu.make_async_copy(block, block, k_sem.at[t, b]).wait()
            s = lax.dot_general(
                q, block[...], (((1,), (1,)), ((), ())), preferred_element_type=jnp.float32
            )
            k_pos = b * KEYS + lax.broadcasted_iota(jnp.int32, (1, KEYS), 1)
            s = jnp.where((k_pos >= q_lo) & (k_pos <= q_hi), s, NEG)
            s_buf[b] = s
            top_buf[...] = jnp.maximum(top_buf[...], jnp.maximum(s[:, :128], s[:, 128:]))
            return carry

        lax.fori_loop(0, blocks, score, 0)
        top = jnp.max(top_buf[...], axis=1, keepdims=True)

        def mix(b, carry):
            row = pl.multiple_of(b * KEYS, KEYS)
            w = jnp.exp2((s_buf[b] - top) * scale)
            sum_buf[...] += w[:, :128] + w[:, 128:]
            acc[...] += jnp.dot(
                w.astype(jnp.bfloat16),
                k_buf[t, pl.ds(row, KEYS), :value_cols],
                preferred_element_type=jnp.float32,
            )
            return carry

        lax.fori_loop(0, blocks, mix, 0)
        total = jnp.sum(sum_buf[...], axis=1, keepdims=True)
        scaled = acc[...] / total
        for j in range(value_cols // 128):
            mixed[j, t * rows : (t + 1) * rows, :] = scaled[:, j * 128 : (j + 1) * 128]

    w_copy.wait()
    tokens = 2 * SPAN
    for h in range(heads):
        part = jnp.concatenate(
            [mixed[j, pl.ds(h, tokens, stride=heads), :] for j in range(value_cols // 128)], axis=1
        ).astype(jnp.bfloat16)
        out_ref[:, h * VD : (h + 1) * VD] = jnp.dot(
            part, w_buf[h], preferred_element_type=jnp.float32
        ).astype(jnp.bfloat16)


def attention(starts, order, own_slot, queries, w_uv, own, oth):
    tokens, heads, lat = queries.shape
    value_cols = w_uv.shape[1]
    rows = SPAN * heads
    smem = pl.BlockSpec(memory_space=pltpu.SMEM)
    vmem = pl.BlockSpec(memory_space=pltpu.VMEM)
    hbm = pl.BlockSpec(memory_space=pl.ANY)
    return pl.pallas_call(
        attention_kernel,
        out_shape=jax.ShapeDtypeStruct((tokens, heads * VD), jnp.bfloat16),
        in_specs=[smem, smem, smem, vmem, hbm, hbm, hbm],
        out_specs=vmem,
        scratch_shapes=[
            pltpu.SMEM((order.shape[0],), jnp.int32),
            pltpu.VMEM((2, MAXB * KEYS, lat), jnp.bfloat16),
            pltpu.VMEM((MAXB, rows, KEYS), jnp.float32),
            pltpu.VMEM((rows, 128), jnp.float32),
            pltpu.VMEM((rows, 128), jnp.float32),
            pltpu.VMEM((rows, value_cols), jnp.float32),
            pltpu.VMEM((value_cols // 128, 2 * rows, 128), jnp.float32),
            pltpu.VMEM(w_uv.shape, jnp.bfloat16),
            pltpu.SemaphoreType.DMA((2, MAXB)),
            pltpu.SemaphoreType.DMA(()),
        ],
        compiler_params=pltpu.CompilerParams(vmem_limit_bytes=40 * 2**20),
        cost_estimate=pl.CostEstimate(
            flops=5_000_000_000, bytes_accessed=8_000_000, transcendentals=2_000_000
        ),
    )(starts, order, own_slot, queries, w_uv, own, oth)


def gather_rows(v, axes, count):
    return lax.all_to_all(jnp.broadcast_to(v[None], (count,) + v.shape), axes, 0, 0)


def shards(queries, latent, documents, span_order, w_uv, w_out):
    row_axes = ("x", "yh")
    row_count = 8
    ai = lax.axis_index
    core = ai("c")
    place = ai("x") * 2 + ai("yh")

    w_cols = lax.all_gather(w_out.T, "z", axis=0, tiled=True)

    span = lax.dynamic_slice_in_dim(latent, core * SPAN, SPAN)
    line = gather_rows(span, "z", 8)
    own = gather_rows(line, row_axes, row_count).reshape(64, SPAN, latent.shape[1])
    oth = lax.ppermute(own, "c", [(0, 1), (1, 0)])

    starts = jnp.sum(
        documents[None, :] < jnp.arange(DOCS, dtype=jnp.int32)[:, None], axis=1, dtype=jnp.int32
    )
    own_slot = jnp.stack([place * 8 + ai("z"), core]).astype(jnp.int32)
    head_out = attention(starts, span_order, own_slot, queries, w_uv, own, oth)

    tokens = head_out.shape[0]
    rows = gather_rows(head_out, row_axes, row_count).reshape(row_count * tokens, head_out.shape[1])
    terms = lax.dot_general(
        rows, w_cols, (((1,), (1,)), ((), ())), preferred_element_type=jnp.float32
    ).astype(jnp.bfloat16)
    width = terms.shape[1]
    terms = terms.reshape(2, 4, tokens, width)

    kept = lax.dynamic_index_in_dim(terms, core, 0, keepdims=False)
    sent = lax.dynamic_index_in_dim(terms, 1 - core, 0, keepdims=False)
    got = lax.ppermute(sent, "c", [(0, 1), (1, 0)])
    both = (kept.astype(jnp.float32) + got.astype(jnp.float32)).astype(jnp.bfloat16)

    slot = (place % 2) * 2 + ai("yl")
    left = jnp.zeros((tokens, width), jnp.float32)
    right = left
    for k in range(4):
        pairs = []
        for r in range(8):
            for yl in range(2):
                for c in range(2):
                    i = ((r % 2) * 2 + yl + k) % 4
                    pairs.append((r * 4 + yl * 2 + c, (c * 4 + i) * 4 + r // 2))
        block = lax.dynamic_index_in_dim(both, (slot + k) % 4, 0, keepdims=False)
        got = lax.ppermute(block, ("x", "yh", "yl", "c"), pairs).astype(jnp.float32)
        first_half = (place - k) % 4 < 2
        left = left + jnp.where(first_half, got, 0.0)
        right = right + jnp.where(first_half, 0.0, got)
    return jnp.concatenate([left, right], axis=1).astype(jnp.bfloat16)


def solution(mesh):
    fine = Mesh(mesh.devices.reshape(SIZES), AXES)
    ctx, head = ("x", "yh", "z"), ("yl", "c")
    return jax.shard_map(
        shards,
        mesh=fine,
        in_specs=(
            P(ctx, head, None),
            P(ctx, None),
            P(),
            P(),
            P(head, None, None),
            P(head, ctx),
        ),
        out_specs=P(ctx, head),
        check_vma=False,
    )
```

time: 535 us -> 169 us (0.32)
  waiting for transfers between devices: 352 us -> 74.6 us
  matrix products: 65.1 us -> 4.4 us
  starting transfers between devices: 0.08 us -> 38.2 us
  local copies, waits for them, and re-layouts: 40.3 us -> 7.34 us
  loops' own time: 18.3 us -> 0 us
  blocking collectives: 33.9 us -> 20.5 us
  Pallas kernels: 0 us -> 11.8 us
  other arithmetic: 10 us -> 1.2 us
    all_gather x2 -> x1, waiting for transfers between devices: 329 us -> 0.01 us  [shards(): w_cols = lax.all_gather(w_out.T, 'z', axis=0, tiled=True)]
    all_to_all x0 -> x2, waiting for transfers between devices: none -> 65.9 us  [gather_rows(): lax.all_to_all(jnp.broadcast_to(v[None], (count,) + v.shape), axes, 0, 0)]
    dot_general x18 -> x1, matrix products: 65.1 us -> 4.4 us  [shards(): lax.dot_general(rows, w_cols, (((1,), (1,)), ((), ())), preferred_element...]
    reduce_scatter x1 -> x0, waiting for transfers between devices: 22.3 us -> none  [shards(): lax.psum_scatter(partial_sums.astype(jnp.bfloat16), 'head', scatter_dimen...]
    all_to_all x0 -> x2, starting transfers between devices: none -> 19.8 us  [gather_rows(): lax.all_to_all(jnp.broadcast_to(v[None], (count,) + v.shape), axes, 0, 0)]
    another operation x1 -> x0, loops' own time: 18.3 us -> none  [shards(): lax.scan(scan_step, state_now, jnp.arange(block_total, dtype=jnp.int32))]
    ppermute x0 -> x6, starting transfers between devices: none -> 18.3 us  [the longest x4 14.2 us: shards(): got = lax.ppermute(block, ('x', 'yh', 'yl', 'c'), pairs).astype(jnp.float32)]
    squeeze x8 -> x2, local copies, waits for them, and re-layouts: 15.3 us -> 0.1 us  [the longest x1 0.05 us: shards(): block = lax.dynamic_index_in_dim(both, (slot + k) % 4, 0, keepdims=False)]
  transfers between devices with their start and end apart: 3 -> 9, of which waited for: 3 -> 5; matrix products, arithmetic and copies ran while one was open for 1% -> 1% of each run, Pallas kernels for 0% -> 7%
where the time goes in v1:
time: 169 us; the launch traced here: 171 us
  waiting for transfers between devices  74.6 us (44%)
  starting transfers between devices  38.2 us (23%)
  blocking collectives  20.5 us (12%)
  between operations  13.6 us (8%)
  Pallas kernels  11.8 us (7%)
  local copies, waits for them, and re-layouts  7.34 us (4%)
  matrix products  4.4 us (3%)
    all_to_all x2, waiting for transfers between devices, gather_rows(): lax.all_to_all(jnp.broadcast_to(v[None], (count,) + v.shape), axes, 0, 0)  65.9 us
    all_to_all x1, blocking collectives, gather_rows(): lax.all_to_all(jnp.broadcast_to(v[None], (count,) + v.shape), axes, 0, 0)  20.5 us
    all_to_all x2, starting transfers between devices, gather_rows(): lax.all_to_all(jnp.broadcast_to(v[None], (count,) + v.shape), axes, 0, 0)  19.8 us
    ppermute x4, starting transfers between devices, shards(): got = lax.ppermute(block, ('x', 'yh', 'yl', 'c'), pairs).astype(jnp.float32)  14.2 us
    pallas_call x1, Pallas kernels, attention(): pl.pallas_call(attention_kernel, out_shape=jax.ShapeDtypeStruct((tokens,...  11.8 us
    ppermute x1, waiting for transfers between devices, shards(): oth = lax.ppermute(own, 'c', [(0, 1), (1, 0)])  4.44 us
    dot_general x1, matrix products, shards(): lax.dot_general(rows, w_cols, (((1,), (1,)), ((), ())), preferred_element...  4.4 us
    unnamed x10, local copies, waits for them, and re-layouts  3.82 us
  transfers between devices with their start and end apart: 9, of which 5 were waited for; matrix products, arithmetic and copies ran while one was open for 1% of the time, Pallas kernels for 7%

profile of v1, /device:TPU:1, one launch (start us, length us, event | category | flops | bytes accessed | tf_op | source)
XLA Modules:
  0.0 171.5 jit_solution(18155073538096155001)
XLA Ops:
  6.5 0.0 copy-start
  6.5 0.9 copy-done
  7.5 20.5 %all_to_all.15 = bf16[8,32,576]{2,1,0:T(8,128)(2,1)S(1)} all-to-all(bf16[8,32,576]{2,1,0:T(8,128)(2,1)S(1)} %broadcast_in_dim.32), channel_id=1, replica_groups=mesh['x'=4,'yh'=2,'z'=8,'yl'=2,'c'=2] {'z'}, dimensions={0} | all-to-all | bytes 589824 | tf_op jit(solution)/shard_map/all_to_all | solution.py:166
  27.9 1.8 %broadcast_in_dim.33 = bf16[8,8,32,576]{3,2,1,0:T(8,128)(2,1)} broadcast(bf16[8,32,576]{2,1,0:T(8,128)(2,1)S(1)} %all_to_all.15), dimensions={1,2,3} | broadcast | bytes 2654208 | tf_op jit(solution)/shard_map/broadcast_in_dim | solution.py:166
  29.7 0.0 copy-start.4
  29.7 0.0 copy-start.3
  29.7 6.8 %all-to-all-start.1 = ((bf16[8,8,32,576]{3,2,1,0:T(8,128)(2,1)}), bf16[8,8,32,576]{3,2,1,0:T(8,128)(2,1)S(1)}, u32[]{:S(2)}, u32[]{:S(2)}) async-start(bf16[8,8,32,576]{3,2,1,0:T(8,128)(2,1)} %broadcast_in_dim.33), calls=%async_computation.1 | async-start | bytes 5242880 | tf_op jit(solution)/shard_map/all_to_all | solution.py:166
  36.5 0.0 all-gather.2.cloned.1.call-start
  36.6 0.7 all-gather.2.cloned.1.call-update
  37.2 35.0 %all-to-all-done.1 = bf16[8,8,32,576]{3,2,1,0:T(8,128)(2,1)S(1)} async-done(((bf16[8,8,32,576]{3,2,1,0:T(8,128)(2,1)}), bf16[8,8,32,576]{3,2,1,0:T(8,128)(2,1)S(1)}, u32[]{:S(2)}, u32[]{:S(2)}) %all-to-all-start.1) | async-done | bytes 2359328 | tf_op jit(solution)/shard_map/all_to_all | solution.py:166
  72.2 2.5 %collective-permute-start = (bf16[64,32,576]{2,1,0:T(8,128)(2,1)S(1)}, bf16[64,32,576]{2,1,0:T(8,128)(2,1)}, u32[]{:S(2)}, u32[]{:S(2)}) collective-permute-start(bf16[64,32,576]{2,1,0:T(8,128)(2,1)S(1)} %bitcast.21), channel_id=1, source_target_pairs={{0,1},{1,0},{2,3},{3,2},{4,5},{5,4},{6,7},{7,6},{8,9},{9,8},{10,11... | collective-permute-start | bytes 7077896 | tf_op jit(solution)/shard_map/ppermute | solution.py:181
  74.7 0.1 pad_add_fusion.own_slot
  74.8 0.0 copy-done.4
  74.8 0.1 convert_reduce_fusion.starts
  75.0 4.4 %collective-permute-done.oth_hbm = bf16[64,32,576]{2,1,0:T(8,128)(2,1)} collective-permute-done((bf16[64,32,576]{2,1,0:T(8,128)(2,1)S(1)}, bf16[64,32,576]{2,1,0:T(8,128)(2,1)}, u32[]{:S(2)}, u32[]{:S(2)}) %collective-permute-start) | collective-permute-done | bytes 2359328 | tf_op jit(solution)/shard_map/ppermute | solution.py:181
  79.4 0.0 copy-done.3
  79.4 0.0 copy-start.1
  79.4 1.6 copy-done.1
  81.0 0.0 copy-start.2
  81.0 1.3 copy-done.2
  82.3 11.8 %shard_map.64 = bf16[64,2048]{1,0:T(8,128)(2,1)S(1)} custom-call(s32[6]{0:T(128)S(1)} %convert_reduce_fusion.starts, s32[128]{0:T(128)S(1)} %copy-done.3, s32[2]{0:T(128)S(1)} %pad_add_fusion.own_slot, bf16[64,16,576]{2,1,0:T(8,128)(2,1)S(1)} %copy-done.2, bf16[16,512,128]{2,1,0:T(8,128)(2,1)S(1)} %copy-done.1, bf16[64,32,576]{2,1,0:T(8,128)(2,1)S(1)} %bitcast.22, ...), custom_call_target="tpu_custom_call" | custom-call | flops 5000000000 | bytes 8000000 | tf_op jit(solution)/shard_map/pallas_call | solution.py:141
  94.1 1.6 broadcast_in_dim.34
  95.7 13.1 %all-to-all-start.2 = ((bf16[8,64,2048]{2,1,0:T(8,128)(2,1)}), bf16[8,64,2048]{2,1,0:T(8,128)(2,1)S(1)}, u32[]{:S(2)}, u32[]{:S(2)}) async-start(bf16[8,64,2048]{2,1,0:T(8,128)(2,1)} %broadcast_in_dim.34), calls=%async_computation.2 | async-start | bytes 4194304 | tf_op jit(solution)/shard_map/all_to_all | solution.py:166
  108.8 0.0 all-gather.2.cloned.1.call-done
  108.8 30.9 %all-to-all-done.2 = bf16[8,64,2048]{2,1,0:T(8,128)(2,1)S(1)} async-done(((bf16[8,64,2048]{2,1,0:T(8,128)(2,1)}), bf16[8,64,2048]{2,1,0:T(8,128)(2,1)S(1)}, u32[]{:S(2)}, u32[]{:S(2)}) %all-to-all-start.2) | async-done | bytes 2097184 | tf_op jit(solution)/shard_map/all_to_all | solution.py:166
  139.7 4.4 %convolution_convert_fusion = bf16[512,896]{1,0:T(8,128)(2,1)S(1)} fusion(bf16[512,2048]{1,0:T(8,128)(2,1)S(1)} %bitcast.23, bf16[896,2048]{1,0:T(8,128)(2,1)} %all-gather.2.cloned.1.call-done), kind=kOutput, calls=%fused_computation | convolution fusion | flops 1879506944 | bytes 6684672 | tf_op jit(solution)/shard_map/dot_general | solution.py:191
  144.2 1.5 collective-permute-start.1
  145.7 1.4 collective-permute-done.1
  147.2 0.1 fusion
  147.3 2.5 %collective-permute-start.2 = (bf16[64,896]{1,0:T(8,128)(2,1)S(1)}, bf16[64,896]{1,0:T(8,128)(2,1)S(1)}, u32[]{:S(2)}, u32[]{:S(2)}) collective-permute-start(bf16[64,896]{1,0:T(8,128)(2,1)S(1)} %get-tuple-element.10), channel_id=1, source_target_pairs={{0,0},{1,128},{2,32},{3,160},{32,64},{33,192},{34,96},{35,224},{64... | collective-permute-start | bytes 344072 | tf_op jit(solution)/shard_map/ppermute | solution.py:213
  149.8 4.2 %collective-permute-start.3 = (bf16[64,896]{1,0:T(8,128)(2,1)S(1)}, bf16[64,896]{1,0:T(8,128)(2,1)S(1)}, u32[]{:S(2)}, u32[]{:S(2)}) collective-permute-start(bf16[64,896]{1,0:T(8,128)(2,1)S(1)} %get-tuple-element.9), channel_id=1, source_target_pairs={{0,32},{1,160},{2,64},{3,192},{32,96},{33,224},{34,0},{35,128},{64... | collective-permute-start | bytes 344072 | tf_op jit(solution)/shard_map/ppermute | solution.py:213
  154.0 2.2 %collective-permute-start.4 = (bf16[64,896]{1,0:T(8,128)(2,1)S(1)}, bf16[64,896]{1,0:T(8,128)(2,1)S(1)}, u32[]{:S(2)}, u32[]{:S(2)}) collective-permute-start(bf16[64,896]{1,0:T(8,128)(2,1)S(1)} %get-tuple-element.8), channel_id=1, source_target_pairs={{0,64},{1,192},{2,96},{3,224},{32,0},{33,128},{34,32},{35,160},{64... | collective-permute-start | bytes 344072 | tf_op jit(solution)/shard_map/ppermute | solution.py:213
  156.2 5.3 %collective-permute-start.5 = (bf16[64,896]{1,0:T(8,128)(2,1)S(1)}, bf16[64,896]{1,0:T(8,128)(2,1)S(1)}, u32[]{:S(2)}, u32[]{:S(2)}) collective-permute-start(bf16[64,896]{1,0:T(8,128)(2,1)S(1)} %get-tuple-element.7), channel_id=1, source_target_pairs={{0,96},{1,224},{2,0},{3,128},{32,32},{33,160},{34,64},{35,192},{64... | collective-permute-start | bytes 344072 | tf_op jit(solution)/shard_map/ppermute | solution.py:213
  161.7 0.0 collective-permute-done.2
  161.7 0.0 collective-permute-done.3
  161.7 0.0 collective-permute-done.4
  161.7 2.1 %collective-permute-done.5 = bf16[64,896]{1,0:T(8,128)(2,1)S(1)} collective-permute-done((bf16[64,896]{1,0:T(8,128)(2,1)S(1)}, bf16[64,896]{1,0:T(8,128)(2,1)S(1)}, u32[]{:S(2)}, u32[]{:S(2)}) %collective-permute-start.5) | collective-permute-done | bytes 114720 | tf_op jit(solution)/shard_map/ppermute | solution.py:213
  163.8 0.1 fusion.4
  163.9 0.7 pad_maximum_fusion
  (4 shorter events, 0.1 us)
Async XLA Ops:
  6.5 0.9 copy-start
  29.7 45.1 %copy-start.4 = (s32[4096]{0:T(1024)S(1)}, s32[4096]{0:T(1024)}, u32[]{:S(2)}) copy-start(s32[4096]{0:T(1024)} %param.8) | copy-start | bytes 49156
  29.7 49.7 %copy-start.3 = (s32[128]{0:T(128)S(1)}, s32[128]{0:T(128)}, u32[]{:S(2)}) copy-start(s32[128]{0:T(128)} %order.1) | copy-start | bytes 1540
  29.7 42.5 %all-to-all-start.1 = ((bf16[8,8,32,576]{3,2,1,0:T(8,128)(2,1)}), bf16[8,8,32,576]{3,2,1,0:T(8,128)(2,1)S(1)}, u32[]{:S(2)}, u32[]{:S(2)}) async-start(bf16[8,8,32,576]{3,2,1,0:T(8,128)(2,1)} %broadcast_in_dim.33), calls=%async_computation.1 | async-start | bytes 5242880 | tf_op jit(solution)/shard_map/all_to_all | solution.py:166
  36.5 72.3 %all-gather.2.cloned.1.call-start = ((), (), s32[]{:S(2)}) async-start(), calls=%async_computation.3 | async-start | bytes 4128768 | tf_op jit(solution)/shard_map/all_gather | solution.py:176
  72.2 7.2 %collective-permute-start = (bf16[64,32,576]{2,1,0:T(8,128)(2,1)S(1)}, bf16[64,32,576]{2,1,0:T(8,128)(2,1)}, u32[]{:S(2)}, u32[]{:S(2)}) collective-permute-start(bf16[64,32,576]{2,1,0:T(8,128)(2,1)S(1)} %bitcast.21), channel_id=1, source_target_pairs={{0,1},{1,0},{2,3},{3,2},{4,5},{5,4},{6,7},{7,6},{8,9},{9,8},{10,11... | collective-permute-start | bytes 7077896 | tf_op jit(solution)/shard_map/ppermute | solution.py:181
  79.4 1.6 copy-start.1
  81.0 1.3 copy-start.2
  95.7 44.0 %all-to-all-start.2 = ((bf16[8,64,2048]{2,1,0:T(8,128)(2,1)}), bf16[8,64,2048]{2,1,0:T(8,128)(2,1)S(1)}, u32[]{:S(2)}, u32[]{:S(2)}) async-start(bf16[8,64,2048]{2,1,0:T(8,128)(2,1)} %broadcast_in_dim.34), calls=%async_computation.2 | async-start | bytes 4194304 | tf_op jit(solution)/shard_map/all_to_all | solution.py:166
  144.2 3.0 %collective-permute-start.1 = (bf16[4,64,896]{2,1,0:T(8,128)(2,1)S(1)}, bf16[4,64,896]{2,1,0:T(8,128)(2,1)S(1)}, u32[]{:S(2)}, u32[]{:S(2)}) collective-permute-start(bf16[4,64,896]{2,1,0:T(8,128)(2,1)S(1)} %dynamic-slice_bitcast_fusion), channel_id=1, source_target_pairs={{0,1},{1,0},{2,3},{3,2},{4,5},{5,4},{6,7},{7,6},{8,9},{9,8},{10,11... | collective-permute-start | bytes 1376264 | tf_op jit(solution)/shard_map/ppermute | solution.py:199
  147.3 14.3 %collective-permute-start.2 = (bf16[64,896]{1,0:T(8,128)(2,1)S(1)}, bf16[64,896]{1,0:T(8,128)(2,1)S(1)}, u32[]{:S(2)}, u32[]{:S(2)}) collective-permute-start(bf16[64,896]{1,0:T(8,128)(2,1)S(1)} %get-tuple-element.10), channel_id=1, source_target_pairs={{0,0},{1,128},{2,32},{3,160},{32,64},{33,192},{34,96},{35,224},{64... | collective-permute-start | bytes 344072 | tf_op jit(solution)/shard_map/ppermute | solution.py:213
  149.8 11.8 %collective-permute-start.3 = (bf16[64,896]{1,0:T(8,128)(2,1)S(1)}, bf16[64,896]{1,0:T(8,128)(2,1)S(1)}, u32[]{:S(2)}, u32[]{:S(2)}) collective-permute-start(bf16[64,896]{1,0:T(8,128)(2,1)S(1)} %get-tuple-element.9), channel_id=1, source_target_pairs={{0,32},{1,160},{2,64},{3,192},{32,96},{33,224},{34,0},{35,128},{64... | collective-permute-start | bytes 344072 | tf_op jit(solution)/shard_map/ppermute | solution.py:213
  154.0 7.7 %collective-permute-start.4 = (bf16[64,896]{1,0:T(8,128)(2,1)S(1)}, bf16[64,896]{1,0:T(8,128)(2,1)S(1)}, u32[]{:S(2)}, u32[]{:S(2)}) collective-permute-start(bf16[64,896]{1,0:T(8,128)(2,1)S(1)} %get-tuple-element.8), channel_id=1, source_target_pairs={{0,64},{1,192},{2,96},{3,224},{32,0},{33,128},{34,32},{35,160},{64... | collective-permute-start | bytes 344072 | tf_op jit(solution)/shard_map/ppermute | solution.py:213
  156.2 7.6 %collective-permute-start.5 = (bf16[64,896]{1,0:T(8,128)(2,1)S(1)}, bf16[64,896]{1,0:T(8,128)(2,1)S(1)}, u32[]{:S(2)}, u32[]{:S(2)}) collective-permute-start(bf16[64,896]{1,0:T(8,128)(2,1)S(1)} %get-tuple-element.7), channel_id=1, source_target_pairs={{0,96},{1,224},{2,0},{3,128},{32,32},{33,160},{34,64},{35,192},{64... | collective-permute-start | bytes 344072 | tf_op jit(solution)/shard_map/ppermute | solution.py:213
Sparse Core Ops, SparseCore 0:
  39.1 48.6 all-gather.1

commit v2 on v1

v2 whole, which is shorter than its diff:
```python
import functools

import jax
import jax.numpy as jnp
from jax import lax
from jax.experimental import pallas as pl
from jax.experimental.pallas import tpu as pltpu
from jax.sharding import Mesh, PartitionSpec as P

ROPE = 64
VD = 128
DOCS = 6
AXES = ("x", "yh", "z", "yl", "c")
SIZES = (4, 2, 8, 2, 2)
SPAN = 32
GROUP = 16
KEYS = SPAN * GROUP
MAXB = 5
NEG = -1e30
COPIES = 8


def attention_kernel(
    starts, place, slot, q_ref, w_hbm, own_ref, oth_ref, out_ref,
    k_buf, s_buf, top_buf, sum_buf, acc, mixed, w_buf, w_sem,
):
    span_total = place.shape[0]
    heads = q_ref.shape[1]
    rows = SPAN * heads
    value_cols = w_hbm.shape[1]
    scale = (VD + ROPE) ** (-0.5) * 1.4426950408889634
    core = slot[2]

    w_copy = pltpu.make_async_copy(w_hbm, w_buf, w_sem)
    w_copy.start()

    def doc_start(pos):
        lo = jnp.zeros_like(pos)
        for d in range(DOCS):
            lo = jnp.maximum(lo, jnp.where(starts[d] <= pos, starts[d], 0))
        return lo

    for t in range(2):
        last = slot[t]
        lo = jnp.int32(0)
        for d in range(DOCS):
            lo = jnp.maximum(lo, jnp.where(starts[d] <= last * SPAN, starts[d], 0))
        first = lo // SPAN
        blocks = (last - first + GROUP) // GROUP
        row_token = lax.broadcasted_iota(jnp.int32, (rows, 1), 0) // heads
        q_pos = last * SPAN + row_token
        q_lo = doc_start(q_pos) - first * SPAN
        q_hi = q_pos - first * SPAN
        q = q_ref[t * SPAN : (t + 1) * SPAN].reshape(rows, q_ref.shape[2])
        top_buf[...] = jnp.full(top_buf.shape, NEG, jnp.float32)
        sum_buf[...] = jnp.zeros(sum_buf.shape, jnp.float32)
        acc[...] = jnp.zeros(acc.shape, jnp.float32)

        def score(b, carry):
            for g in range(GROUP):
                stored = place[jnp.minimum(first + b * GROUP + g, span_total - 1)]
                mine = lax.rem(stored, 2) == core
                k_buf[b, g * SPAN : (g + 1) * SPAN] = jnp.where(
                    mine, own_ref[stored // 2], oth_ref[stored // 2]
                )
            s = lax.dot_general(
                q, k_buf[b], (((1,), (1,)), ((), ())), preferred_element_type=jnp.float32
            )
            k_pos = b * KEYS + lax.broadcasted_iota(jnp.int32, (1, KEYS), 1)
            s = jnp.where((k_pos >= q_lo) & (k_pos <= q_hi), s, NEG)
            s_buf[b] = s
            top = top_buf[...]
            for j in range(KEYS // 128):
                top = jnp.maximum(top, s[:, j * 128 : (j + 1) * 128])
            top_buf[...] = top
            return carry

        lax.fori_loop(0, blocks, score, 0)
        top = jnp.max(top_buf[...], axis=1, keepdims=True)

        def mix(b, carry):
            w = jnp.exp2((s_buf[b] - top) * scale)
            part = sum_buf[...]
            for j in range(KEYS // 128):
                part = part + w[:, j * 128 : (j + 1) * 128]
            sum_buf[...] = part
            acc[...] += jnp.dot(
                w.astype(jnp.bfloat16), k_buf[b, :, :value_cols], preferred_element_type=jnp.float32
            )
            return carry

        lax.fori_loop(0, blocks, mix, 0)
        total = jnp.sum(sum_buf[...], axis=1, keepdims=True)
        scaled = acc[...] / total
        for j in range(value_cols // 128):
            mixed[j, t * rows : (t + 1) * rows, :] = scaled[:, j * 128 : (j + 1) * 128]

    w_copy.wait()
    tokens = 2 * SPAN
    for h in range(heads):
        part = jnp.concatenate(
            [mixed[j, pl.ds(h, tokens, stride=heads), :] for j in range(value_cols // 128)], axis=1
        ).astype(jnp.bfloat16)
        piece = jnp.dot(part, w_buf[h], preferred_element_type=jnp.float32).astype(jnp.bfloat16)
        for r in range(out_ref.shape[0]):
            out_ref[r, :, h * VD : (h + 1) * VD] = piece


def attention(starts, place, slot, queries, w_uv, own, oth):
    tokens, heads, lat = queries.shape
    value_cols = w_uv.shape[1]
    rows = SPAN * heads
    smem = pl.BlockSpec(memory_space=pltpu.SMEM)
    vmem = pl.BlockSpec(memory_space=pltpu.VMEM)
    hbm = pl.BlockSpec(memory_space=pl.ANY)
    return pl.pallas_call(
        attention_kernel,
        out_shape=jax.ShapeDtypeStruct((COPIES, tokens, heads * VD), jnp.bfloat16),
        in_specs=[smem, smem, smem, vmem, hbm, vmem, vmem],
        out_specs=vmem,
        scratch_shapes=[
            pltpu.VMEM((MAXB, KEYS, lat), jnp.bfloat16),
            pltpu.VMEM((MAXB, rows, KEYS), jnp.float32),
            pltpu.VMEM((rows, 128), jnp.float32),
            pltpu.VMEM((rows, 128), jnp.float32),
            pltpu.VMEM((rows, value_cols), jnp.float32),
            pltpu.VMEM((value_cols // 128, 2 * rows, 128), jnp.float32),
            pltpu.VMEM(w_uv.shape, jnp.bfloat16),
            pltpu.SemaphoreType.DMA(()),
        ],
        compiler_params=pltpu.CompilerParams(vmem_limit_bytes=40 * 2**20),
        cost_estimate=pl.CostEstimate(
            flops=5_000_000_000, bytes_accessed=8_000_000, transcendentals=2_000_000
        ),
    )(starts, place, slot, queries, w_uv, own, oth)


def gather_rows(v, axes, count):
    return lax.all_to_all(jnp.broadcast_to(v[None], (count,) + v.shape), axes, 0, 0)


def shards(queries, latent, documents, span_order, w_uv, w_out):
    row_axes = ("x", "yh")
    ai = lax.axis_index
    core, zi = ai("c"), ai("z")
    place = ai("x") * 2 + ai("yh")
    tie = lax.optimization_barrier

    def shift(v, k):
        return lax.ppermute(v, "z", [(i, (i + k) % 8) for i in range(8)])

    w_own = w_out.T
    half = 64
    span = lax.dynamic_slice_in_dim(latent, core * SPAN, SPAN)
    line = gather_rows(span, "z", 8)
    line, w_own = tie((line, w_own))

    up1, down1 = shift(w_own, 1), shift(w_own, -1)
    up2, down2 = shift(up1, 1), shift(down1, -1)
    own = gather_rows(line, row_axes, COPIES).reshape(64, SPAN, latent.shape[1])
    own, up2, down2 = tie((own, up2, down2))

    up3, down3 = shift(up2, 1), shift(down2, -1)
    oth = lax.ppermute(own, "c", [(0, 1), (1, 0)])
    starts = jnp.sum(
        documents[None, :] < jnp.arange(DOCS, dtype=jnp.int32)[:, None], axis=1, dtype=jnp.int32
    )
    spans = jnp.arange(span_order.shape[0], dtype=jnp.int32)
    stored = jnp.sum(jnp.where(span_order[None, :] == spans[:, None], spans[None, :], 0), axis=1)
    slot = jnp.concatenate(
        [lax.dynamic_slice_in_dim(span_order, 2 * (place * 8 + zi), 2), core[None].astype(jnp.int32)]
    )
    head_out = attention(starts, stored, slot, queries, w_uv, own, oth)
    head_out, up3, down3 = tie((head_out, up3, down3))

    far = jnp.concatenate([shift(up3[:half], 1), shift(down3[half:], -1)], axis=0)
    tokens = head_out.shape[1]
    rows = lax.all_to_all(head_out, row_axes, 0, 0).reshape(COPIES * tokens, head_out.shape[2])
    w_all = jnp.zeros((8,) + w_own.shape, w_own.dtype)
    for k, v in enumerate((w_own, up1, up2, up3, far, down3, down2, down1)):
        w_all = lax.dynamic_update_index_in_dim(w_all, v, (zi - k) % 8, 0)
    w_cols = w_all.reshape(-1, w_own.shape[1])
    terms = lax.dot_general(
        rows, w_cols, (((1,), (1,)), ((), ())), preferred_element_type=jnp.float32
    ).astype(jnp.bfloat16)
    width = terms.shape[1]
    terms = terms.reshape(2, 4, tokens, width)

    kept = lax.dynamic_index_in_dim(terms, core, 0, keepdims=False)
    sent = lax.dynamic_index_in_dim(terms, 1 - core, 0, keepdims=False)
    got = lax.ppermute(sent, "c", [(0, 1), (1, 0)])
    both = (kept.astype(jnp.float32) + got.astype(jnp.float32)).astype(jnp.bfloat16)

    slot = (place % 2) * 2 + ai("yl")
    left = jnp.zeros((tokens, width), jnp.float32)
    right = left
    for k in range(4):
        pairs = []
        for r in range(8):
            for yl in range(2):
                for c in range(2):
                    i = ((r % 2) * 2 + yl + k) % 4
                    pairs.append((r * 4 + yl * 2 + c, (c * 4 + i) * 4 + r // 2))
        block = lax.dynamic_index_in_dim(both, (slot + k) % 4, 0, keepdims=False)
        got = lax.ppermute(block, ("x", "yh", "yl", "c"), pairs).astype(jnp.float32)
        first_half = (place - k) % 4 < 2
        left = left + jnp.where(first_half, got, 0.0)
        right = right + jnp.where(first_half, 0.0, got)
    return jnp.concatenate([left, right], axis=1).astype(jnp.bfloat16)


def solution(mesh):
    fine = Mesh(mesh.devices.reshape(SIZES), AXES)
    ctx, head = ("x", "yh", "z"), ("yl", "c")
    return jax.shard_map(
        shards,
        mesh=fine,
        in_specs=(
            P(ctx, head, None),
            P(ctx, None),
            P(),
            P(),
            P(head, None, None),
            P(head, ctx),
        ),
        out_specs=P(ctx, head),
        check_vma=False,
    )
```

time: 169 us -> 144 us (0.85); the launches traced: 171 us -> 144 us
  waiting for transfers between devices: 74.6 us -> 55.3 us
  between operations: 13.6 us -> 0.31 us
  local copies, waits for them, and re-layouts: 7.34 us -> 13.8 us
  Pallas kernels: 11.8 us -> 9.34 us
    all_to_all x2 -> x1, waiting for transfers between devices: 65.9 us -> 15 us  [gather_rows(): lax.all_to_all(jnp.broadcast_to(v[None], (count,) + v.shape), axes, 0, 0)]
    ppermute x0 -> x8, waiting for transfers between devices: none -> 21 us  [shift(): return lax.ppermute(v, 'z', [(i, (i + k) % 8) for i in range(8)])]
    all_to_all x0 -> x1, waiting for transfers between devices: none -> 15.5 us  [shards(): lax.all_to_all(head_out, row_axes, 0, 0)]
    all_to_all x2 -> x1, starting transfers between devices: 19.8 us -> 6.65 us  [gather_rows(): lax.all_to_all(jnp.broadcast_to(v[None], (count,) + v.shape), axes, 0, 0)]
    ppermute x0 -> x8, starting transfers between devices: none -> 9.89 us  [shift(): return lax.ppermute(v, 'z', [(i, (i + k) % 8) for i in range(8)])]
    dynamic_update_slice x0 -> x7, local copies, waits for them, and re-layouts: none -> 5.42 us  [shards(): w_all = lax.dynamic_update_index_in_dim(w_all, v, (zi - k) % 8, 0)]
    ppermute x1, waiting for transfers between devices: 4.44 us -> 0.01 us  [shards(): oth = lax.ppermute(own, 'c', [(0, 1), (1, 0)])]
    all_to_all x0 -> x1, starting transfers between devices: none -> 3.75 us  [shards(): lax.all_to_all(head_out, row_axes, 0, 0)]
  transfers between devices with their start and end apart: 9 -> 16, of which waited for: 5 -> 8; matrix products, arithmetic and copies ran while one was open for 1% -> 6% of each run, Pallas kernels for 7% -> 6%
where the time goes in v2:
time: 144 us
  waiting for transfers between devices  55.3 us (38%)
  starting transfers between devices  38.5 us (27%)
  blocking collectives  20.5 us (14%)
  local copies, waits for them, and re-layouts  13.8 us (10%)
  Pallas kernels  9.34 us (6%)
  matrix products  4.4 us (3%)
  other arithmetic  2.12 us (1%)
    ppermute x8, waiting for transfers between devices, shift(): return lax.ppermute(v, 'z', [(i, (i + k) % 8) for i in range(8)])  21 us
    all_to_all x1, blocking collectives, gather_rows(): lax.all_to_all(jnp.broadcast_to(v[None], (count,) + v.shape), axes, 0, 0)  20.5 us
    all_to_all x1, waiting for transfers between devices, shards(): lax.all_to_all(head_out, row_axes, 0, 0)  15.5 us
    all_to_all x1, waiting for transfers between devices, gather_rows(): lax.all_to_all(jnp.broadcast_to(v[None], (count,) + v.shape), axes, 0, 0)  15 us
    ppermute x4, starting transfers between devices, shards(): got = lax.ppermute(block, ('x', 'yh', 'yl', 'c'), pairs).astype(jnp.float32)  14.2 us
    ppermute x8, starting transfers between devices, shift(): return lax.ppermute(v, 'z', [(i, (i + k) % 8) for i in range(8)])  9.89 us
    pallas_call x1, Pallas kernels, attention(): pl.pallas_call(attention_kernel, out_shape=jax.ShapeDtypeStruct((COPIES,...  9.34 us
    all_to_all x1, starting transfers between devices, gather_rows(): lax.all_to_all(jnp.broadcast_to(v[None], (count,) + v.shape), axes, 0, 0)  6.65 us
  transfers between devices with their start and end apart: 16, of which 8 were waited for; matrix products, arithmetic and copies ran while one was open for 6% of the time, Pallas kernels for 6%

profile of v2, /device:TPU:1, one launch (start us, length us, event | category | flops | bytes accessed | tf_op | source)
XLA Modules:
  0.0 144.3 jit_solution(14829920842282518721)
XLA Ops:
  0.0 0.0 copy-start
  0.0 0.9 copy-done
  0.9 20.5 %all_to_all.15 = bf16[8,32,576]{2,1,0:T(8,128)(2,1)S(1)} all-to-all(bf16[8,32,576]{2,1,0:T(8,128)(2,1)S(1)} %broadcast_in_dim.75), channel_id=1, replica_groups=mesh['x'=4,'yh'=2,'z'=8,'yl'=2,'c'=2] {'z'}, dimensions={0} | all-to-all | bytes 589824 | tf_op jit(solution)/shard_map/all_to_all | solution.py:139
  21.4 1.8 %broadcast_in_dim.76 = bf16[8,8,32,576]{3,2,1,0:T(8,128)(2,1)} broadcast(bf16[8,32,576]{2,1,0:T(8,128)(2,1)S(1)} %all_to_all.15), dimensions={1,2,3} | broadcast | bytes 2654208 | tf_op jit(solution)/shard_map/broadcast_in_dim | solution.py:139
  23.2 6.7 %all-to-all-start.1 = ((bf16[8,8,32,576]{3,2,1,0:T(8,128)(2,1)}), bf16[8,8,32,576]{3,2,1,0:T(8,128)(2,1)S(1)}, u32[]{:S(2)}, u32[]{:S(2)}) async-start(bf16[8,8,32,576]{3,2,1,0:T(8,128)(2,1)} %broadcast_in_dim.76), calls=%async_computation.1 | async-start | bytes 5242880 | tf_op jit(solution)/shard_map/all_to_all | solution.py:139
  29.8 0.0 copy-done.5
  29.8 0.1 collective-permute-start
  29.9 2.7 %collective-permute-start.2 = (bf16[112,2048]{1,0:T(8,128)(2,1)S(1)}, bf16[112,2048]{1,0:T(8,128)(2,1)S(1)}, u32[]{:S(2)}, u32[]{:S(2)}) collective-permute-start(bf16[112,2048]{1,0:T(8,128)(2,1)S(1)} %bitcast.46), channel_id=1, source_target_pairs={{0,28},{4,0},{8,4},{12,8},{16,12},{20,16},{24,20},{28,24},{1,29},{... | collective-permute-start | bytes 1376264 | tf_op jit(solution)/shard_map/ppermute | solution.py:150
  32.6 7.7 %collective-permute-done = bf16[112,2048]{1,0:T(8,128)(2,1)S(1)} collective-permute-done((bf16[112,2048]{1,0:T(8,128)(2,1)S(1)}, bf16[112,2048]{1,0:T(8,128)(2,1)S(1)}, u32[]{:S(2)}, u32[]{:S(2)}) %collective-permute-start) | collective-permute-done | bytes 458784 | tf_op jit(solution)/shard_map/ppermute | solution.py:150
  40.3 0.0 collective-permute-start.1
  40.3 0.0 collective-permute-done.2
  40.3 0.0 copy-start.6
  40.3 2.7 %collective-permute-start.3 = (bf16[112,2048]{1,0:T(8,128)(2,1)S(1)}, bf16[112,2048]{1,0:T(8,128)(2,1)}, u32[]{:S(2)}, u32[]{:S(2)}) collective-permute-start(bf16[112,2048]{1,0:T(8,128)(2,1)S(1)} %collective-permute-done.2), channel_id=1, source_target_pairs={{0,28},{4,0},{8,4},{12,8},{16,12},{20,16},{24,20},{28,24},{1,29},{... | collective-permute-start | bytes 1376264 | tf_op jit(solution)/shard_map/ppermute | solution.py:150
  43.0 6.8 %collective-permute-done.1 = bf16[112,2048]{1,0:T(8,128)(2,1)S(1)} collective-permute-done((bf16[112,2048]{1,0:T(8,128)(2,1)S(1)}, bf16[112,2048]{1,0:T(8,128)(2,1)S(1)}, u32[]{:S(2)}, u32[]{:S(2)}) %collective-permute-start.1) | collective-permute-done | bytes 458784 | tf_op jit(solution)/shard_map/ppermute | solution.py:150
  49.8 0.0 copy-done.10
  49.8 0.0 copy-done.6
  49.8 0.8 copy-done.8
  50.5 0.0 collective-permute-done.3
  50.5 15.0 %all-to-all-done.1 = bf16[8,8,32,576]{3,2,1,0:T(8,128)(2,1)S(1)} async-done(((bf16[8,8,32,576]{3,2,1,0:T(8,128)(2,1)}), bf16[8,8,32,576]{3,2,1,0:T(8,128)(2,1)S(1)}, u32[]{:S(2)}, u32[]{:S(2)}) %all-to-all-start.1) | async-done | bytes 2359328 | tf_op jit(solution)/shard_map/all_to_all | solution.py:139
  65.6 2.5 %collective-permute-start.4 = (bf16[64,32,576]{2,1,0:T(8,128)(2,1)S(1)}, bf16[64,32,576]{2,1,0:T(8,128)(2,1)}, u32[]{:S(2)}, u32[]{:S(2)}) collective-permute-start(bf16[64,32,576]{2,1,0:T(8,128)(2,1)S(1)} %bitcast.39), channel_id=1, source_target_pairs={{0,1},{1,0},{2,3},{3,2},{4,5},{5,4},{6,7},{7,6},{8,9},{9,8},{10,11... | collective-permute-start | bytes 7077896 | tf_op jit(solution)/shard_map/ppermute | solution.py:164
  68.1 0.0 copy-done.13
  68.1 0.1 dynamic_slice.26
  68.2 0.0 copy-start.2
  68.2 0.0 copy-start.3
  68.2 0.1 pad_add_fusion.slot
  68.3 0.1 select_reduce_fusion.place
  68.4 0.1 convert_reduce_fusion.starts
  68.5 0.4 broadcast_in_dim.77
  69.0 0.1 copy-done.11
  69.2 0.1 copy-done.9
  69.3 0.0 collective-permute-start.5
  69.3 2.7 %collective-permute-start.6 = (bf16[112,2048]{1,0:T(8,128)(2,1)}, bf16[112,2048]{1,0:T(8,128)(2,1)}, u32[]{:S(2)}, u32[]{:S(2)}) collective-permute-start(bf16[112,2048]{1,0:T(8,128)(2,1)} %collective-permute-done.3), channel_id=1, source_target_pairs={{0,28},{4,0},{8,4},{12,8},{16,12},{20,16},{24,20},{28,24},{1,29},{... | collective-permute-start | bytes 1376264 | tf_op jit(solution)/shard_map/ppermute | solution.py:150
  72.1 1.8 %copy-done.4 = bf16[8,112,2048]{2,1,0:T(8,128)(2,1)} copy-done((bf16[8,112,2048]{2,1,0:T(8,128)(2,1)}, bf16[8,112,2048]{2,1,0:T(8,128)(2,1)S(1)}, u32[]{:S(2)}) %copy-start.4) | copy-done | bytes 3670040
  73.8 0.0 collective-permute-done.4.oth_ref
  73.8 9.3 %shard_map.64 = bf16[8,64,2048]{2,1,0:T(8,128)(2,1)S(1)} custom-call(s32[6]{0:T(128)S(1)} %convert_reduce_fusion.starts, s32[128]{0:T(128)S(1)} %select_reduce_fusion.place, s32[3]{0:T(128)S(1)} %pad_add_fusion.slot, bf16[64,16,576]{2,1,0:T(8,128)(2,1)S(1)} %copy-done.3, bf16[16,512,128]{2,1,0:T(8,128)(2,1)S(1)} %copy-done.2, ...), custom_call_target="tpu_custom_call" | custom-call | flops 5000000000 | bytes 8000000 | tf_op jit(solution)/shard_map/pallas_call | solution.py:116
  83.2 1.3 copy-done.1
  84.5 0.0 collective-permute-done.5
  84.5 0.0 collective-permute-done.6
  84.5 3.7 %all-to-all-start.2 = ((bf16[8,64,2048]{2,1,0:T(8,128)(2,1)}), bf16[8,64,2048]{2,1,0:T(8,128)(2,1)S(1)}, u32[]{:S(2)}, u32[]{:S(2)}) async-start(bf16[8,64,2048]{2,1,0:T(8,128)(2,1)} %copy-done.1), calls=%async_computation.2 | async-start | bytes 4194304 | tf_op jit(solution)/shard_map/all_to_all | solution.py:178
  88.3 0.9 slice.7
  89.2 1.0 collective-permute-start.8
  90.2 0.8 collective-permute-start.7
  91.1 0.8 bitcast_dynamic-update-slice_fusion.3
  91.9 3.3 %collective-permute-done.8 = bf16[48,2048]{1,0:T(8,128)(2,1)S(1)} collective-permute-done((bf16[48,2048]{1,0:T(8,128)(2,1)S(1)}, bf16[48,2048]{1,0:T(8,128)(2,1)S(1)}, u32[]{:S(2)}, u32[]{:S(2)}) %collective-permute-start.8) | collective-permute-done | bytes 196640 | tf_op jit(solution)/shard_map/ppermute | solution.py:150
  95.2 3.2 %collective-permute-done.7 = bf16[64,2048]{1,0:T(8,128)(2,1)S(1)} collective-permute-done((bf16[64,2048]{1,0:T(8,128)(2,1)S(1)}, bf16[64,2048]{1,0:T(8,128)(2,1)S(1)}, u32[]{:S(2)}, u32[]{:S(2)}) %collective-permute-start.7) | collective-permute-done | bytes 262176 | tf_op jit(solution)/shard_map/ppermute | solution.py:150
  98.4 0.8 fusion.1
  99.2 1.8 %bitcast_dynamic-update-slice_fusion.2 = bf16[8,112,2048]{2,1,0:T(8,128)(2,1)} fusion(bf16[8,112,2048]{2,1,0:T(8,128)(2,1)} %fusion.1, s32[]{:T(128)S(6)} %select_n.186, bf16[112,2048]{1,0:T(8,128)(2,1)} %collective-permute-done.6), kind=kLoop, calls=%fused_computation.7 | loop fusion | bytes 917508 | tf_op jit(solution)/shard_map/jit(dynamic_update_index_in_dim)/dynamic_update_slice | solution.py:181
  101.0 1.8 %bitcast_dynamic-update-slice_fusion.1 = bf16[8,112,2048]{2,1,0:T(8,128)(2,1)} fusion(bf16[8,112,2048]{2,1,0:T(8,128)(2,1)} %bitcast_dynamic-update-slice_fusion.2, s32[]{:T(128)S(6)} %select_n.188, bf16[112,2048]{1,0:T(8,128)(2,1)} %collective-permute-done.3), kind=kLoop, calls=%fused_computation.6 | loop fusion | bytes 917508 | tf_op jit(solution)/shard_map/jit(dynamic_update_index_in_dim)/dynamic_update_slice | solution.py:181
  102.9 0.8 bitcast_dynamic-update-slice_fusion
  103.7 15.5 %all-to-all-done.2 = bf16[8,64,2048]{2,1,0:T(8,128)(2,1)S(1)} async-done(((bf16[8,64,2048]{2,1,0:T(8,128)(2,1)}), bf16[8,64,2048]{2,1,0:T(8,128)(2,1)S(1)}, u32[]{:S(2)}, u32[]{:S(2)}) %all-to-all-start.2) | async-done | bytes 2097184 | tf_op jit(solution)/shard_map/all_to_all | solution.py:178
  119.2 4.4 %convolution_convert_fusion = bf16[512,896]{1,0:T(8,128)(2,1)S(1)} fusion(bf16[512,2048]{1,0:T(8,128)(2,1)S(1)} %bitcast.42, bf16[896,2048]{1,0:T(8,128)(2,1)} %bitcast.41), kind=kOutput, calls=%fused_computation | convolution fusion | flops 1879506944 | bytes 6684672 | tf_op jit(solution)/shard_map/dot_general | solution.py:183
  123.7 1.5 %collective-permute-start.9 = (bf16[4,64,896]{2,1,0:T(8,128)(2,1)S(1)}, bf16[4,64,896]{2,1,0:T(8,128)(2,1)S(1)}, u32[]{:S(2)}, u32[]{:S(2)}) collective-permute-start(bf16[4,64,896]{2,1,0:T(8,128)(2,1)S(1)} %dynamic-slice_bitcast_fusion), channel_id=1, source_target_pairs={{0,1},{1,0},{2,3},{3,2},{4,5},{5,4},{6,7},{7,6},{8,9},{9,8},{10,11... | collective-permute-start | bytes 1376264 | tf_op jit(solution)/shard_map/ppermute | solution.py:191
  125.1 1.4 %collective-permute-done.9 = bf16[4,64,896]{2,1,0:T(8,128)(2,1)S(1)} collective-permute-done((bf16[4,64,896]{2,1,0:T(8,128)(2,1)S(1)}, bf16[4,64,896]{2,1,0:T(8,128)(2,1)S(1)}, u32[]{:S(2)}, u32[]{:S(2)}) %collective-permute-start.9) | collective-permute-done | bytes 458784 | tf_op jit(solution)/shard_map/ppermute | solution.py:191
  126.6 0.1 fusion
  126.8 2.6 %collective-permute-start.10 = (bf16[64,896]{1,0:T(8,128)(2,1)S(1)}, bf16[64,896]{1,0:T(8,128)(2,1)S(1)}, u32[]{:S(2)}, u32[]{:S(2)}) collective-permute-start(bf16[64,896]{1,0:T(8,128)(2,1)S(1)} %get-tuple-element.26), channel_id=1, source_target_pairs={{0,0},{1,128},{2,32},{3,160},{32,64},{33,192},{34,96},{35,224},{64... | collective-permute-start | bytes 344072 | tf_op jit(solution)/shard_map/ppermute | solution.py:205
  129.4 4.1 %collective-permute-start.11 = (bf16[64,896]{1,0:T(8,128)(2,1)S(1)}, bf16[64,896]{1,0:T(8,128)(2,1)S(1)}, u32[]{:S(2)}, u32[]{:S(2)}) collective-permute-start(bf16[64,896]{1,0:T(8,128)(2,1)S(1)} %get-tuple-element.25), channel_id=1, source_target_pairs={{0,32},{1,160},{2,64},{3,192},{32,96},{33,224},{34,0},{35,128},{64... | collective-permute-start | bytes 344072 | tf_op jit(solution)/shard_map/ppermute | solution.py:205
  133.5 2.4 %collective-permute-start.12 = (bf16[64,896]{1,0:T(8,128)(2,1)S(1)}, bf16[64,896]{1,0:T(8,128)(2,1)S(1)}, u32[]{:S(2)}, u32[]{:S(2)}) collective-permute-start(bf16[64,896]{1,0:T(8,128)(2,1)S(1)} %get-tuple-element.24), channel_id=1, source_target_pairs={{0,64},{1,192},{2,96},{3,224},{32,0},{33,128},{34,32},{35,160},{64... | collective-permute-start | bytes 344072 | tf_op jit(solution)/shard_map/ppermute | solution.py:205
  135.9 5.1 %collective-permute-start.13 = (bf16[64,896]{1,0:T(8,128)(2,1)S(1)}, bf16[64,896]{1,0:T(8,128)(2,1)S(1)}, u32[]{:S(2)}, u32[]{:S(2)}) collective-permute-start(bf16[64,896]{1,0:T(8,128)(2,1)S(1)} %get-tuple-element.23), channel_id=1, source_target_pairs={{0,96},{1,224},{2,0},{3,128},{32,32},{33,160},{34,64},{35,192},{64... | collective-permute-start | bytes 344072 | tf_op jit(solution)/shard_map/ppermute | solution.py:205
  141.1 0.0 collective-permute-done.10
  141.1 0.0 collective-permute-done.11
  141.1 0.0 collective-permute-done.12
  141.1 2.3 %collective-permute-done.13 = bf16[64,896]{1,0:T(8,128)(2,1)S(1)} collective-permute-done((bf16[64,896]{1,0:T(8,128)(2,1)S(1)}, bf16[64,896]{1,0:T(8,128)(2,1)S(1)}, u32[]{:S(2)}, u32[]{:S(2)}) %collective-permute-start.13) | collective-permute-done | bytes 114720 | tf_op jit(solution)/shard_map/ppermute | solution.py:205
  143.4 0.1 fusion.5
  143.6 0.7 pad_maximum_fusion
  (22 shorter events, 0.3 us)
Async XLA Ops:
  0.0 0.9 copy-start
  21.4 8.4 %copy-start.5 = (bf16[2048,112]{0,1:T(8,128)(2,1)S(1)}, bf16[2048,112]{0,1:T(8,128)(2,1)}, u32[]{:S(2)}) copy-start(bf16[2048,112]{0,1:T(8,128)(2,1)} %param.11) | copy-start | bytes 1376260
  21.4 46.7 %copy-start.13 = (s32[128]{0:T(128)S(1)}, s32[128]{0:T(128)}, u32[]{:S(2)}) copy-start(s32[128]{0:T(128)} %param.9) | copy-start | bytes 1540
  21.4 47.0 %copy-start.12 = (s32[4096]{0:T(1024)S(1)}, s32[4096]{0:T(1024)}, u32[]{:S(2)}) copy-start(s32[4096]{0:T(1024)} %param.8) | copy-start | bytes 49156
  23.2 42.4 %all-to-all-start.1 = ((bf16[8,8,32,576]{3,2,1,0:T(8,128)(2,1)}), bf16[8,8,32,576]{3,2,1,0:T(8,128)(2,1)S(1)}, u32[]{:S(2)}, u32[]{:S(2)}) async-start(bf16[8,8,32,576]{3,2,1,0:T(8,128)(2,1)} %broadcast_in_dim.76), calls=%async_computation.1 | async-start | bytes 5242880 | tf_op jit(solution)/shard_map/all_to_all | solution.py:139
  29.8 10.5 %collective-permute-start = (bf16[112,2048]{1,0:T(8,128)(2,1)S(1)}, bf16[112,2048]{1,0:T(8,128)(2,1)S(1)}, u32[]{:S(2)}, u32[]{:S(2)}) collective-permute-start(bf16[112,2048]{1,0:T(8,128)(2,1)S(1)} %bitcast.45), channel_id=1, source_target_pairs={{0,4},{4,8},{8,12},{12,16},{16,20},{20,24},{24,28},{28,0},{1,5},{5... | collective-permute-start | bytes 1376264 | tf_op jit(solution)/shard_map/ppermute | solution.py:150
  29.9 10.4 %collective-permute-start.2 = (bf16[112,2048]{1,0:T(8,128)(2,1)S(1)}, bf16[112,2048]{1,0:T(8,128)(2,1)S(1)}, u32[]{:S(2)}, u32[]{:S(2)}) collective-permute-start(bf16[112,2048]{1,0:T(8,128)(2,1)S(1)} %bitcast.46), channel_id=1, source_target_pairs={{0,28},{4,0},{8,4},{12,8},{16,12},{20,16},{24,20},{28,24},{1,29},{... | collective-permute-start | bytes 1376264 | tf_op jit(solution)/shard_map/ppermute | solution.py:150
  40.3 9.5 %copy-start.10 = (bf16[112,2048]{1,0:T(8,128)(2,1)}, bf16[112,2048]{1,0:T(8,128)(2,1)S(1)}, u32[]{:S(2)}) copy-start(bf16[112,2048]{1,0:T(8,128)(2,1)S(1)} %collective-permute-done) | copy-start | bytes 1376260
  40.3 9.5 %collective-permute-start.1 = (bf16[112,2048]{1,0:T(8,128)(2,1)S(1)}, bf16[112,2048]{1,0:T(8,128)(2,1)S(1)}, u32[]{:S(2)}, u32[]{:S(2)}) collective-permute-start(bf16[112,2048]{1,0:T(8,128)(2,1)S(1)} %collective-permute-done), channel_id=1, source_target_pairs={{0,4},{4,8},{8,12},{12,16},{16,20},{20,24},{24,28},{28,0},{1,5},{5... | collective-permute-start | bytes 1376264 | tf_op jit(solution)/shard_map/ppermute | solution.py:150
  40.3 9.5 %copy-start.6 = (bf16[112,2048]{1,0:T(8,128)(2,1)}, bf16[112,2048]{1,0:T(8,128)(2,1)S(1)}, u32[]{:S(2)}) copy-start(bf16[112,2048]{1,0:T(8,128)(2,1)S(1)} %collective-permute-done.2) | copy-start | bytes 1376260
  40.3 10.2 %collective-permute-start.3 = (bf16[112,2048]{1,0:T(8,128)(2,1)S(1)}, bf16[112,2048]{1,0:T(8,128)(2,1)}, u32[]{:S(2)}, u32[]{:S(2)}) collective-permute-start(bf16[112,2048]{1,0:T(8,128)(2,1)S(1)} %collective-permute-done.2), channel_id=1, source_target_pairs={{0,28},{4,0},{8,4},{12,8},{16,12},{20,16},{24,20},{28,24},{1,29},{... | collective-permute-start | bytes 1376264 | tf_op jit(solution)/shard_map/ppermute | solution.py:150
  49.8 0.8 copy-start.8
  65.6 8.2 %collective-permute-start.4 = (bf16[64,32,576]{2,1,0:T(8,128)(2,1)S(1)}, bf16[64,32,576]{2,1,0:T(8,128)(2,1)}, u32[]{:S(2)}, u32[]{:S(2)}) collective-permute-start(bf16[64,32,576]{2,1,0:T(8,128)(2,1)S(1)} %bitcast.39), channel_id=1, source_target_pairs={{0,1},{1,0},{2,3},{3,2},{4,5},{5,4},{6,7},{7,6},{8,9},{9,8},{10,11... | collective-permute-start | bytes 7077896 | tf_op jit(solution)/shard_map/ppermute | solution.py:164
  68.2 1.0 copy-start.11
  68.2 1.2 copy-start.9
  68.2 5.7 %copy-start.2 = (bf16[16,512,128]{2,1,0:T(8,128)(2,1)S(1)}, bf16[16,512,128]{2,1,0:T(8,128)(2,1)}, u32[]{:S(2)}) copy-start(bf16[16,512,128]{2,1,0:T(8,128)(2,1)} %w_hbm.1) | copy-start | bytes 6291460
  68.2 5.7 %copy-start.3 = (bf16[64,16,576]{2,1,0:T(8,128)(2,1)S(1)}, bf16[64,16,576]{2,1,0:T(8,128)(2,1)}, u32[]{:S(2)}) copy-start(bf16[64,16,576]{2,1,0:T(8,128)(2,1)} %q_ref.1) | copy-start | bytes 3538948
  69.3 15.2 %collective-permute-start.5 = (bf16[112,2048]{1,0:T(8,128)(2,1)S(1)}, bf16[112,2048]{1,0:T(8,128)(2,1)S(1)}, u32[]{:S(2)}, u32[]{:S(2)}) collective-permute-start(bf16[112,2048]{1,0:T(8,128)(2,1)S(1)} %copy-done.9), channel_id=1, source_target_pairs={{0,4},{4,8},{8,12},{12,16},{16,20},{20,24},{24,28},{28,0},{1,5},{5... | collective-permute-start | bytes 1376264 | tf_op jit(solution)/shard_map/ppermute | solution.py:150
  69.3 15.2 %collective-permute-start.6 = (bf16[112,2048]{1,0:T(8,128)(2,1)}, bf16[112,2048]{1,0:T(8,128)(2,1)}, u32[]{:S(2)}, u32[]{:S(2)}) collective-permute-start(bf16[112,2048]{1,0:T(8,128)(2,1)} %collective-permute-done.3), channel_id=1, source_target_pairs={{0,28},{4,0},{8,4},{12,8},{16,12},{20,16},{24,20},{28,24},{1,29},{... | collective-permute-start | bytes 1376264 | tf_op jit(solution)/shard_map/ppermute | solution.py:150
  72.0 1.8 %copy-start.4 = (bf16[8,112,2048]{2,1,0:T(8,128)(2,1)}, bf16[8,112,2048]{2,1,0:T(8,128)(2,1)S(1)}, u32[]{:S(2)}) copy-start(bf16[8,112,2048]{2,1,0:T(8,128)(2,1)S(1)} %bitcast_dynamic-update-slice_fusion.4) | copy-start | bytes 11010052
  83.2 1.3 copy-start.1
  84.5 18.3 %copy-start.7 = (bf16[112,2048]{1,0:T(8,128)(2,1)S(1)}, bf16[112,2048]{1,0:T(8,128)(2,1)}, u32[]{:S(2)}) copy-start(bf16[112,2048]{1,0:T(8,128)(2,1)} %copy-done.6) | copy-start | bytes 1376260
  84.5 34.7 %all-to-all-start.2 = ((bf16[8,64,2048]{2,1,0:T(8,128)(2,1)}), bf16[8,64,2048]{2,1,0:T(8,128)(2,1)S(1)}, u32[]{:S(2)}, u32[]{:S(2)}) async-start(bf16[8,64,2048]{2,1,0:T(8,128)(2,1)} %copy-done.1), calls=%async_computation.2 | async-start | bytes 4194304 | tf_op jit(solution)/shard_map/all_to_all | solution.py:178
  89.2 6.0 %collective-permute-start.8 = (bf16[48,2048]{1,0:T(8,128)(2,1)S(1)}, bf16[48,2048]{1,0:T(8,128)(2,1)S(1)}, u32[]{:S(2)}, u32[]{:S(2)}) collective-permute-start(bf16[48,2048]{1,0:T(8,128)(2,1)S(1)} %slice.7), channel_id=1, source_target_pairs={{0,28},{4,0},{8,4},{12,8},{16,12},{20,16},{24,20},{28,24},{1,29},{... | collective-permute-start | bytes 589832 | tf_op jit(solution)/shard_map/ppermute | solution.py:150
  90.2 8.1 %collective-permute-start.7 = (bf16[64,2048]{1,0:T(8,128)(2,1)S(1)}, bf16[64,2048]{1,0:T(8,128)(2,1)S(1)}, u32[]{:S(2)}, u32[]{:S(2)}) collective-permute-start(bf16[64,2048]{1,0:T(8,128)(2,1)S(1)} %slice.6), channel_id=1, source_target_pairs={{0,4},{4,8},{8,12},{12,16},{16,20},{20,24},{24,28},{28,0},{1,5},{5... | collective-permute-start | bytes 786440 | tf_op jit(solution)/shard_map/ppermute | solution.py:150
  123.7 2.9 %collective-permute-start.9 = (bf16[4,64,896]{2,1,0:T(8,128)(2,1)S(1)}, bf16[4,64,896]{2,1,0:T(8,128)(2,1)S(1)}, u32[]{:S(2)}, u32[]{:S(2)}) collective-permute-start(bf16[4,64,896]{2,1,0:T(8,128)(2,1)S(1)} %dynamic-slice_bitcast_fusion), channel_id=1, source_target_pairs={{0,1},{1,0},{2,3},{3,2},{4,5},{5,4},{6,7},{7,6},{8,9},{9,8},{10,11... | collective-permute-start | bytes 1376264 | tf_op jit(solution)/shard_map/ppermute | solution.py:191
  126.8 14.3 %collective-permute-start.10 = (bf16[64,896]{1,0:T(8,128)(2,1)S(1)}, bf16[64,896]{1,0:T(8,128)(2,1)S(1)}, u32[]{:S(2)}, u32[]{:S(2)}) collective-permute-start(bf16[64,896]{1,0:T(8,128)(2,1)S(1)} %get-tuple-element.26), channel_id=1, source_target_pairs={{0,0},{1,128},{2,32},{3,160},{32,64},{33,192},{34,96},{35,224},{64... | collective-permute-start | bytes 344072 | tf_op jit(solution)/shard_map/ppermute | solution.py:205
  129.4 11.7 %collective-permute-start.11 = (bf16[64,896]{1,0:T(8,128)(2,1)S(1)}, bf16[64,896]{1,0:T(8,128)(2,1)S(1)}, u32[]{:S(2)}, u32[]{:S(2)}) collective-permute-start(bf16[64,896]{1,0:T(8,128)(2,1)S(1)} %get-tuple-element.25), channel_id=1, source_target_pairs={{0,32},{1,160},{2,64},{3,192},{32,96},{33,224},{34,0},{35,128},{64... | collective-permute-start | bytes 344072 | tf_op jit(solution)/shard_map/ppermute | solution.py:205
  133.5 7.6 %collective-permute-start.12 = (bf16[64,896]{1,0:T(8,128)(2,1)S(1)}, bf16[64,896]{1,0:T(8,128)(2,1)S(1)}, u32[]{:S(2)}, u32[]{:S(2)}) collective-permute-start(bf16[64,896]{1,0:T(8,128)(2,1)S(1)} %get-tuple-element.24), channel_id=1, source_target_pairs={{0,64},{1,192},{2,96},{3,224},{32,0},{33,128},{34,32},{35,160},{64... | collective-permute-start | bytes 344072 | tf_op jit(solution)/shard_map/ppermute | solution.py:205
  135.9 7.5 %collective-permute-start.13 = (bf16[64,896]{1,0:T(8,128)(2,1)S(1)}, bf16[64,896]{1,0:T(8,128)(2,1)S(1)}, u32[]{:S(2)}, u32[]{:S(2)}) collective-permute-start(bf16[64,896]{1,0:T(8,128)(2,1)S(1)} %get-tuple-element.23), channel_id=1, source_target_pairs={{0,96},{1,224},{2,0},{3,128},{32,32},{33,160},{34,64},{35,192},{64... | collective-permute-start | bytes 344072 | tf_op jit(solution)/shard_map/ppermute | solution.py:205

commit v3 on v2

--- a/solution.py
+++ b/solution.py
@@ -13,6 +13,7 @@
 AXES = ("x", "yh", "z", "yl", "c")
 SIZES = (4, 2, 8, 2, 2)
 SPAN = 32
+HALF = SPAN // 2
 GROUP = 16
 KEYS = SPAN * GROUP
 MAXB = 5
@@ -21,15 +22,19 @@
 
 
 def attention_kernel(
-    starts, place, slot, q_ref, w_hbm, own_ref, oth_ref, out_ref,
-    k_buf, s_buf, top_buf, sum_buf, acc, mixed, w_buf, w_sem,
+    starts, place, slot, q_hbm, w_hbm, own_ref, oth_ref, out_ref,
+    k_buf, s_buf, top_buf, sum_buf, acc, mixed, q_ref, w_buf, head_out, q_sem, w_sem, out_sem,
 ):
     span_total = place.shape[0]
-    heads = q_ref.shape[1]
+    heads = q_hbm.shape[1]
+    q_copy = pltpu.make_async_copy(q_hbm, q_ref, q_sem)
+    q_copy.start()
     rows = SPAN * heads
     value_cols = w_hbm.shape[1]
     scale = (VD + ROPE) ** (-0.5) * 1.4426950408889634
     core = slot[2]
+    line_rows = 8 * HALF
+    low_lanes = lax.broadcasted_iota(jnp.int32, (HALF, 2 * ROPE), 1) < ROPE
 
     w_copy = pltpu.make_async_copy(w_hbm, w_buf, w_sem)
     w_copy.start()
@@ -39,6 +44,10 @@
         for d in range(DOCS):
             lo = jnp.maximum(lo, jnp.where(starts[d] <= pos, starts[d], 0))
         return lo
+
+    lane = lax.broadcasted_iota(jnp.int32, (1, KEYS), 1)
+    key_half = jnp.where(lane < KEYS // 2, core, 1 - core)
+    key_place = ((lane & (KEYS // 2 - 1)) >> 4) * SPAN + key_half * HALF + (lane & (HALF - 1))
 
     for t in range(2):
         last = slot[t]
@@ -51,22 +60,35 @@
         q_pos = last * SPAN + row_token
         q_lo = doc_start(q_pos) - first * SPAN
         q_hi = q_pos - first * SPAN
+        if t == 0:
+            q_copy.wait()
         q = q_ref[t * SPAN : (t + 1) * SPAN].reshape(rows, q_ref.shape[2])
+        q = jnp.concatenate([q, q[:, value_cols:]], axis=1)
         top_buf[...] = jnp.full(top_buf.shape, NEG, jnp.float32)
         sum_buf[...] = jnp.zeros(sum_buf.shape, jnp.float32)
         acc[...] = jnp.zeros(acc.shape, jnp.float32)
 
         def score(b, carry):
             for g in range(GROUP):
-                stored = place[jnp.minimum(first + b * GROUP + g, span_total - 1)]
-                mine = lax.rem(stored, 2) == core
-                k_buf[b, g * SPAN : (g + 1) * SPAN] = jnp.where(
-                    mine, own_ref[stored // 2], oth_ref[stored // 2]
-                )
+                code = place[jnp.minimum(first + b * GROUP + g, span_total - 1)]
+                block = lax.shift_right_logical(code, 3)
+                z = code & 7
+                for i, ref in enumerate((own_ref, oth_ref)):
+                    row = i * KEYS // 2 + g * HALF
+                    for j in range(value_cols // 128):
+                        src = pl.multiple_of(j * line_rows + z * HALF, HALF)
+                        k_buf[b, row : row + HALF, j * 128 : (j + 1) * 128] = ref[
+                            block, pl.ds(src, HALF)
+                        ]
+                    src = pl.multiple_of(value_cols // 128 * line_rows + (z & 3) * HALF, HALF)
+                    rope = ref[block, pl.ds(src, HALF)]
+                    k_buf[b, row : row + HALF, value_cols:] = jnp.where(
+                        low_lanes == (z < 4), rope, jnp.zeros_like(rope)
+                    )
             s = lax.dot_general(
                 q, k_buf[b], (((1,), (1,)), ((), ())), preferred_element_type=jnp.float32
             )
-            k_pos = b * KEYS + lax.broadcasted_iota(jnp.int32, (1, KEYS), 1)
+            k_pos = b * KEYS + key_place
             s = jnp.where((k_pos >= q_lo) & (k_pos <= q_hi), s, NEG)
             s_buf[b] = s
             top = top_buf[...]
@@ -91,19 +113,38 @@
 
         lax.fori_loop(0, blocks, mix, 0)
         total = jnp.sum(sum_buf[...], axis=1, keepdims=True)
-        scaled = acc[...] / total
+        scaled = acc[...] * (1.0 / total)
         for j in range(value_cols // 128):
             mixed[j, t * rows : (t + 1) * rows, :] = scaled[:, j * 128 : (j + 1) * 128]
 
     w_copy.wait()
     tokens = 2 * SPAN
-    for h in range(heads):
-        part = jnp.concatenate(
-            [mixed[j, pl.ds(h, tokens, stride=heads), :] for j in range(value_cols // 128)], axis=1
+    for h in range(0, heads, 2):
+        pair = jnp.concatenate(
+            [
+                jnp.concatenate(
+                    [mixed[j, pl.ds(h + i, tokens, stride=heads), :] for j in range(value_cols // 128)],
+                    axis=1,
+                )
+                for i in range(2)
+            ],
+            axis=0,
         ).astype(jnp.bfloat16)
-        piece = jnp.dot(part, w_buf[h], preferred_element_type=jnp.float32).astype(jnp.bfloat16)
-        for r in range(out_ref.shape[0]):
-            out_ref[r, :, h * VD : (h + 1) * VD] = piece
+        both = jnp.dot(
+            pair,
+            jnp.concatenate([w_buf[h], w_buf[h + 1]], axis=1),
+            preferred_element_type=jnp.float32,
+        ).astype(jnp.bfloat16)
+        head_out[:, h * VD : (h + 1) * VD] = both[:tokens, :VD]
+        head_out[:, (h + 1) * VD : (h + 2) * VD] = both[tokens:, VD:]
+    copies = [
+        pltpu.make_async_copy(head_out, out_ref.at[r], out_sem.at[r])
+        for r in range(out_ref.shape[0])
+    ]
+    for copy in copies:
+        copy.start()
+    for copy in copies:
+        copy.wait()
 
 
 def attention(starts, place, slot, queries, w_uv, own, oth):
@@ -116,23 +157,63 @@
     return pl.pallas_call(
         attention_kernel,
         out_shape=jax.ShapeDtypeStruct((COPIES, tokens, heads * VD), jnp.bfloat16),
-        in_specs=[smem, smem, smem, vmem, hbm, vmem, vmem],
-        out_specs=vmem,
+        in_specs=[smem, smem, smem, hbm, hbm, vmem, vmem],
+        out_specs=hbm,
         scratch_shapes=[
-            pltpu.VMEM((MAXB, KEYS, lat), jnp.bfloat16),
+            pltpu.VMEM((MAXB, KEYS, lat + ROPE), jnp.bfloat16),
             pltpu.VMEM((MAXB, rows, KEYS), jnp.float32),
             pltpu.VMEM((rows, 128), jnp.float32),
             pltpu.VMEM((rows, 128), jnp.float32),
             pltpu.VMEM((rows, value_cols), jnp.float32),
             pltpu.VMEM((value_cols // 128, 2 * rows, 128), jnp.float32),
+            pltpu.VMEM(queries.shape, jnp.bfloat16),
             pltpu.VMEM(w_uv.shape, jnp.bfloat16),
+            pltpu.VMEM((tokens, heads * VD), jnp.bfloat16),
             pltpu.SemaphoreType.DMA(()),
+            pltpu.SemaphoreType.DMA(()),
+            pltpu.SemaphoreType.DMA((COPIES,)),
         ],
-        compiler_params=pltpu.CompilerParams(vmem_limit_bytes=40 * 2**20),
+        compiler_params=pltpu.CompilerParams(vmem_limit_bytes=50 * 2**20),
         cost_estimate=pl.CostEstimate(
             flops=5_000_000_000, bytes_accessed=8_000_000, transcendentals=2_000_000
         ),
     )(starts, place, slot, queries, w_uv, own, oth)
+
+
+def pack_kernel(line_ref, out_ref, buf, sem):
+    blocks, rows, width = line_ref.shape
+    count = blocks * rows
+    value_cols = width - ROPE
+    for j in range(value_cols // 128):
+        buf[j * count : (j + 1) * count] = line_ref[:, :, j * 128 : (j + 1) * 128].reshape(count, 128)
+    rope = line_ref[:, :, value_cols:].reshape(count, ROPE)
+    first = value_cols // 128 * count
+    buf[first : first + count // 2] = jnp.concatenate(
+        [rope[: count // 2], rope[count // 2 :]], axis=1
+    )
+    copies = [
+        pltpu.make_async_copy(buf, out_ref.at[r], sem.at[r]) for r in range(out_ref.shape[0])
+    ]
+    for copy in copies:
+        copy.start()
+    for copy in copies:
+        copy.wait()
+
+
+def pack(line, count):
+    rows = line.shape[0] * line.shape[1] * line.shape[2] // 128
+    return pl.pallas_call(
+        pack_kernel,
+        out_shape=jax.ShapeDtypeStruct((count, rows, 128), jnp.bfloat16),
+        in_specs=[pl.BlockSpec(memory_space=pltpu.VMEM)],
+        out_specs=pl.BlockSpec(memory_space=pl.ANY),
+        scratch_shapes=[
+            pltpu.VMEM((rows, 128), jnp.bfloat16),
+            pltpu.SemaphoreType.DMA((count,)),
+        ],
+        compiler_params=pltpu.CompilerParams(vmem_limit_bytes=58 * 2**20),
+        cost_estimate=pl.CostEstimate(flops=0, bytes_accessed=3_000_000, transcendentals=0),
+    )(line)
 
 
 def gather_rows(v, axes, count):
@@ -151,22 +232,26 @@
 
     w_own = w_out.T
     half = 64
-    span = lax.dynamic_slice_in_dim(latent, core * SPAN, SPAN)
-    line = gather_rows(span, "z", 8)
+    quarter = ai("yl") * 2 + core
+    line = gather_rows(lax.dynamic_slice_in_dim(latent, quarter * HALF, HALF), "z", 8)
     line, w_own = tie((line, w_own))
 
     up1, down1 = shift(w_own, 1), shift(w_own, -1)
     up2, down2 = shift(up1, 1), shift(down1, -1)
-    own = gather_rows(line, row_axes, COPIES).reshape(64, SPAN, latent.shape[1])
-    own, up2, down2 = tie((own, up2, down2))
-
+    own = lax.all_to_all(pack(line, 16), ("x", "yh", "yl"), 0, 0)
     up3, down3 = shift(up2, 1), shift(down2, -1)
+    w_all = jnp.zeros((8,) + w_own.shape, w_own.dtype)
+    for k, v in ((0, w_own), (1, up1), (7, down1)):
+        w_all = lax.dynamic_update_index_in_dim(w_all, v, (zi - k) % 8, 0)
+    own, up2, down2, w_all = tie((own, up2, down2, w_all))
+
     oth = lax.ppermute(own, "c", [(0, 1), (1, 0)])
     starts = jnp.sum(
         documents[None, :] < jnp.arange(DOCS, dtype=jnp.int32)[:, None], axis=1, dtype=jnp.int32
     )
     spans = jnp.arange(span_order.shape[0], dtype=jnp.int32)
-    stored = jnp.sum(jnp.where(span_order[None, :] == spans[:, None], spans[None, :], 0), axis=1)
+    where = (spans // 16 * 2 + spans % 2) * 8 + spans // 2 % 8
+    stored = jnp.sum(jnp.where(span_order[None, :] == spans[:, None], where[None, :], 0), axis=1)
     slot = jnp.concatenate(
         [lax.dynamic_slice_in_dim(span_order, 2 * (place * 8 + zi), 2), core[None].astype(jnp.int32)]
     )
@@ -176,8 +261,7 @@
     far = jnp.concatenate([shift(up3[:half], 1), shift(down3[half:], -1)], axis=0)
     tokens = head_out.shape[1]
     rows = lax.all_to_all(head_out, row_axes, 0, 0).reshape(COPIES * tokens, head_out.shape[2])
-    w_all = jnp.zeros((8,) + w_own.shape, w_own.dtype)
-    for k, v in enumerate((w_own, up1, up2, up3, far, down3, down2, down1)):
+    for k, v in ((2, up2), (6, down2), (3, up3), (5, down3), (4, far)):
         w_all = lax.dynamic_update_index_in_dim(w_all, v, (zi - k) % 8, 0)
     w_cols = w_all.reshape(-1, w_own.shape[1])
     terms = lax.dot_general(

time: 144 us -> 138 us (0.958)
  waiting for transfers between devices: 55.3 us -> 45 us
  Pallas kernels: 9.34 us -> 14.9 us
  starting transfers between devices: 38.5 us -> 43.7 us
  local copies, waits for them, and re-layouts: 13.8 us -> 10 us
  blocking collectives: 20.5 us -> 17.1 us
    all_to_all x1, waiting for transfers between devices: 15 us -> 7.47 us  [shards(): own = lax.all_to_all(pack(line, 16), ('x', 'yh', 'yl'), 0, 0)]
    ppermute x8, waiting for transfers between devices: 21 us -> 14.6 us  [shift(): return lax.ppermute(v, 'z', [(i, (i + k) % 8) for i in range(8)])]
    unnamed x28 -> x12, local copies, waits for them, and re-layouts: 5.02 us -> 0.91 us
    ppermute x1, starting transfers between devices: 2.5 us -> 5.96 us  [shards(): oth = lax.ppermute(own, 'c', [(0, 1), (1, 0)])]
    all_to_all x1, blocking collectives: 20.5 us -> 17.1 us  [gather_rows(): lax.all_to_all(jnp.broadcast_to(v[None], (count,) + v.shape), axes, 0, 0)]
    pallas_call x1, Pallas kernels: 9.34 us -> 12.3 us  [attention(): pl.pallas_call(attention_kernel, out_shape=jax.ShapeDtypeStruct((COPIES,...]
    pallas_call x0 -> x1, Pallas kernels: none -> 2.62 us  [pack(): pl.pallas_call(pack_kernel, out_shape=jax.ShapeDtypeStruct((count, rows,...]
    all_to_all x1, waiting for transfers between devices: 15.5 us -> 17.8 us  [shards(): lax.all_to_all(head_out, row_axes, 0, 0)]
  transfers between devices with their start and end apart: 16 -> 16, of which waited for: 8 -> 9; matrix products, arithmetic and copies ran while one was open for 6% -> 7% of each run, Pallas kernels for 6% -> 9%
where the time goes in v3:
time: 138 us
  waiting for transfers between devices  45 us (33%)
  starting transfers between devices  43.7 us (32%)
  blocking collectives  17.1 us (12%)
  Pallas kernels  14.9 us (11%)
  local copies, waits for them, and re-layouts  10 us (7%)
  matrix products  4.4 us (3%)
  other arithmetic  2.12 us (2%)
    all_to_all x1, waiting for transfers between devices, shards(): lax.all_to_all(head_out, row_axes, 0, 0)  17.8 us
    all_to_all x1, blocking collectives, gather_rows(): lax.all_to_all(jnp.broadcast_to(v[None], (count,) + v.shape), axes, 0, 0)  17.1 us
    ppermute x8, waiting for transfers between devices, shift(): return lax.ppermute(v, 'z', [(i, (i + k) % 8) for i in range(8)])  14.6 us
    ppermute x4, starting transfers between devices, shards(): got = lax.ppermute(block, ('x', 'yh', 'yl', 'c'), pairs).astype(jnp.float32)  13.9 us
    pallas_call x1, Pallas kernels, attention(): pl.pallas_call(attention_kernel, out_shape=jax.ShapeDtypeStruct((COPIES,...  12.3 us
    ppermute x8, starting transfers between devices, shift(): return lax.ppermute(v, 'z', [(i, (i + k) % 8) for i in range(8)])  11.7 us
    all_to_all x1, waiting for transfers between devices, shards(): own = lax.all_to_all(pack(line, 16), ('x', 'yh', 'yl'), 0, 0)  7.47 us
    all_to_all x1, starting transfers between devices, shards(): own = lax.all_to_all(pack(line, 16), ('x', 'yh', 'yl'), 0, 0)  6.81 us
  transfers between devices with their start and end apart: 16, of which 9 were waited for; matrix products, arithmetic and copies ran while one was open for 7% of the time, Pallas kernels for 9%

profile of v3, /device:TPU:1, one launch (start us, length us, event | category | flops | bytes accessed | tf_op | source)
XLA Modules:
  0.0 137.6 jit_solution(2526344958431406845)
XLA Ops:
  0.0 0.0 copy-start
  0.0 0.9 copy-done
  0.9 17.1 %all_to_all.15.line_ref = bf16[8,16,576]{2,1,0:T(8,128)(2,1)} all-to-all(bf16[8,16,576]{2,1,0:T(8,128)(2,1)S(1)} %broadcast_in_dim.69), channel_id=1, replica_groups=mesh['x'=4,'yh'=2,'z'=8,'yl'=2,'c'=2] {'z'}, dimensions={0} | all-to-all | bytes 294912 | tf_op jit(solution)/shard_map/all_to_all | solution.py:220
  18.0 0.0 copy-start.2
  18.0 2.6 %shard_map.64 = bf16[16,576,128]{2,1,0:T(8,128)(2,1)} custom-call(bf16[8,16,576]{2,1,0:T(8,128)(2,1)} %all_to_all.15.line_ref), custom_call_target="tpu_custom_call" | custom-call | bytes 3000000 | tf_op jit(solution)/shard_map/pallas_call | solution.py:205
  20.6 6.8 %all-to-all-start.1 = ((bf16[16,576,128]{2,1,0:T(8,128)(2,1)}), bf16[16,576,128]{2,1,0:T(8,128)(2,1)}, u32[]{:S(2)}, u32[]{:S(2)}) async-start(bf16[16,576,128]{2,1,0:T(8,128)(2,1)} %shard_map.64), calls=%async_computation.1 | async-start | bytes 4718592 | tf_op jit(solution)/shard_map/all_to_all | solution.py:241
  27.4 0.0 copy-start.5
  27.4 0.0 copy-start.4
  27.4 0.0 copy-start.1
  27.5 0.0 copy-done.2
  27.5 0.7 collective-permute-start
  28.2 2.1 %collective-permute-start.2 = (bf16[112,2048]{1,0:T(8,128)(2,1)S(1)}, bf16[112,2048]{1,0:T(8,128)(2,1)S(1)}, u32[]{:S(2)}, u32[]{:S(2)}) collective-permute-start(bf16[112,2048]{1,0:T(8,128)(2,1)S(1)} %bitcast.42), channel_id=1, source_target_pairs={{0,28},{4,0},{8,4},{12,8},{16,12},{20,16},{24,20},{28,24},{1,29},{... | collective-permute-start | bytes 1376264 | tf_op jit(solution)/shard_map/ppermute | solution.py:231
  30.3 2.2 %broadcast_in_dim.70 = bf16[8,112,2048]{2,1,0:T(8,128)(2,1)} broadcast(bf16[]{:T(256)} %constant.209.clone.1), dimensions={} | broadcast | bytes 3670018 | tf_op jit(solution)/shard_map/broadcast_in_dim | solution.py:243
  32.5 0.8 bitcast_dynamic-update-slice_fusion.6
  33.3 4.8 %collective-permute-done = bf16[112,2048]{1,0:T(8,128)(2,1)S(1)} collective-permute-done((bf16[112,2048]{1,0:T(8,128)(2,1)S(1)}, bf16[112,2048]{1,0:T(8,128)(2,1)S(1)}, u32[]{:S(2)}, u32[]{:S(2)}) %collective-permute-start) | collective-permute-done | bytes 458784 | tf_op jit(solution)/shard_map/ppermute | solution.py:231
  38.1 0.0 collective-permute-start.1
  38.1 0.0 collective-permute-done.2
  38.1 2.7 %collective-permute-start.3 = (bf16[112,2048]{1,0:T(8,128)(2,1)S(1)}, bf16[112,2048]{1,0:T(8,128)(2,1)S(1)}, u32[]{:S(2)}, u32[]{:S(2)}) collective-permute-start(bf16[112,2048]{1,0:T(8,128)(2,1)S(1)} %collective-permute-done.2), channel_id=1, source_target_pairs={{0,28},{4,0},{8,4},{12,8},{16,12},{20,16},{24,20},{28,24},{1,29},{... | collective-permute-start | bytes 1376264 | tf_op jit(solution)/shard_map/ppermute | solution.py:231
  40.8 0.8 bitcast_dynamic-update-slice_fusion.5
  41.5 0.8 bitcast_dynamic-update-slice_fusion.4
  42.4 5.4 %collective-permute-done.1 = bf16[112,2048]{1,0:T(8,128)(2,1)S(1)} collective-permute-done((bf16[112,2048]{1,0:T(8,128)(2,1)S(1)}, bf16[112,2048]{1,0:T(8,128)(2,1)S(1)}, u32[]{:S(2)}, u32[]{:S(2)}) %collective-permute-start.1) | collective-permute-done | bytes 458784 | tf_op jit(solution)/shard_map/ppermute | solution.py:231
  47.7 0.0 collective-permute-done.3
  47.7 0.0 copy-start.3
  47.7 7.5 %all-to-all-done.1.own_ref = bf16[16,576,128]{2,1,0:T(8,128)(2,1)} async-done(((bf16[16,576,128]{2,1,0:T(8,128)(2,1)}), bf16[16,576,128]{2,1,0:T(8,128)(2,1)}, u32[]{:S(2)}, u32[]{:S(2)}) %all-to-all-start.1) | async-done | bytes 2359328 | tf_op jit(solution)/shard_map/all_to_all | solution.py:241
  55.2 6.0 %collective-permute-start.4 = (bf16[16,576,128]{2,1,0:T(8,128)(2,1)}, bf16[16,576,128]{2,1,0:T(8,128)(2,1)}, u32[]{:S(2)}, u32[]{:S(2)}) collective-permute-start(bf16[16,576,128]{2,1,0:T(8,128)(2,1)} %all-to-all-done.1.own_ref), channel_id=1, source_target_pairs={{0,1},{1,0},{2,3},{3,2},{4,5},{5,4},{6,7},{7,6},{8,9},{9,8},{10,11... | collective-permute-start | bytes 7077896 | tf_op jit(solution)/shard_map/ppermute | solution.py:248
  61.2 0.0 copy-done.5
  61.2 0.1 dynamic_slice.26
  61.2 0.1 pad_add_fusion.slot
  61.3 0.1 select_reduce_fusion.place
  61.4 0.0 copy-done.4
  61.4 0.1 convert_reduce_fusion.starts
  61.6 0.7 collective-permute-start.5
  62.2 2.1 %collective-permute-start.6 = (bf16[112,2048]{1,0:T(8,128)(2,1)S(1)}, bf16[112,2048]{1,0:T(8,128)(2,1)S(1)}, u32[]{:S(2)}, u32[]{:S(2)}) collective-permute-start(bf16[112,2048]{1,0:T(8,128)(2,1)S(1)} %collective-permute-done.3), channel_id=1, source_target_pairs={{0,28},{4,0},{8,4},{12,8},{16,12},{20,16},{24,20},{28,24},{1,29},{... | collective-permute-start | bytes 1376264 | tf_op jit(solution)/shard_map/ppermute | solution.py:231
  64.3 1.3 collective-permute-done.4.oth_ref
  65.7 0.0 copy-done.1
  65.7 12.3 %shard_map.65 = bf16[8,64,2048]{2,1,0:T(8,128)(2,1)} custom-call(s32[6]{0:T(128)S(1)} %convert_reduce_fusion.starts, s32[128]{0:T(128)S(1)} %select_reduce_fusion.place, s32[3]{0:T(128)S(1)} %pad_add_fusion.slot, bf16[64,16,576]{2,1,0:T(8,128)(2,1)S(1)} %copy-done.1, bf16[16,512,128]{2,1,0:T(8,128)(2,1)} %w_hbm.1, ...), custom_call_target="tpu_custom_call" | custom-call | flops 5000000000 | bytes 8000000 | tf_op jit(solution)/shard_map/pallas_call | solution.py:157
  78.0 0.0 collective-permute-done.5
  78.0 0.0 collective-permute-done.6
  78.0 0.0 copy-done.3
  78.0 3.7 %all-to-all-start.2 = ((bf16[8,64,2048]{2,1,0:T(8,128)(2,1)}), bf16[8,64,2048]{2,1,0:T(8,128)(2,1)S(1)}, u32[]{:S(2)}, u32[]{:S(2)}) async-start(bf16[8,64,2048]{2,1,0:T(8,128)(2,1)} %shard_map.65), calls=%async_computation.2 | async-start | bytes 4194304 | tf_op jit(solution)/shard_map/all_to_all | solution.py:263
  81.8 0.8 bitcast_dynamic-update-slice_fusion.3
  82.6 1.8 %bitcast_dynamic-update-slice_fusion.2 = bf16[8,112,2048]{2,1,0:T(8,128)(2,1)} fusion(bf16[8,112,2048]{2,1,0:T(8,128)(2,1)} %bitcast_dynamic-update-slice_fusion.3, s32[]{:T(128)S(6)} %select_n.222, bf16[112,2048]{1,0:T(8,128)(2,1)} %copy-done.3), kind=kLoop, calls=%fused_computation.7 | loop fusion | bytes 917508 | tf_op jit(solution)/shard_map/jit(dynamic_update_index_in_dim)/dynamic_update_slice | solution.py:265
  84.4 1.4 %collective-permute-start.7 = (bf16[64,2048]{1,0:T(8,128)(2,1)S(1)}, bf16[64,2048]{1,0:T(8,128)(2,1)S(1)}, u32[]{:S(2)}, u32[]{:S(2)}) collective-permute-start(bf16[64,2048]{1,0:T(8,128)(2,1)S(1)} %slice.6), channel_id=1, source_target_pairs={{0,4},{4,8},{8,12},{12,16},{16,20},{20,24},{24,28},{28,0},{1,5},{5... | collective-permute-start | bytes 786440 | tf_op jit(solution)/shard_map/ppermute | solution.py:231
  85.9 2.2 %collective-permute-start.8 = (bf16[48,2048]{1,0:T(8,128)(2,1)S(1)}, bf16[48,2048]{1,0:T(8,128)(2,1)S(1)}, u32[]{:S(2)}, u32[]{:S(2)}) collective-permute-start(bf16[48,2048]{1,0:T(8,128)(2,1)S(1)} %slice.7), channel_id=1, source_target_pairs={{0,28},{4,0},{8,4},{12,8},{16,12},{20,16},{24,20},{28,24},{1,29},{... | collective-permute-start | bytes 589832 | tf_op jit(solution)/shard_map/ppermute | solution.py:231
  88.0 0.8 bitcast_dynamic-update-slice_fusion.1
  88.8 0.8 bitcast_dynamic-update-slice_fusion
  89.6 2.3 %collective-permute-done.8 = bf16[48,2048]{1,0:T(8,128)(2,1)S(1)} collective-permute-done((bf16[48,2048]{1,0:T(8,128)(2,1)S(1)}, bf16[48,2048]{1,0:T(8,128)(2,1)S(1)}, u32[]{:S(2)}, u32[]{:S(2)}) %collective-permute-start.8) | collective-permute-done | bytes 196640 | tf_op jit(solution)/shard_map/ppermute | solution.py:231
  91.9 2.2 %collective-permute-done.7 = bf16[64,2048]{1,0:T(8,128)(2,1)S(1)} collective-permute-done((bf16[64,2048]{1,0:T(8,128)(2,1)S(1)}, bf16[64,2048]{1,0:T(8,128)(2,1)S(1)}, u32[]{:S(2)}, u32[]{:S(2)}) %collective-permute-start.7) | collective-permute-done | bytes 262176 | tf_op jit(solution)/shard_map/ppermute | solution.py:231
  94.1 0.8 fusion.1
  94.9 17.8 %all-to-all-done.2 = bf16[8,64,2048]{2,1,0:T(8,128)(2,1)S(1)} async-done(((bf16[8,64,2048]{2,1,0:T(8,128)(2,1)}), bf16[8,64,2048]{2,1,0:T(8,128)(2,1)S(1)}, u32[]{:S(2)}, u32[]{:S(2)}) %all-to-all-start.2) | async-done | bytes 2097184 | tf_op jit(solution)/shard_map/all_to_all | solution.py:263
  112.7 4.4 %convolution_convert_fusion = bf16[512,896]{1,0:T(8,128)(2,1)S(1)} fusion(bf16[512,2048]{1,0:T(8,128)(2,1)S(1)} %bitcast.38, bf16[896,2048]{1,0:T(8,128)(2,1)} %bitcast.11), kind=kOutput, calls=%fused_computation | convolution fusion | flops 1879506944 | bytes 6684672 | tf_op jit(solution)/shard_map/dot_general | solution.py:267
  117.2 1.5 %collective-permute-start.9 = (bf16[4,64,896]{2,1,0:T(8,128)(2,1)S(1)}, bf16[4,64,896]{2,1,0:T(8,128)(2,1)S(1)}, u32[]{:S(2)}, u32[]{:S(2)}) collective-permute-start(bf16[4,64,896]{2,1,0:T(8,128)(2,1)S(1)} %dynamic-slice_bitcast_fusion), channel_id=1, source_target_pairs={{0,1},{1,0},{2,3},{3,2},{4,5},{5,4},{6,7},{7,6},{8,9},{9,8},{10,11... | collective-permute-start | bytes 1376264 | tf_op jit(solution)/shard_map/ppermute | solution.py:275
  118.7 1.4 %collective-permute-done.9 = bf16[4,64,896]{2,1,0:T(8,128)(2,1)S(1)} collective-permute-done((bf16[4,64,896]{2,1,0:T(8,128)(2,1)S(1)}, bf16[4,64,896]{2,1,0:T(8,128)(2,1)S(1)}, u32[]{:S(2)}, u32[]{:S(2)}) %collective-permute-start.9) | collective-permute-done | bytes 458784 | tf_op jit(solution)/shard_map/ppermute | solution.py:275
  120.1 0.1 fusion
  120.3 2.5 %collective-permute-start.10 = (bf16[64,896]{1,0:T(8,128)(2,1)S(1)}, bf16[64,896]{1,0:T(8,128)(2,1)S(1)}, u32[]{:S(2)}, u32[]{:S(2)}) collective-permute-start(bf16[64,896]{1,0:T(8,128)(2,1)S(1)} %get-tuple-element.28), channel_id=1, source_target_pairs={{0,0},{1,128},{2,32},{3,160},{32,64},{33,192},{34,96},{35,224},{64... | collective-permute-start | bytes 344072 | tf_op jit(solution)/shard_map/ppermute | solution.py:289
  122.8 4.0 %collective-permute-start.11 = (bf16[64,896]{1,0:T(8,128)(2,1)S(1)}, bf16[64,896]{1,0:T(8,128)(2,1)S(1)}, u32[]{:S(2)}, u32[]{:S(2)}) collective-permute-start(bf16[64,896]{1,0:T(8,128)(2,1)S(1)} %get-tuple-element.27), channel_id=1, source_target_pairs={{0,32},{1,160},{2,64},{3,192},{32,96},{33,224},{34,0},{35,128},{64... | collective-permute-start | bytes 344072 | tf_op jit(solution)/shard_map/ppermute | solution.py:289
  126.8 2.4 %collective-permute-start.12 = (bf16[64,896]{1,0:T(8,128)(2,1)S(1)}, bf16[64,896]{1,0:T(8,128)(2,1)S(1)}, u32[]{:S(2)}, u32[]{:S(2)}) collective-permute-start(bf16[64,896]{1,0:T(8,128)(2,1)S(1)} %get-tuple-element.26), channel_id=1, source_target_pairs={{0,64},{1,192},{2,96},{3,224},{32,0},{33,128},{34,32},{35,160},{64... | collective-permute-start | bytes 344072 | tf_op jit(solution)/shard_map/ppermute | solution.py:289
  129.2 5.0 %collective-permute-start.13 = (bf16[64,896]{1,0:T(8,128)(2,1)S(1)}, bf16[64,896]{1,0:T(8,128)(2,1)S(1)}, u32[]{:S(2)}, u32[]{:S(2)}) collective-permute-start(bf16[64,896]{1,0:T(8,128)(2,1)S(1)} %get-tuple-element.25), channel_id=1, source_target_pairs={{0,96},{1,224},{2,0},{3,128},{32,32},{33,160},{34,64},{35,192},{64... | collective-permute-start | bytes 344072 | tf_op jit(solution)/shard_map/ppermute | solution.py:289
  134.4 0.0 collective-permute-done.10
  134.4 0.0 collective-permute-done.11
  134.4 0.0 collective-permute-done.12
  134.4 2.4 %collective-permute-done.13 = bf16[64,896]{1,0:T(8,128)(2,1)S(1)} collective-permute-done((bf16[64,896]{1,0:T(8,128)(2,1)S(1)}, bf16[64,896]{1,0:T(8,128)(2,1)S(1)}, u32[]{:S(2)}, u32[]{:S(2)}) %collective-permute-start.13) | collective-permute-done | bytes 114720 | tf_op jit(solution)/shard_map/ppermute | solution.py:289
  136.8 0.1 fusion.5
  136.9 0.7 pad_maximum_fusion
  (7 shorter events, 0.2 us)
Async XLA Ops:
  0.0 0.9 copy-start
  18.0 9.5 %copy-start.2 = (bf16[2048,112]{0,1:T(8,128)(2,1)S(1)}, bf16[2048,112]{0,1:T(8,128)(2,1)}, u32[]{:S(2)}) copy-start(bf16[2048,112]{0,1:T(8,128)(2,1)} %param.11) | copy-start | bytes 1376260
  20.6 34.6 %all-to-all-start.1 = ((bf16[16,576,128]{2,1,0:T(8,128)(2,1)}), bf16[16,576,128]{2,1,0:T(8,128)(2,1)}, u32[]{:S(2)}, u32[]{:S(2)}) async-start(bf16[16,576,128]{2,1,0:T(8,128)(2,1)} %shard_map.64), calls=%async_computation.1 | async-start | bytes 4718592 | tf_op jit(solution)/shard_map/all_to_all | solution.py:241
  27.4 33.7 %copy-start.5 = (s32[128]{0:T(128)S(1)}, s32[128]{0:T(128)}, u32[]{:S(2)}) copy-start(s32[128]{0:T(128)} %param.9) | copy-start | bytes 1540
  27.4 34.0 %copy-start.4 = (s32[4096]{0:T(1024)S(1)}, s32[4096]{0:T(1024)}, u32[]{:S(2)}) copy-start(s32[4096]{0:T(1024)} %param.8) | copy-start | bytes 49156
  27.4 38.2 %copy-start.1 = (bf16[64,16,576]{2,1,0:T(8,128)(2,1)S(1)}, bf16[64,16,576]{2,1,0:T(8,128)(2,1)}, u32[]{:S(2)}) copy-start(bf16[64,16,576]{2,1,0:T(8,128)(2,1)} %q_hbm.1) | copy-start | bytes 3538948
  27.5 10.5 %collective-permute-start = (bf16[112,2048]{1,0:T(8,128)(2,1)S(1)}, bf16[112,2048]{1,0:T(8,128)(2,1)S(1)}, u32[]{:S(2)}, u32[]{:S(2)}) collective-permute-start(bf16[112,2048]{1,0:T(8,128)(2,1)S(1)} %bitcast.41), channel_id=1, source_target_pairs={{0,4},{4,8},{8,12},{12,16},{16,20},{20,24},{24,28},{28,0},{1,5},{5... | collective-permute-start | bytes 1376264 | tf_op jit(solution)/shard_map/ppermute | solution.py:231
  28.2 9.9 %collective-permute-start.2 = (bf16[112,2048]{1,0:T(8,128)(2,1)S(1)}, bf16[112,2048]{1,0:T(8,128)(2,1)S(1)}, u32[]{:S(2)}, u32[]{:S(2)}) collective-permute-start(bf16[112,2048]{1,0:T(8,128)(2,1)S(1)} %bitcast.42), channel_id=1, source_target_pairs={{0,28},{4,0},{8,4},{12,8},{16,12},{20,16},{24,20},{28,24},{1,29},{... | collective-permute-start | bytes 1376264 | tf_op jit(solution)/shard_map/ppermute | solution.py:231
  38.1 9.7 %collective-permute-start.1 = (bf16[112,2048]{1,0:T(8,128)(2,1)S(1)}, bf16[112,2048]{1,0:T(8,128)(2,1)S(1)}, u32[]{:S(2)}, u32[]{:S(2)}) collective-permute-start(bf16[112,2048]{1,0:T(8,128)(2,1)S(1)} %collective-permute-done), channel_id=1, source_target_pairs={{0,4},{4,8},{8,12},{12,16},{16,20},{20,24},{24,28},{28,0},{1,5},{5... | collective-permute-start | bytes 1376264 | tf_op jit(solution)/shard_map/ppermute | solution.py:231
  38.1 9.7 %collective-permute-start.3 = (bf16[112,2048]{1,0:T(8,128)(2,1)S(1)}, bf16[112,2048]{1,0:T(8,128)(2,1)S(1)}, u32[]{:S(2)}, u32[]{:S(2)}) collective-permute-start(bf16[112,2048]{1,0:T(8,128)(2,1)S(1)} %collective-permute-done.2), channel_id=1, source_target_pairs={{0,28},{4,0},{8,4},{12,8},{16,12},{20,16},{24,20},{28,24},{1,29},{... | collective-permute-start | bytes 1376264 | tf_op jit(solution)/shard_map/ppermute | solution.py:231
  47.7 30.3 %copy-start.3 = (bf16[112,2048]{1,0:T(8,128)(2,1)}, bf16[112,2048]{1,0:T(8,128)(2,1)S(1)}, u32[]{:S(2)}) copy-start(bf16[112,2048]{1,0:T(8,128)(2,1)S(1)} %collective-permute-done.3) | copy-start | bytes 1376260
  55.2 10.5 %collective-permute-start.4 = (bf16[16,576,128]{2,1,0:T(8,128)(2,1)}, bf16[16,576,128]{2,1,0:T(8,128)(2,1)}, u32[]{:S(2)}, u32[]{:S(2)}) collective-permute-start(bf16[16,576,128]{2,1,0:T(8,128)(2,1)} %all-to-all-done.1.own_ref), channel_id=1, source_target_pairs={{0,1},{1,0},{2,3},{3,2},{4,5},{5,4},{6,7},{7,6},{8,9},{9,8},{10,11... | collective-permute-start | bytes 7077896 | tf_op jit(solution)/shard_map/ppermute | solution.py:248
  61.6 16.4 %collective-permute-start.5 = (bf16[112,2048]{1,0:T(8,128)(2,1)S(1)}, bf16[112,2048]{1,0:T(8,128)(2,1)S(1)}, u32[]{:S(2)}, u32[]{:S(2)}) collective-permute-start(bf16[112,2048]{1,0:T(8,128)(2,1)S(1)} %collective-permute-done.1), channel_id=1, source_target_pairs={{0,4},{4,8},{8,12},{12,16},{16,20},{20,24},{24,28},{28,0},{1,5},{5... | collective-permute-start | bytes 1376264 | tf_op jit(solution)/shard_map/ppermute | solution.py:231
  62.2 15.8 %collective-permute-start.6 = (bf16[112,2048]{1,0:T(8,128)(2,1)S(1)}, bf16[112,2048]{1,0:T(8,128)(2,1)S(1)}, u32[]{:S(2)}, u32[]{:S(2)}) collective-permute-start(bf16[112,2048]{1,0:T(8,128)(2,1)S(1)} %collective-permute-done.3), channel_id=1, source_target_pairs={{0,28},{4,0},{8,4},{12,8},{16,12},{20,16},{24,20},{28,24},{1,29},{... | collective-permute-start | bytes 1376264 | tf_op jit(solution)/shard_map/ppermute | solution.py:231
  78.0 34.7 %all-to-all-start.2 = ((bf16[8,64,2048]{2,1,0:T(8,128)(2,1)}), bf16[8,64,2048]{2,1,0:T(8,128)(2,1)S(1)}, u32[]{:S(2)}, u32[]{:S(2)}) async-start(bf16[8,64,2048]{2,1,0:T(8,128)(2,1)} %shard_map.65), calls=%async_computation.2 | async-start | bytes 4194304 | tf_op jit(solution)/shard_map/all_to_all | solution.py:263
  84.4 9.6 %collective-permute-start.7 = (bf16[64,2048]{1,0:T(8,128)(2,1)S(1)}, bf16[64,2048]{1,0:T(8,128)(2,1)S(1)}, u32[]{:S(2)}, u32[]{:S(2)}) collective-permute-start(bf16[64,2048]{1,0:T(8,128)(2,1)S(1)} %slice.6), channel_id=1, source_target_pairs={{0,4},{4,8},{8,12},{12,16},{16,20},{20,24},{24,28},{28,0},{1,5},{5... | collective-permute-start | bytes 786440 | tf_op jit(solution)/shard_map/ppermute | solution.py:231
  85.9 6.0 %collective-permute-start.8 = (bf16[48,2048]{1,0:T(8,128)(2,1)S(1)}, bf16[48,2048]{1,0:T(8,128)(2,1)S(1)}, u32[]{:S(2)}, u32[]{:S(2)}) collective-permute-start(bf16[48,2048]{1,0:T(8,128)(2,1)S(1)} %slice.7), channel_id=1, source_target_pairs={{0,28},{4,0},{8,4},{12,8},{16,12},{20,16},{24,20},{28,24},{1,29},{... | collective-permute-start | bytes 589832 | tf_op jit(solution)/shard_map/ppermute | solution.py:231
  117.2 3.0 %collective-permute-start.9 = (bf16[4,64,896]{2,1,0:T(8,128)(2,1)S(1)}, bf16[4,64,896]{2,1,0:T(8,128)(2,1)S(1)}, u32[]{:S(2)}, u32[]{:S(2)}) collective-permute-start(bf16[4,64,896]{2,1,0:T(8,128)(2,1)S(1)} %dynamic-slice_bitcast_fusion), channel_id=1, source_target_pairs={{0,1},{1,0},{2,3},{3,2},{4,5},{5,4},{6,7},{7,6},{8,9},{9,8},{10,11... | collective-permute-start | bytes 1376264 | tf_op jit(solution)/shard_map/ppermute | solution.py:275
  120.3 14.0 %collective-permute-start.10 = (bf16[64,896]{1,0:T(8,128)(2,1)S(1)}, bf16[64,896]{1,0:T(8,128)(2,1)S(1)}, u32[]{:S(2)}, u32[]{:S(2)}) collective-permute-start(bf16[64,896]{1,0:T(8,128)(2,1)S(1)} %get-tuple-element.28), channel_id=1, source_target_pairs={{0,0},{1,128},{2,32},{3,160},{32,64},{33,192},{34,96},{35,224},{64... | collective-permute-start | bytes 344072 | tf_op jit(solution)/shard_map/ppermute | solution.py:289
  122.8 11.5 %collective-permute-start.11 = (bf16[64,896]{1,0:T(8,128)(2,1)S(1)}, bf16[64,896]{1,0:T(8,128)(2,1)S(1)}, u32[]{:S(2)}, u32[]{:S(2)}) collective-permute-start(bf16[64,896]{1,0:T(8,128)(2,1)S(1)} %get-tuple-element.27), channel_id=1, source_target_pairs={{0,32},{1,160},{2,64},{3,192},{32,96},{33,224},{34,0},{35,128},{64... | collective-permute-start | bytes 344072 | tf_op jit(solution)/shard_map/ppermute | solution.py:289
  126.8 7.6 %collective-permute-start.12 = (bf16[64,896]{1,0:T(8,128)(2,1)S(1)}, bf16[64,896]{1,0:T(8,128)(2,1)S(1)}, u32[]{:S(2)}, u32[]{:S(2)}) collective-permute-start(bf16[64,896]{1,0:T(8,128)(2,1)S(1)} %get-tuple-element.26), channel_id=1, source_target_pairs={{0,64},{1,192},{2,96},{3,224},{32,0},{33,128},{34,32},{35,160},{64... | collective-permute-start | bytes 344072 | tf_op jit(solution)/shard_map/ppermute | solution.py:289
  129.2 7.5 %collective-permute-start.13 = (bf16[64,896]{1,0:T(8,128)(2,1)S(1)}, bf16[64,896]{1,0:T(8,128)(2,1)S(1)}, u32[]{:S(2)}, u32[]{:S(2)}) collective-permute-start(bf16[64,896]{1,0:T(8,128)(2,1)S(1)} %get-tuple-element.25), channel_id=1, source_target_pairs={{0,96},{1,224},{2,0},{3,128},{32,32},{33,160},{34,64},{35,192},{64... | collective-permute-start | bytes 344072 | tf_op jit(solution)/shard_map/ppermute | solution.py:289

commit v4 on v3

--- a/solution.py
+++ b/solution.py
@@ -147,6 +147,10 @@
         copy.wait()
 
 
+def in_hbm(v):
+    return pltpu.with_memory_space_constraint(v, pltpu.HBM)
+
+
 def attention(starts, place, slot, queries, w_uv, own, oth):
     tokens, heads, lat = queries.shape
     value_cols = w_uv.shape[1]
@@ -156,7 +160,7 @@
     hbm = pl.BlockSpec(memory_space=pl.ANY)
     return pl.pallas_call(
         attention_kernel,
-        out_shape=jax.ShapeDtypeStruct((COPIES, tokens, heads * VD), jnp.bfloat16),
+        out_shape=pltpu.HBM((COPIES, tokens, heads * VD), jnp.bfloat16),
         in_specs=[smem, smem, smem, hbm, hbm, vmem, vmem],
         out_specs=hbm,
         scratch_shapes=[
@@ -173,11 +177,11 @@
             pltpu.SemaphoreType.DMA(()),
             pltpu.SemaphoreType.DMA((COPIES,)),
         ],
-        compiler_params=pltpu.CompilerParams(vmem_limit_bytes=50 * 2**20),
+        compiler_params=pltpu.CompilerParams(vmem_limit_bytes=36 * 2**20),
         cost_estimate=pl.CostEstimate(
             flops=5_000_000_000, bytes_accessed=8_000_000, transcendentals=2_000_000
         ),
-    )(starts, place, slot, queries, w_uv, own, oth)
+    )(starts, place, slot, in_hbm(queries), in_hbm(w_uv), own, oth)
 
 
 def pack_kernel(line_ref, out_ref, buf, sem):
@@ -204,14 +208,14 @@
     rows = line.shape[0] * line.shape[1] * line.shape[2] // 128
     return pl.pallas_call(
         pack_kernel,
-        out_shape=jax.ShapeDtypeStruct((count, rows, 128), jnp.bfloat16),
+        out_shape=pltpu.HBM((count, rows, 128), jnp.bfloat16),
         in_specs=[pl.BlockSpec(memory_space=pltpu.VMEM)],
         out_specs=pl.BlockSpec(memory_space=pl.ANY),
         scratch_shapes=[
             pltpu.VMEM((rows, 128), jnp.bfloat16),
             pltpu.SemaphoreType.DMA((count,)),
         ],
-        compiler_params=pltpu.CompilerParams(vmem_limit_bytes=58 * 2**20),
+        compiler_params=pltpu.CompilerParams(vmem_limit_bytes=16 * 2**20),
         cost_estimate=pl.CostEstimate(flops=0, bytes_accessed=3_000_000, transcendentals=0),
     )(line)
 

time: 138 us -> 137 us (level)
  waiting for transfers between devices: 45 us -> 48.9 us
  local copies, waits for them, and re-layouts: 10 us -> 6.95 us
    ppermute x8, waiting for transfers between devices: 14.6 us -> 18.1 us  [shift(): return lax.ppermute(v, 'z', [(i, (i + k) % 8) for i in range(8)])]
    broadcast_in_dim x1, local copies, waits for them, and re-layouts: 2.23 us -> 0.44 us  [shards(): w_all = jnp.zeros((8,) + w_own.shape, w_own.dtype)]
  transfers between devices with their start and end apart: 16 -> 16, of which waited for: 9 -> 9; matrix products, arithmetic and copies ran while one was open for 7% -> 5% of each run, Pallas kernels for 9% -> 10%
where the time goes in v4:
time: 137 us; the launch traced here: 138 us
  waiting for transfers between devices  48.9 us (36%)
  starting transfers between devices  42.9 us (31%)
  blocking collectives  17 us (12%)
  Pallas kernels  15.3 us (11%)
  local copies, waits for them, and re-layouts  6.95 us (5%)
  matrix products  4.4 us (3%)
  other arithmetic  2.11 us (2%)
    ppermute x8, waiting for transfers between devices, shift(): return lax.ppermute(v, 'z', [(i, (i + k) % 8) for i in range(8)])  18.1 us
    all_to_all x1, waiting for transfers between devices, shards(): lax.all_to_all(head_out, row_axes, 0, 0)  17.8 us
    all_to_all x1, blocking collectives, gather_rows(): lax.all_to_all(jnp.broadcast_to(v[None], (count,) + v.shape), axes, 0, 0)  17 us
    ppermute x4, starting transfers between devices, shards(): got = lax.ppermute(block, ('x', 'yh', 'yl', 'c'), pairs).astype(jnp.float32)  14.1 us
    pallas_call x1, Pallas kernels, attention(): pl.pallas_call(attention_kernel, out_shape=pltpu.HBM((COPIES, tokens, hea...  13.7 us
    ppermute x8, starting transfers between devices, shift(): return lax.ppermute(v, 'z', [(i, (i + k) % 8) for i in range(8)])  11.2 us
    all_to_all x1, waiting for transfers between devices, shards(): own = lax.all_to_all(pack(line, 16), ('x', 'yh', 'yl'), 0, 0)  7.63 us
    all_to_all x1, starting transfers between devices, shards(): own = lax.all_to_all(pack(line, 16), ('x', 'yh', 'yl'), 0, 0)  6.77 us
  transfers between devices with their start and end apart: 16, of which 9 were waited for; matrix products, arithmetic and copies ran while one was open for 5% of the time, Pallas kernels for 10%

profile of v4, /device:TPU:1, one launch (start us, length us, event | category | flops | bytes accessed | tf_op | source)
XLA Modules:
  0.0 137.9 jit_solution(7536755138256429073)
XLA Ops:
  0.0 0.0 copy-start
  0.0 0.9 copy-done
  0.9 17.0 %all_to_all.15.line_ref = bf16[8,16,576]{2,1,0:T(8,128)(2,1)S(1)} all-to-all(bf16[8,16,576]{2,1,0:T(8,128)(2,1)S(1)} %broadcast_in_dim.69), channel_id=1, replica_groups=mesh['x'=4,'yh'=2,'z'=8,'yl'=2,'c'=2] {'z'}, dimensions={0} | all-to-all | bytes 294912 | tf_op jit(solution)/shard_map/all_to_all | solution.py:224
  17.9 0.0 copy-start.2
  17.9 1.6 %shard_map.64 = bf16[16,576,128]{2,1,0:T(8,128)(2,1)} custom-call(bf16[8,16,576]{2,1,0:T(8,128)(2,1)S(1)} %all_to_all.15.line_ref), custom_call_target="tpu_custom_call" | custom-call | bytes 3000000 | tf_op jit(solution)/shard_map/pallas_call | solution.py:209
  19.5 6.8 %all-to-all-start.1 = ((bf16[16,576,128]{2,1,0:T(8,128)(2,1)}), bf16[16,576,128]{2,1,0:T(8,128)(2,1)S(1)}, u32[]{:S(2)}, u32[]{:S(2)}) async-start(bf16[16,576,128]{2,1,0:T(8,128)(2,1)} %shard_map.64), calls=%async_computation.1 | async-start | bytes 4718592 | tf_op jit(solution)/shard_map/all_to_all | solution.py:245
  26.3 0.0 copy-start.4
  26.3 0.0 copy-start.3
  26.3 0.0 copy-done.2
  26.4 0.7 collective-permute-start
  27.0 2.1 %collective-permute-start.2 = (bf16[112,2048]{1,0:T(8,128)(2,1)S(1)}, bf16[112,2048]{1,0:T(8,128)(2,1)S(1)}, u32[]{:S(2)}, u32[]{:S(2)}) collective-permute-start(bf16[112,2048]{1,0:T(8,128)(2,1)S(1)} %bitcast.43), channel_id=1, source_target_pairs={{0,28},{4,0},{8,4},{12,8},{16,12},{20,16},{24,20},{28,24},{1,29},{... | collective-permute-start | bytes 1376264 | tf_op jit(solution)/shard_map/ppermute | solution.py:235
  29.1 0.4 broadcast_in_dim.70
  29.6 7.2 %collective-permute-done = bf16[112,2048]{1,0:T(8,128)(2,1)S(1)} collective-permute-done((bf16[112,2048]{1,0:T(8,128)(2,1)S(1)}, bf16[112,2048]{1,0:T(8,128)(2,1)S(1)}, u32[]{:S(2)}, u32[]{:S(2)}) %collective-permute-start) | collective-permute-done | bytes 458784 | tf_op jit(solution)/shard_map/ppermute | solution.py:235
  36.8 0.0 collective-permute-start.1
  36.8 0.0 collective-permute-done.2
  36.8 2.7 %collective-permute-start.3 = (bf16[112,2048]{1,0:T(8,128)(2,1)S(1)}, bf16[112,2048]{1,0:T(8,128)(2,1)}, u32[]{:S(2)}, u32[]{:S(2)}) collective-permute-start(bf16[112,2048]{1,0:T(8,128)(2,1)S(1)} %collective-permute-done.2), channel_id=1, source_target_pairs={{0,28},{4,0},{8,4},{12,8},{16,12},{20,16},{24,20},{28,24},{1,29},{... | collective-permute-start | bytes 1376264 | tf_op jit(solution)/shard_map/ppermute | solution.py:235
  39.6 0.0 copy-start.1
  39.6 6.8 %collective-permute-done.1 = bf16[112,2048]{1,0:T(8,128)(2,1)} collective-permute-done((bf16[112,2048]{1,0:T(8,128)(2,1)S(1)}, bf16[112,2048]{1,0:T(8,128)(2,1)}, u32[]{:S(2)}, u32[]{:S(2)}) %collective-permute-start.1) | collective-permute-done | bytes 458784 | tf_op jit(solution)/shard_map/ppermute | solution.py:235
  46.3 0.0 copy-done.1
  46.4 0.0 collective-permute-done.3
  46.4 7.6 %all-to-all-done.1.own_ref = bf16[16,576,128]{2,1,0:T(8,128)(2,1)S(1)} async-done(((bf16[16,576,128]{2,1,0:T(8,128)(2,1)}), bf16[16,576,128]{2,1,0:T(8,128)(2,1)S(1)}, u32[]{:S(2)}, u32[]{:S(2)}) %all-to-all-start.1) | async-done | bytes 2359328 | tf_op jit(solution)/shard_map/all_to_all | solution.py:245
  54.0 6.0 %collective-permute-start.4 = (bf16[16,576,128]{2,1,0:T(8,128)(2,1)S(1)}, bf16[16,576,128]{2,1,0:T(8,128)(2,1)}, u32[]{:S(2)}, u32[]{:S(2)}) collective-permute-start(bf16[16,576,128]{2,1,0:T(8,128)(2,1)S(1)} %all-to-all-done.1.own_ref), channel_id=1, source_target_pairs={{0,1},{1,0},{2,3},{3,2},{4,5},{5,4},{6,7},{7,6},{8,9},{9,8},{10,11... | collective-permute-start | bytes 7077896 | tf_op jit(solution)/shard_map/ppermute | solution.py:252
  59.9 0.0 copy-done.4
  59.9 0.1 dynamic_slice.26
  60.0 0.1 pad_add_fusion.slot
  60.1 0.1 select_reduce_fusion.place
  60.2 0.0 copy-done.3
  60.2 0.1 convert_reduce_fusion.starts
  60.4 0.7 collective-permute-start.5
  61.0 2.1 %collective-permute-start.6 = (bf16[112,2048]{1,0:T(8,128)(2,1)}, bf16[112,2048]{1,0:T(8,128)(2,1)S(1)}, u32[]{:S(2)}, u32[]{:S(2)}) collective-permute-start(bf16[112,2048]{1,0:T(8,128)(2,1)} %collective-permute-done.3), channel_id=1, source_target_pairs={{0,28},{4,0},{8,4},{12,8},{16,12},{20,16},{24,20},{28,24},{1,29},{... | collective-permute-start | bytes 1376264 | tf_op jit(solution)/shard_map/ppermute | solution.py:235
  63.1 1.1 collective-permute-done.4.oth_ref
  64.2 13.7 %shard_map.65 = bf16[8,64,2048]{2,1,0:T(8,128)(2,1)} custom-call(s32[6]{0:T(128)S(1)} %convert_reduce_fusion.starts, s32[128]{0:T(128)S(1)} %select_reduce_fusion.place, s32[3]{0:T(128)S(1)} %pad_add_fusion.slot, bf16[64,16,576]{2,1,0:T(8,128)(2,1)} %q_hbm.1, bf16[16,512,128]{2,1,0:T(8,128)(2,1)} %w_hbm.1, bf16[16,576,128]{2,1,0:T(8,128)(2,1)S(1)} %all-to-all-done.1.own_ref, ...), custom_call_target="tpu_custom_call" | custom-call | flops 5000000000 | bytes 8000000 | tf_op jit(solution)/shard_map/pallas_call | solution.py:161
  78.0 0.0 collective-permute-done.5
  78.0 0.0 collective-permute-done.6
  78.0 3.6 %all-to-all-start.2 = ((bf16[8,64,2048]{2,1,0:T(8,128)(2,1)}), bf16[8,64,2048]{2,1,0:T(8,128)(2,1)S(1)}, u32[]{:S(2)}, u32[]{:S(2)}) async-start(bf16[8,64,2048]{2,1,0:T(8,128)(2,1)} %shard_map.65), calls=%async_computation.2 | async-start | bytes 4194304 | tf_op jit(solution)/shard_map/all_to_all | solution.py:267
  81.6 1.8 %bitcast_dynamic-update-slice_fusion.3 = bf16[8,112,2048]{2,1,0:T(8,128)(2,1)} fusion(bf16[8,112,2048]{2,1,0:T(8,128)(2,1)} %copy-done.1, s32[]{:T(128)S(6)} %select_n.220, bf16[112,2048]{1,0:T(8,128)(2,1)} %collective-permute-done.1), kind=kLoop, calls=%fused_computation.8 | loop fusion | bytes 917508 | tf_op jit(solution)/shard_map/jit(dynamic_update_index_in_dim)/dynamic_update_slice | solution.py:269
  83.5 1.8 %bitcast_dynamic-update-slice_fusion.2 = bf16[8,112,2048]{2,1,0:T(8,128)(2,1)} fusion(bf16[8,112,2048]{2,1,0:T(8,128)(2,1)} %bitcast_dynamic-update-slice_fusion.3, s32[]{:T(128)S(6)} %select_n.222, bf16[112,2048]{1,0:T(8,128)(2,1)} %collective-permute-done.3), kind=kLoop, calls=%fused_computation.7 | loop fusion | bytes 917508 | tf_op jit(solution)/shard_map/jit(dynamic_update_index_in_dim)/dynamic_update_slice | solution.py:269
  85.3 0.1 collective-permute-start.7
  85.4 2.9 %collective-permute-start.8 = (bf16[48,2048]{1,0:T(8,128)(2,1)S(1)}, bf16[48,2048]{1,0:T(8,128)(2,1)S(1)}, u32[]{:S(2)}, u32[]{:S(2)}) collective-permute-start(bf16[48,2048]{1,0:T(8,128)(2,1)S(1)} %slice.7), channel_id=1, source_target_pairs={{0,28},{4,0},{8,4},{12,8},{16,12},{20,16},{24,20},{28,24},{1,29},{... | collective-permute-start | bytes 589832 | tf_op jit(solution)/shard_map/ppermute | solution.py:235
  88.3 0.8 bitcast_dynamic-update-slice_fusion.1
  89.1 0.8 bitcast_dynamic-update-slice_fusion
  89.9 2.0 %collective-permute-done.8 = bf16[48,2048]{1,0:T(8,128)(2,1)S(1)} collective-permute-done((bf16[48,2048]{1,0:T(8,128)(2,1)S(1)}, bf16[48,2048]{1,0:T(8,128)(2,1)S(1)}, u32[]{:S(2)}, u32[]{:S(2)}) %collective-permute-start.8) | collective-permute-done | bytes 196640 | tf_op jit(solution)/shard_map/ppermute | solution.py:235
  91.9 2.2 %collective-permute-done.7 = bf16[64,2048]{1,0:T(8,128)(2,1)S(1)} collective-permute-done((bf16[64,2048]{1,0:T(8,128)(2,1)S(1)}, bf16[64,2048]{1,0:T(8,128)(2,1)S(1)}, u32[]{:S(2)}, u32[]{:S(2)}) %collective-permute-start.7) | collective-permute-done | bytes 262176 | tf_op jit(solution)/shard_map/ppermute | solution.py:235
  94.1 0.8 fusion.1
  94.9 17.8 %all-to-all-done.2 = bf16[8,64,2048]{2,1,0:T(8,128)(2,1)S(1)} async-done(((bf16[8,64,2048]{2,1,0:T(8,128)(2,1)}), bf16[8,64,2048]{2,1,0:T(8,128)(2,1)S(1)}, u32[]{:S(2)}, u32[]{:S(2)}) %all-to-all-start.2) | async-done | bytes 2097184 | tf_op jit(solution)/shard_map/all_to_all | solution.py:267
  112.7 4.4 %convolution_convert_fusion = bf16[512,896]{1,0:T(8,128)(2,1)S(1)} fusion(bf16[512,2048]{1,0:T(8,128)(2,1)S(1)} %bitcast.39, bf16[896,2048]{1,0:T(8,128)(2,1)} %bitcast.38), kind=kOutput, calls=%fused_computation | convolution fusion | flops 1879506944 | bytes 6684672 | tf_op jit(solution)/shard_map/dot_general | solution.py:271
  117.2 1.3 collective-permute-start.9
  118.5 1.4 %collective-permute-done.9 = bf16[4,64,896]{2,1,0:T(8,128)(2,1)S(1)} collective-permute-done((bf16[4,64,896]{2,1,0:T(8,128)(2,1)S(1)}, bf16[4,64,896]{2,1,0:T(8,128)(2,1)S(1)}, u32[]{:S(2)}, u32[]{:S(2)}) %collective-permute-start.9) | collective-permute-done | bytes 458784 | tf_op jit(solution)/shard_map/ppermute | solution.py:279
  119.9 0.1 fusion
  120.1 2.9 %collective-permute-start.10 = (bf16[64,896]{1,0:T(8,128)(2,1)S(1)}, bf16[64,896]{1,0:T(8,128)(2,1)S(1)}, u32[]{:S(2)}, u32[]{:S(2)}) collective-permute-start(bf16[64,896]{1,0:T(8,128)(2,1)S(1)} %get-tuple-element.28), channel_id=1, source_target_pairs={{0,0},{1,128},{2,32},{3,160},{32,64},{33,192},{34,96},{35,224},{64... | collective-permute-start | bytes 344072 | tf_op jit(solution)/shard_map/ppermute | solution.py:293
  123.1 3.8 %collective-permute-start.11 = (bf16[64,896]{1,0:T(8,128)(2,1)S(1)}, bf16[64,896]{1,0:T(8,128)(2,1)S(1)}, u32[]{:S(2)}, u32[]{:S(2)}) collective-permute-start(bf16[64,896]{1,0:T(8,128)(2,1)S(1)} %get-tuple-element.27), channel_id=1, source_target_pairs={{0,32},{1,160},{2,64},{3,192},{32,96},{33,224},{34,0},{35,128},{64... | collective-permute-start | bytes 344072 | tf_op jit(solution)/shard_map/ppermute | solution.py:293
  126.9 2.7 %collective-permute-start.12 = (bf16[64,896]{1,0:T(8,128)(2,1)S(1)}, bf16[64,896]{1,0:T(8,128)(2,1)S(1)}, u32[]{:S(2)}, u32[]{:S(2)}) collective-permute-start(bf16[64,896]{1,0:T(8,128)(2,1)S(1)} %get-tuple-element.26), channel_id=1, source_target_pairs={{0,64},{1,192},{2,96},{3,224},{32,0},{33,128},{34,32},{35,160},{64... | collective-permute-start | bytes 344072 | tf_op jit(solution)/shard_map/ppermute | solution.py:293
  129.5 4.7 %collective-permute-start.13 = (bf16[64,896]{1,0:T(8,128)(2,1)S(1)}, bf16[64,896]{1,0:T(8,128)(2,1)S(1)}, u32[]{:S(2)}, u32[]{:S(2)}) collective-permute-start(bf16[64,896]{1,0:T(8,128)(2,1)S(1)} %get-tuple-element.25), channel_id=1, source_target_pairs={{0,96},{1,224},{2,0},{3,128},{32,32},{33,160},{34,64},{35,192},{64... | collective-permute-start | bytes 344072 | tf_op jit(solution)/shard_map/ppermute | solution.py:293
  134.3 0.0 collective-permute-done.10
  134.3 0.0 collective-permute-done.11
  134.4 0.0 collective-permute-done.12
  134.4 2.7 %collective-permute-done.13 = bf16[64,896]{1,0:T(8,128)(2,1)S(1)} collective-permute-done((bf16[64,896]{1,0:T(8,128)(2,1)S(1)}, bf16[64,896]{1,0:T(8,128)(2,1)S(1)}, u32[]{:S(2)}, u32[]{:S(2)}) %collective-permute-start.13) | collective-permute-done | bytes 114720 | tf_op jit(solution)/shard_map/ppermute | solution.py:293
  137.1 0.1 fusion.5
  137.2 0.7 pad_maximum_fusion
  (10 shorter events, 0.3 us)
Async XLA Ops:
  0.0 0.9 copy-start
  17.9 8.5 %copy-start.2 = (bf16[2048,112]{0,1:T(8,128)(2,1)S(1)}, bf16[2048,112]{0,1:T(8,128)(2,1)}, u32[]{:S(2)}) copy-start(bf16[2048,112]{0,1:T(8,128)(2,1)} %param.11) | copy-start | bytes 1376260
  19.5 34.5 %all-to-all-start.1 = ((bf16[16,576,128]{2,1,0:T(8,128)(2,1)}), bf16[16,576,128]{2,1,0:T(8,128)(2,1)S(1)}, u32[]{:S(2)}, u32[]{:S(2)}) async-start(bf16[16,576,128]{2,1,0:T(8,128)(2,1)} %shard_map.64), calls=%async_computation.1 | async-start | bytes 4718592 | tf_op jit(solution)/shard_map/all_to_all | solution.py:245
  26.3 33.7 %copy-start.4 = (s32[128]{0:T(128)S(1)}, s32[128]{0:T(128)}, u32[]{:S(2)}) copy-start(s32[128]{0:T(128)} %param.9) | copy-start | bytes 1540
  26.3 33.9 %copy-start.3 = (s32[4096]{0:T(1024)S(1)}, s32[4096]{0:T(1024)}, u32[]{:S(2)}) copy-start(s32[4096]{0:T(1024)} %param.8) | copy-start | bytes 49156
  26.4 10.4 %collective-permute-start = (bf16[112,2048]{1,0:T(8,128)(2,1)S(1)}, bf16[112,2048]{1,0:T(8,128)(2,1)S(1)}, u32[]{:S(2)}, u32[]{:S(2)}) collective-permute-start(bf16[112,2048]{1,0:T(8,128)(2,1)S(1)} %bitcast.42), channel_id=1, source_target_pairs={{0,4},{4,8},{8,12},{12,16},{16,20},{20,24},{24,28},{28,0},{1,5},{5... | collective-permute-start | bytes 1376264 | tf_op jit(solution)/shard_map/ppermute | solution.py:235
  27.0 9.8 %collective-permute-start.2 = (bf16[112,2048]{1,0:T(8,128)(2,1)S(1)}, bf16[112,2048]{1,0:T(8,128)(2,1)S(1)}, u32[]{:S(2)}, u32[]{:S(2)}) collective-permute-start(bf16[112,2048]{1,0:T(8,128)(2,1)S(1)} %bitcast.43), channel_id=1, source_target_pairs={{0,28},{4,0},{8,4},{12,8},{16,12},{20,16},{24,20},{28,24},{1,29},{... | collective-permute-start | bytes 1376264 | tf_op jit(solution)/shard_map/ppermute | solution.py:235
  36.8 9.5 %collective-permute-start.1 = (bf16[112,2048]{1,0:T(8,128)(2,1)S(1)}, bf16[112,2048]{1,0:T(8,128)(2,1)}, u32[]{:S(2)}, u32[]{:S(2)}) collective-permute-start(bf16[112,2048]{1,0:T(8,128)(2,1)S(1)} %collective-permute-done), channel_id=1, source_target_pairs={{0,4},{4,8},{8,12},{12,16},{16,20},{20,24},{24,28},{28,0},{1,5},{5... | collective-permute-start | bytes 1376264 | tf_op jit(solution)/shard_map/ppermute | solution.py:235
  36.8 9.5 %collective-permute-start.3 = (bf16[112,2048]{1,0:T(8,128)(2,1)S(1)}, bf16[112,2048]{1,0:T(8,128)(2,1)}, u32[]{:S(2)}, u32[]{:S(2)}) collective-permute-start(bf16[112,2048]{1,0:T(8,128)(2,1)S(1)} %collective-permute-done.2), channel_id=1, source_target_pairs={{0,28},{4,0},{8,4},{12,8},{16,12},{20,16},{24,20},{28,24},{1,29},{... | collective-permute-start | bytes 1376264 | tf_op jit(solution)/shard_map/ppermute | solution.py:235
  39.6 6.8 %copy-start.1 = (bf16[8,112,2048]{2,1,0:T(8,128)(2,1)}, bf16[8,112,2048]{2,1,0:T(8,128)(2,1)S(1)}, u32[]{:S(2)}) copy-start(bf16[8,112,2048]{2,1,0:T(8,128)(2,1)S(1)} %bitcast_dynamic-update-slice_fusion.4) | copy-start | bytes 11010052
  54.0 10.3 %collective-permute-start.4 = (bf16[16,576,128]{2,1,0:T(8,128)(2,1)S(1)}, bf16[16,576,128]{2,1,0:T(8,128)(2,1)}, u32[]{:S(2)}, u32[]{:S(2)}) collective-permute-start(bf16[16,576,128]{2,1,0:T(8,128)(2,1)S(1)} %all-to-all-done.1.own_ref), channel_id=1, source_target_pairs={{0,1},{1,0},{2,3},{3,2},{4,5},{5,4},{6,7},{7,6},{8,9},{9,8},{10,11... | collective-permute-start | bytes 7077896 | tf_op jit(solution)/shard_map/ppermute | solution.py:252
  60.4 17.6 %collective-permute-start.5 = (bf16[112,2048]{1,0:T(8,128)(2,1)}, bf16[112,2048]{1,0:T(8,128)(2,1)S(1)}, u32[]{:S(2)}, u32[]{:S(2)}) collective-permute-start(bf16[112,2048]{1,0:T(8,128)(2,1)} %collective-permute-done.1), channel_id=1, source_target_pairs={{0,4},{4,8},{8,12},{12,16},{16,20},{20,24},{24,28},{28,0},{1,5},{5... | collective-permute-start | bytes 1376264 | tf_op jit(solution)/shard_map/ppermute | solution.py:235
  61.0 17.0 %collective-permute-start.6 = (bf16[112,2048]{1,0:T(8,128)(2,1)}, bf16[112,2048]{1,0:T(8,128)(2,1)S(1)}, u32[]{:S(2)}, u32[]{:S(2)}) collective-permute-start(bf16[112,2048]{1,0:T(8,128)(2,1)} %collective-permute-done.3), channel_id=1, source_target_pairs={{0,28},{4,0},{8,4},{12,8},{16,12},{20,16},{24,20},{28,24},{1,29},{... | collective-permute-start | bytes 1376264 | tf_op jit(solution)/shard_map/ppermute | solution.py:235
  78.0 34.7 %all-to-all-start.2 = ((bf16[8,64,2048]{2,1,0:T(8,128)(2,1)}), bf16[8,64,2048]{2,1,0:T(8,128)(2,1)S(1)}, u32[]{:S(2)}, u32[]{:S(2)}) async-start(bf16[8,64,2048]{2,1,0:T(8,128)(2,1)} %shard_map.65), calls=%async_computation.2 | async-start | bytes 4194304 | tf_op jit(solution)/shard_map/all_to_all | solution.py:267
  85.3 8.8 %collective-permute-start.7 = (bf16[64,2048]{1,0:T(8,128)(2,1)S(1)}, bf16[64,2048]{1,0:T(8,128)(2,1)S(1)}, u32[]{:S(2)}, u32[]{:S(2)}) collective-permute-start(bf16[64,2048]{1,0:T(8,128)(2,1)S(1)} %slice.6), channel_id=1, source_target_pairs={{0,4},{4,8},{8,12},{12,16},{16,20},{20,24},{24,28},{28,0},{1,5},{5... | collective-permute-start | bytes 786440 | tf_op jit(solution)/shard_map/ppermute | solution.py:235
  85.4 6.5 %collective-permute-start.8 = (bf16[48,2048]{1,0:T(8,128)(2,1)S(1)}, bf16[48,2048]{1,0:T(8,128)(2,1)S(1)}, u32[]{:S(2)}, u32[]{:S(2)}) collective-permute-start(bf16[48,2048]{1,0:T(8,128)(2,1)S(1)} %slice.7), channel_id=1, source_target_pairs={{0,28},{4,0},{8,4},{12,8},{16,12},{20,16},{24,20},{28,24},{1,29},{... | collective-permute-start | bytes 589832 | tf_op jit(solution)/shard_map/ppermute | solution.py:235
  117.2 2.7 %collective-permute-start.9 = (bf16[4,64,896]{2,1,0:T(8,128)(2,1)S(1)}, bf16[4,64,896]{2,1,0:T(8,128)(2,1)S(1)}, u32[]{:S(2)}, u32[]{:S(2)}) collective-permute-start(bf16[4,64,896]{2,1,0:T(8,128)(2,1)S(1)} %dynamic-slice_bitcast_fusion), channel_id=1, source_target_pairs={{0,1},{1,0},{2,3},{3,2},{4,5},{5,4},{6,7},{7,6},{8,9},{9,8},{10,11... | collective-permute-start | bytes 1376264 | tf_op jit(solution)/shard_map/ppermute | solution.py:279
  120.1 14.2 %collective-permute-start.10 = (bf16[64,896]{1,0:T(8,128)(2,1)S(1)}, bf16[64,896]{1,0:T(8,128)(2,1)S(1)}, u32[]{:S(2)}, u32[]{:S(2)}) collective-permute-start(bf16[64,896]{1,0:T(8,128)(2,1)S(1)} %get-tuple-element.28), channel_id=1, source_target_pairs={{0,0},{1,128},{2,32},{3,160},{32,64},{33,192},{34,96},{35,224},{64... | collective-permute-start | bytes 344072 | tf_op jit(solution)/shard_map/ppermute | solution.py:293
  123.1 11.3 %collective-permute-start.11 = (bf16[64,896]{1,0:T(8,128)(2,1)S(1)}, bf16[64,896]{1,0:T(8,128)(2,1)S(1)}, u32[]{:S(2)}, u32[]{:S(2)}) collective-permute-start(bf16[64,896]{1,0:T(8,128)(2,1)S(1)} %get-tuple-element.27), channel_id=1, source_target_pairs={{0,32},{1,160},{2,64},{3,192},{32,96},{33,224},{34,0},{35,128},{64... | collective-permute-start | bytes 344072 | tf_op jit(solution)/shard_map/ppermute | solution.py:293
  126.9 7.5 %collective-permute-start.12 = (bf16[64,896]{1,0:T(8,128)(2,1)S(1)}, bf16[64,896]{1,0:T(8,128)(2,1)S(1)}, u32[]{:S(2)}, u32[]{:S(2)}) collective-permute-start(bf16[64,896]{1,0:T(8,128)(2,1)S(1)} %get-tuple-element.26), channel_id=1, source_target_pairs={{0,64},{1,192},{2,96},{3,224},{32,0},{33,128},{34,32},{35,160},{64... | collective-permute-start | bytes 344072 | tf_op jit(solution)/shard_map/ppermute | solution.py:293
  129.5 7.5 %collective-permute-start.13 = (bf16[64,896]{1,0:T(8,128)(2,1)S(1)}, bf16[64,896]{1,0:T(8,128)(2,1)S(1)}, u32[]{:S(2)}, u32[]{:S(2)}) collective-permute-start(bf16[64,896]{1,0:T(8,128)(2,1)S(1)} %get-tuple-element.25), channel_id=1, source_target_pairs={{0,96},{1,224},{2,0},{3,128},{32,32},{33,160},{34,64},{35,192},{64... | collective-permute-start | bytes 344072 | tf_op jit(solution)/shard_map/ppermute | solution.py:293

commit v5 on v4

--- a/solution.py
+++ b/solution.py
@@ -272,14 +272,15 @@
         rows, w_cols, (((1,), (1,)), ((), ())), preferred_element_type=jnp.float32
     ).astype(jnp.bfloat16)
     width = terms.shape[1]
-    terms = terms.reshape(2, 4, tokens, width)
-
-    kept = lax.dynamic_index_in_dim(terms, core, 0, keepdims=False)
-    sent = lax.dynamic_index_in_dim(terms, 1 - core, 0, keepdims=False)
+    terms = terms.reshape(2, 2, 2, tokens, width)
+
+    kept = lax.dynamic_index_in_dim(terms, core, 1, keepdims=False)
+    sent = lax.dynamic_index_in_dim(terms, 1 - core, 1, keepdims=False)
     got = lax.ppermute(sent, "c", [(0, 1), (1, 0)])
     both = (kept.astype(jnp.float32) + got.astype(jnp.float32)).astype(jnp.bfloat16)
-
-    slot = (place % 2) * 2 + ai("yl")
+    both = both.reshape(4, tokens, width)
+
+    slot = ai("yl") * 2 + ai("yh")
     left = jnp.zeros((tokens, width), jnp.float32)
     right = left
     for k in range(4):
@@ -287,11 +288,11 @@
         for r in range(8):
             for yl in range(2):
                 for c in range(2):
-                    i = ((r % 2) * 2 + yl + k) % 4
-                    pairs.append((r * 4 + yl * 2 + c, (c * 4 + i) * 4 + r // 2))
-        block = lax.dynamic_index_in_dim(both, (slot + k) % 4, 0, keepdims=False)
+                    i = (yl * 2 + r % 2) ^ k
+                    pairs.append((r * 4 + yl * 2 + c, (i // 2 * 4 + c * 2 + i % 2) * 4 + r // 2))
+        block = lax.dynamic_index_in_dim(both, slot ^ k, 0, keepdims=False)
         got = lax.ppermute(block, ("x", "yh", "yl", "c"), pairs).astype(jnp.float32)
-        first_half = (place - k) % 4 < 2
+        first_half = (ai("yh") ^ (k & 1)) == 0
         left = left + jnp.where(first_half, got, 0.0)
         right = right + jnp.where(first_half, 0.0, got)
     return jnp.concatenate([left, right], axis=1).astype(jnp.bfloat16)

time: 137 us -> 135 us (0.985); the launches traced: 138 us -> 134 us
  Pallas kernels: 15.3 us -> 10.4 us
  waiting for transfers between devices: 48.9 us -> 52.7 us
  starting transfers between devices: 42.9 us -> 40.7 us
    ppermute x4, starting transfers between devices: 14.1 us -> 7.65 us  [shards(): got = lax.ppermute(block, ('x', 'yh', 'yl', 'c'), pairs).astype(jnp.float32)]
    pallas_call x1, Pallas kernels: 13.7 us -> 8.82 us  [attention(): pl.pallas_call(attention_kernel, out_shape=pltpu.HBM((COPIES, tokens, hea...]
    all_to_all x1, starting transfers between devices: 3.61 us -> 7.56 us  [shards(): lax.all_to_all(head_out, row_axes, 0, 0)]
    ppermute x4, waiting for transfers between devices: 2.7 us -> 5.77 us  [shards(): got = lax.ppermute(block, ('x', 'yh', 'yl', 'c'), pairs).astype(jnp.float32)]
  transfers between devices with their start and end apart: 16 -> 16, of which waited for: 9 -> 12; matrix products, arithmetic and copies ran while one was open for 5% -> 5% of each run, Pallas kernels for 10% -> 7%
where the time goes in v5:
time: 135 us; the launch traced here: 134 us
  waiting for transfers between devices  52.7 us (39%)
  starting transfers between devices  40.7 us (30%)
  blocking collectives  17 us (13%)
  Pallas kernels  10.4 us (8%)
  local copies, waits for them, and re-layouts  6.94 us (5%)
  matrix products  4.4 us (3%)
  other arithmetic  2.11 us (2%)
    ppermute x8, waiting for transfers between devices, shift(): return lax.ppermute(v, 'z', [(i, (i + k) % 8) for i in range(8)])  18.7 us
    all_to_all x1, waiting for transfers between devices, shards(): lax.all_to_all(head_out, row_axes, 0, 0)  18 us
    all_to_all x1, blocking collectives, gather_rows(): lax.all_to_all(jnp.broadcast_to(v[None], (count,) + v.shape), axes, 0, 0)  17 us
    ppermute x8, starting transfers between devices, shift(): return lax.ppermute(v, 'z', [(i, (i + k) % 8) for i in range(8)])  11.2 us
    pallas_call x1, Pallas kernels, attention(): pl.pallas_call(attention_kernel, out_shape=pltpu.HBM((COPIES, tokens, hea...  8.82 us
    ppermute x4, starting transfers between devices, shards(): got = lax.ppermute(block, ('x', 'yh', 'yl', 'c'), pairs).astype(jnp.float32)  7.65 us
    all_to_all x1, waiting for transfers between devices, shards(): own = lax.all_to_all(pack(line, 16), ('x', 'yh', 'yl'), 0, 0)  7.63 us
    all_to_all x1, starting transfers between devices, shards(): lax.all_to_all(head_out, row_axes, 0, 0)  7.56 us
  transfers between devices with their start and end apart: 16, of which 12 were waited for; matrix products, arithmetic and copies ran while one was open for 5% of the time, Pallas kernels for 7%

profile of v5, /device:TPU:1, one launch (start us, length us, event | category | flops | bytes accessed | tf_op | source)
XLA Modules:
  0.0 134.4 jit_solution(15179473359952747647)
XLA Ops:
  0.0 0.0 copy-start
  0.0 0.9 copy-done
  0.9 17.0 %all_to_all.15.line_ref = bf16[8,16,576]{2,1,0:T(8,128)(2,1)S(1)} all-to-all(bf16[8,16,576]{2,1,0:T(8,128)(2,1)S(1)} %broadcast_in_dim.69), channel_id=1, replica_groups=mesh['x'=4,'yh'=2,'z'=8,'yl'=2,'c'=2] {'z'}, dimensions={0} | all-to-all | bytes 294912 | tf_op jit(solution)/shard_map/all_to_all | solution.py:224
  17.9 0.0 copy-start.2
  17.9 1.6 %shard_map.64 = bf16[16,576,128]{2,1,0:T(8,128)(2,1)} custom-call(bf16[8,16,576]{2,1,0:T(8,128)(2,1)S(1)} %all_to_all.15.line_ref), custom_call_target="tpu_custom_call" | custom-call | bytes 3000000 | tf_op jit(solution)/shard_map/pallas_call | solution.py:209
  19.5 6.8 %all-to-all-start.1 = ((bf16[16,576,128]{2,1,0:T(8,128)(2,1)}), bf16[16,576,128]{2,1,0:T(8,128)(2,1)S(1)}, u32[]{:S(2)}, u32[]{:S(2)}) async-start(bf16[16,576,128]{2,1,0:T(8,128)(2,1)} %shard_map.64), calls=%async_computation.1 | async-start | bytes 4718592 | tf_op jit(solution)/shard_map/all_to_all | solution.py:245
  26.3 0.0 copy-start.4
  26.3 0.0 copy-start.3
  26.3 0.0 copy-done.2
  26.4 0.7 collective-permute-start
  27.0 2.1 %collective-permute-start.2 = (bf16[112,2048]{1,0:T(8,128)(2,1)S(1)}, bf16[112,2048]{1,0:T(8,128)(2,1)S(1)}, u32[]{:S(2)}, u32[]{:S(2)}) collective-permute-start(bf16[112,2048]{1,0:T(8,128)(2,1)S(1)} %bitcast.45), channel_id=1, source_target_pairs={{0,28},{4,0},{8,4},{12,8},{16,12},{20,16},{24,20},{28,24},{1,29},{... | collective-permute-start | bytes 1376264 | tf_op jit(solution)/shard_map/ppermute | solution.py:235
  29.1 0.4 broadcast_in_dim.70
  29.6 7.2 %collective-permute-done = bf16[112,2048]{1,0:T(8,128)(2,1)S(1)} collective-permute-done((bf16[112,2048]{1,0:T(8,128)(2,1)S(1)}, bf16[112,2048]{1,0:T(8,128)(2,1)S(1)}, u32[]{:S(2)}, u32[]{:S(2)}) %collective-permute-start) | collective-permute-done | bytes 458784 | tf_op jit(solution)/shard_map/ppermute | solution.py:235
  36.8 0.0 collective-permute-start.1
  36.8 0.0 collective-permute-done.2
  36.8 2.7 %collective-permute-start.3 = (bf16[112,2048]{1,0:T(8,128)(2,1)S(1)}, bf16[112,2048]{1,0:T(8,128)(2,1)}, u32[]{:S(2)}, u32[]{:S(2)}) collective-permute-start(bf16[112,2048]{1,0:T(8,128)(2,1)S(1)} %collective-permute-done.2), channel_id=1, source_target_pairs={{0,28},{4,0},{8,4},{12,8},{16,12},{20,16},{24,20},{28,24},{1,29},{... | collective-permute-start | bytes 1376264 | tf_op jit(solution)/shard_map/ppermute | solution.py:235
  39.6 0.0 copy-start.1
  39.6 6.8 %collective-permute-done.1 = bf16[112,2048]{1,0:T(8,128)(2,1)} collective-permute-done((bf16[112,2048]{1,0:T(8,128)(2,1)S(1)}, bf16[112,2048]{1,0:T(8,128)(2,1)}, u32[]{:S(2)}, u32[]{:S(2)}) %collective-permute-start.1) | collective-permute-done | bytes 458784 | tf_op jit(solution)/shard_map/ppermute | solution.py:235
  46.3 0.0 copy-done.1
  46.4 0.0 collective-permute-done.3
  46.4 7.6 %all-to-all-done.1.own_ref = bf16[16,576,128]{2,1,0:T(8,128)(2,1)S(1)} async-done(((bf16[16,576,128]{2,1,0:T(8,128)(2,1)}), bf16[16,576,128]{2,1,0:T(8,128)(2,1)S(1)}, u32[]{:S(2)}, u32[]{:S(2)}) %all-to-all-start.1) | async-done | bytes 2359328 | tf_op jit(solution)/shard_map/all_to_all | solution.py:245
  54.0 6.0 %collective-permute-start.4 = (bf16[16,576,128]{2,1,0:T(8,128)(2,1)S(1)}, bf16[16,576,128]{2,1,0:T(8,128)(2,1)}, u32[]{:S(2)}, u32[]{:S(2)}) collective-permute-start(bf16[16,576,128]{2,1,0:T(8,128)(2,1)S(1)} %all-to-all-done.1.own_ref), channel_id=1, source_target_pairs={{0,1},{1,0},{2,3},{3,2},{4,5},{5,4},{6,7},{7,6},{8,9},{9,8},{10,11... | collective-permute-start | bytes 7077896 | tf_op jit(solution)/shard_map/ppermute | solution.py:252
  59.9 0.0 copy-done.4
  59.9 0.1 dynamic_slice.26
  60.0 0.1 pad_add_fusion.slot
  60.1 0.1 select_reduce_fusion.place
  60.2 0.0 copy-done.3
  60.2 0.1 convert_reduce_fusion.starts
  60.4 0.7 collective-permute-start.5
  61.0 2.1 %collective-permute-start.6 = (bf16[112,2048]{1,0:T(8,128)(2,1)}, bf16[112,2048]{1,0:T(8,128)(2,1)S(1)}, u32[]{:S(2)}, u32[]{:S(2)}) collective-permute-start(bf16[112,2048]{1,0:T(8,128)(2,1)} %collective-permute-done.3), channel_id=1, source_target_pairs={{0,28},{4,0},{8,4},{12,8},{16,12},{20,16},{24,20},{28,24},{1,29},{... | collective-permute-start | bytes 1376264 | tf_op jit(solution)/shard_map/ppermute | solution.py:235
  63.1 1.1 collective-permute-done.4.oth_ref
  64.2 8.8 %shard_map.65 = bf16[8,64,2048]{2,1,0:T(8,128)(2,1)} custom-call(s32[6]{0:T(128)S(1)} %convert_reduce_fusion.starts, s32[128]{0:T(128)S(1)} %select_reduce_fusion.place, s32[3]{0:T(128)S(1)} %pad_add_fusion.slot, bf16[64,16,576]{2,1,0:T(8,128)(2,1)} %q_hbm.1, bf16[16,512,128]{2,1,0:T(8,128)(2,1)} %w_hbm.1, bf16[16,576,128]{2,1,0:T(8,128)(2,1)S(1)} %all-to-all-done.1.own_ref, ...), custom_call_target="tpu_custom_call" | custom-call | flops 5000000000 | bytes 8000000 | tf_op jit(solution)/shard_map/pallas_call | solution.py:161
  73.1 0.9 collective-permute-done.5
  74.0 0.0 collective-permute-done.6
  74.0 7.6 %all-to-all-start.2 = ((bf16[8,64,2048]{2,1,0:T(8,128)(2,1)}), bf16[8,64,2048]{2,1,0:T(8,128)(2,1)S(1)}, u32[]{:S(2)}, u32[]{:S(2)}) async-start(bf16[8,64,2048]{2,1,0:T(8,128)(2,1)} %shard_map.65), calls=%async_computation.2 | async-start | bytes 4194304 | tf_op jit(solution)/shard_map/all_to_all | solution.py:267
  81.6 1.8 %bitcast_dynamic-update-slice_fusion.3 = bf16[8,112,2048]{2,1,0:T(8,128)(2,1)} fusion(bf16[8,112,2048]{2,1,0:T(8,128)(2,1)} %copy-done.1, s32[]{:T(128)S(6)} %select_n.179, bf16[112,2048]{1,0:T(8,128)(2,1)} %collective-permute-done.1), kind=kLoop, calls=%fused_computation.8 | loop fusion | bytes 917508 | tf_op jit(solution)/shard_map/jit(dynamic_update_index_in_dim)/dynamic_update_slice | solution.py:269
  83.4 1.8 %bitcast_dynamic-update-slice_fusion.2 = bf16[8,112,2048]{2,1,0:T(8,128)(2,1)} fusion(bf16[8,112,2048]{2,1,0:T(8,128)(2,1)} %bitcast_dynamic-update-slice_fusion.3, s32[]{:T(128)S(6)} %select_n.181, bf16[112,2048]{1,0:T(8,128)(2,1)} %collective-permute-done.3), kind=kLoop, calls=%fused_computation.7 | loop fusion | bytes 917508 | tf_op jit(solution)/shard_map/jit(dynamic_update_index_in_dim)/dynamic_update_slice | solution.py:269
  85.2 1.1 collective-permute-start.7
  86.3 2.0 %collective-permute-start.8 = (bf16[48,2048]{1,0:T(8,128)(2,1)S(1)}, bf16[48,2048]{1,0:T(8,128)(2,1)S(1)}, u32[]{:S(2)}, u32[]{:S(2)}) collective-permute-start(bf16[48,2048]{1,0:T(8,128)(2,1)S(1)} %slice.7), channel_id=1, source_target_pairs={{0,28},{4,0},{8,4},{12,8},{16,12},{20,16},{24,20},{28,24},{1,29},{... | collective-permute-start | bytes 589832 | tf_op jit(solution)/shard_map/ppermute | solution.py:235
  88.3 0.8 bitcast_dynamic-update-slice_fusion.1
  89.1 0.8 bitcast_dynamic-update-slice_fusion
  89.9 2.2 %collective-permute-done.8 = bf16[48,2048]{1,0:T(8,128)(2,1)S(1)} collective-permute-done((bf16[48,2048]{1,0:T(8,128)(2,1)S(1)}, bf16[48,2048]{1,0:T(8,128)(2,1)S(1)}, u32[]{:S(2)}, u32[]{:S(2)}) %collective-permute-start.8) | collective-permute-done | bytes 196640 | tf_op jit(solution)/shard_map/ppermute | solution.py:235
  92.0 1.7 %collective-permute-done.7 = bf16[64,2048]{1,0:T(8,128)(2,1)S(1)} collective-permute-done((bf16[64,2048]{1,0:T(8,128)(2,1)S(1)}, bf16[64,2048]{1,0:T(8,128)(2,1)S(1)}, u32[]{:S(2)}, u32[]{:S(2)}) %collective-permute-start.7) | collective-permute-done | bytes 262176 | tf_op jit(solution)/shard_map/ppermute | solution.py:235
  93.7 0.8 fusion.1
  94.5 18.0 %all-to-all-done.2 = bf16[8,64,2048]{2,1,0:T(8,128)(2,1)S(1)} async-done(((bf16[8,64,2048]{2,1,0:T(8,128)(2,1)}), bf16[8,64,2048]{2,1,0:T(8,128)(2,1)S(1)}, u32[]{:S(2)}, u32[]{:S(2)}) %all-to-all-start.2) | async-done | bytes 2097184 | tf_op jit(solution)/shard_map/all_to_all | solution.py:267
  112.5 4.4 %convolution_convert_fusion = bf16[512,896]{1,0:T(8,128)(2,1)S(1)} fusion(bf16[512,2048]{1,0:T(8,128)(2,1)S(1)} %bitcast.40, bf16[896,2048]{1,0:T(8,128)(2,1)} %bitcast.39), kind=kOutput, calls=%fused_computation | convolution fusion | flops 1879506944 | bytes 6684672 | tf_op jit(solution)/shard_map/dot_general | solution.py:271
  116.9 1.5 %collective-permute-start.9 = (bf16[2,2,64,896]{3,2,1,0:T(8,128)(2,1)S(1)}, bf16[2,2,64,896]{3,2,1,0:T(8,128)(2,1)S(1)}, u32[]{:S(2)}, u32[]{:S(2)}) collective-permute-start(bf16[2,2,64,896]{3,2,1,0:T(8,128)(2,1)S(1)} %dynamic-slice_bitcast_fusion), channel_id=1, source_target_pairs={{0,1},{1,0},{2,3},{3,2},{4,5},{5,4},{6,7},{7,6},{8,9},{9,8},{10,11... | collective-permute-start | bytes 1376264 | tf_op jit(solution)/shard_map/ppermute | solution.py:279
  118.5 1.4 %collective-permute-done.9 = bf16[2,2,64,896]{3,2,1,0:T(8,128)(2,1)S(1)} collective-permute-done((bf16[2,2,64,896]{3,2,1,0:T(8,128)(2,1)S(1)}, bf16[2,2,64,896]{3,2,1,0:T(8,128)(2,1)S(1)}, u32[]{:S(2)}, u32[]{:S(2)}) %collective-permute-start.9) | collective-permute-done | bytes 458784 | tf_op jit(solution)/shard_map/ppermute | solution.py:279
  119.9 0.1 fusion
  120.1 1.9 %collective-permute-start.10 = (bf16[64,896]{1,0:T(8,128)(2,1)S(1)}, bf16[64,896]{1,0:T(8,128)(2,1)S(1)}, u32[]{:S(2)}, u32[]{:S(2)}) collective-permute-start(bf16[64,896]{1,0:T(8,128)(2,1)S(1)} %get-tuple-element.28), channel_id=1, source_target_pairs={{0,0},{1,64},{2,128},{3,192},{32,32},{33,96},{34,160},{35,224},{64... | collective-permute-start | bytes 344072 | tf_op jit(solution)/shard_map/ppermute | solution.py:294
  122.0 3.2 %collective-permute-start.11 = (bf16[64,896]{1,0:T(8,128)(2,1)S(1)}, bf16[64,896]{1,0:T(8,128)(2,1)S(1)}, u32[]{:S(2)}, u32[]{:S(2)}) collective-permute-start(bf16[64,896]{1,0:T(8,128)(2,1)S(1)} %get-tuple-element.27), channel_id=1, source_target_pairs={{0,32},{1,96},{2,160},{3,224},{32,0},{33,64},{34,128},{35,192},{64... | collective-permute-start | bytes 344072 | tf_op jit(solution)/shard_map/ppermute | solution.py:294
  125.2 1.9 %collective-permute-start.12 = (bf16[64,896]{1,0:T(8,128)(2,1)S(1)}, bf16[64,896]{1,0:T(8,128)(2,1)S(1)}, u32[]{:S(2)}, u32[]{:S(2)}) collective-permute-start(bf16[64,896]{1,0:T(8,128)(2,1)S(1)} %get-tuple-element.26), channel_id=1, source_target_pairs={{0,128},{1,192},{2,0},{3,64},{32,160},{33,224},{34,32},{35,96},{64... | collective-permute-start | bytes 344072 | tf_op jit(solution)/shard_map/ppermute | solution.py:294
  127.1 0.7 collective-permute-start.13
  127.8 0.0 collective-permute-done.10
  127.8 1.7 %collective-permute-done.11 = bf16[64,896]{1,0:T(8,128)(2,1)S(1)} collective-permute-done((bf16[64,896]{1,0:T(8,128)(2,1)S(1)}, bf16[64,896]{1,0:T(8,128)(2,1)S(1)}, u32[]{:S(2)}, u32[]{:S(2)}) %collective-permute-start.11) | collective-permute-done | bytes 114720 | tf_op jit(solution)/shard_map/ppermute | solution.py:294
  129.4 1.8 %collective-permute-done.12 = bf16[64,896]{1,0:T(8,128)(2,1)S(1)} collective-permute-done((bf16[64,896]{1,0:T(8,128)(2,1)S(1)}, bf16[64,896]{1,0:T(8,128)(2,1)S(1)}, u32[]{:S(2)}, u32[]{:S(2)}) %collective-permute-start.12) | collective-permute-done | bytes 114720 | tf_op jit(solution)/shard_map/ppermute | solution.py:294
  131.3 2.2 %collective-permute-done.13 = bf16[64,896]{1,0:T(8,128)(2,1)S(1)} collective-permute-done((bf16[64,896]{1,0:T(8,128)(2,1)S(1)}, bf16[64,896]{1,0:T(8,128)(2,1)S(1)}, u32[]{:S(2)}, u32[]{:S(2)}) %collective-permute-start.13) | collective-permute-done | bytes 114720 | tf_op jit(solution)/shard_map/ppermute | solution.py:294
  133.5 0.1 fusion.5
  133.7 0.7 pad_maximum_fusion
  (10 shorter events, 0.3 us)
Async XLA Ops:
  0.0 0.9 copy-start
  17.9 8.5 %copy-start.2 = (bf16[2048,112]{0,1:T(8,128)(2,1)S(1)}, bf16[2048,112]{0,1:T(8,128)(2,1)}, u32[]{:S(2)}) copy-start(bf16[2048,112]{0,1:T(8,128)(2,1)} %param.11) | copy-start | bytes 1376260
  19.5 34.5 %all-to-all-start.1 = ((bf16[16,576,128]{2,1,0:T(8,128)(2,1)}), bf16[16,576,128]{2,1,0:T(8,128)(2,1)S(1)}, u32[]{:S(2)}, u32[]{:S(2)}) async-start(bf16[16,576,128]{2,1,0:T(8,128)(2,1)} %shard_map.64), calls=%async_computation.1 | async-start | bytes 4718592 | tf_op jit(solution)/shard_map/all_to_all | solution.py:245
  26.3 33.7 %copy-start.4 = (s32[128]{0:T(128)S(1)}, s32[128]{0:T(128)}, u32[]{:S(2)}) copy-start(s32[128]{0:T(128)} %param.9) | copy-start | bytes 1540
  26.3 33.9 %copy-start.3 = (s32[4096]{0:T(1024)S(1)}, s32[4096]{0:T(1024)}, u32[]{:S(2)}) copy-start(s32[4096]{0:T(1024)} %param.8) | copy-start | bytes 49156
  26.4 10.4 %collective-permute-start = (bf16[112,2048]{1,0:T(8,128)(2,1)S(1)}, bf16[112,2048]{1,0:T(8,128)(2,1)S(1)}, u32[]{:S(2)}, u32[]{:S(2)}) collective-permute-start(bf16[112,2048]{1,0:T(8,128)(2,1)S(1)} %bitcast.44), channel_id=1, source_target_pairs={{0,4},{4,8},{8,12},{12,16},{16,20},{20,24},{24,28},{28,0},{1,5},{5... | collective-permute-start | bytes 1376264 | tf_op jit(solution)/shard_map/ppermute | solution.py:235
  27.0 9.8 %collective-permute-start.2 = (bf16[112,2048]{1,0:T(8,128)(2,1)S(1)}, bf16[112,2048]{1,0:T(8,128)(2,1)S(1)}, u32[]{:S(2)}, u32[]{:S(2)}) collective-permute-start(bf16[112,2048]{1,0:T(8,128)(2,1)S(1)} %bitcast.45), channel_id=1, source_target_pairs={{0,28},{4,0},{8,4},{12,8},{16,12},{20,16},{24,20},{28,24},{1,29},{... | collective-permute-start | bytes 1376264 | tf_op jit(solution)/shard_map/ppermute | solution.py:235
  36.8 9.5 %collective-permute-start.1 = (bf16[112,2048]{1,0:T(8,128)(2,1)S(1)}, bf16[112,2048]{1,0:T(8,128)(2,1)}, u32[]{:S(2)}, u32[]{:S(2)}) collective-permute-start(bf16[112,2048]{1,0:T(8,128)(2,1)S(1)} %collective-permute-done), channel_id=1, source_target_pairs={{0,4},{4,8},{8,12},{12,16},{16,20},{20,24},{24,28},{28,0},{1,5},{5... | collective-permute-start | bytes 1376264 | tf_op jit(solution)/shard_map/ppermute | solution.py:235
  36.8 9.5 %collective-permute-start.3 = (bf16[112,2048]{1,0:T(8,128)(2,1)S(1)}, bf16[112,2048]{1,0:T(8,128)(2,1)}, u32[]{:S(2)}, u32[]{:S(2)}) collective-permute-start(bf16[112,2048]{1,0:T(8,128)(2,1)S(1)} %collective-permute-done.2), channel_id=1, source_target_pairs={{0,28},{4,0},{8,4},{12,8},{16,12},{20,16},{24,20},{28,24},{1,29},{... | collective-permute-start | bytes 1376264 | tf_op jit(solution)/shard_map/ppermute | solution.py:235
  39.6 6.8 %copy-start.1 = (bf16[8,112,2048]{2,1,0:T(8,128)(2,1)}, bf16[8,112,2048]{2,1,0:T(8,128)(2,1)S(1)}, u32[]{:S(2)}) copy-start(bf16[8,112,2048]{2,1,0:T(8,128)(2,1)S(1)} %bitcast_dynamic-update-slice_fusion.4) | copy-start | bytes 11010052
  54.0 10.3 %collective-permute-start.4 = (bf16[16,576,128]{2,1,0:T(8,128)(2,1)S(1)}, bf16[16,576,128]{2,1,0:T(8,128)(2,1)}, u32[]{:S(2)}, u32[]{:S(2)}) collective-permute-start(bf16[16,576,128]{2,1,0:T(8,128)(2,1)S(1)} %all-to-all-done.1.own_ref), channel_id=1, source_target_pairs={{0,1},{1,0},{2,3},{3,2},{4,5},{5,4},{6,7},{7,6},{8,9},{9,8},{10,11... | collective-permute-start | bytes 7077896 | tf_op jit(solution)/shard_map/ppermute | solution.py:252
  60.4 13.6 %collective-permute-start.5 = (bf16[112,2048]{1,0:T(8,128)(2,1)}, bf16[112,2048]{1,0:T(8,128)(2,1)S(1)}, u32[]{:S(2)}, u32[]{:S(2)}) collective-permute-start(bf16[112,2048]{1,0:T(8,128)(2,1)} %collective-permute-done.1), channel_id=1, source_target_pairs={{0,4},{4,8},{8,12},{12,16},{16,20},{20,24},{24,28},{28,0},{1,5},{5... | collective-permute-start | bytes 1376264 | tf_op jit(solution)/shard_map/ppermute | solution.py:235
  61.0 13.0 %collective-permute-start.6 = (bf16[112,2048]{1,0:T(8,128)(2,1)}, bf16[112,2048]{1,0:T(8,128)(2,1)S(1)}, u32[]{:S(2)}, u32[]{:S(2)}) collective-permute-start(bf16[112,2048]{1,0:T(8,128)(2,1)} %collective-permute-done.3), channel_id=1, source_target_pairs={{0,28},{4,0},{8,4},{12,8},{16,12},{20,16},{24,20},{28,24},{1,29},{... | collective-permute-start | bytes 1376264 | tf_op jit(solution)/shard_map/ppermute | solution.py:235
  74.0 38.5 %all-to-all-start.2 = ((bf16[8,64,2048]{2,1,0:T(8,128)(2,1)}), bf16[8,64,2048]{2,1,0:T(8,128)(2,1)S(1)}, u32[]{:S(2)}, u32[]{:S(2)}) async-start(bf16[8,64,2048]{2,1,0:T(8,128)(2,1)} %shard_map.65), calls=%async_computation.2 | async-start | bytes 4194304 | tf_op jit(solution)/shard_map/all_to_all | solution.py:267
  85.2 8.5 %collective-permute-start.7 = (bf16[64,2048]{1,0:T(8,128)(2,1)S(1)}, bf16[64,2048]{1,0:T(8,128)(2,1)S(1)}, u32[]{:S(2)}, u32[]{:S(2)}) collective-permute-start(bf16[64,2048]{1,0:T(8,128)(2,1)S(1)} %slice.6), channel_id=1, source_target_pairs={{0,4},{4,8},{8,12},{12,16},{16,20},{20,24},{24,28},{28,0},{1,5},{5... | collective-permute-start | bytes 786440 | tf_op jit(solution)/shard_map/ppermute | solution.py:235
  86.3 5.7 %collective-permute-start.8 = (bf16[48,2048]{1,0:T(8,128)(2,1)S(1)}, bf16[48,2048]{1,0:T(8,128)(2,1)S(1)}, u32[]{:S(2)}, u32[]{:S(2)}) collective-permute-start(bf16[48,2048]{1,0:T(8,128)(2,1)S(1)} %slice.7), channel_id=1, source_target_pairs={{0,28},{4,0},{8,4},{12,8},{16,12},{20,16},{24,20},{28,24},{1,29},{... | collective-permute-start | bytes 589832 | tf_op jit(solution)/shard_map/ppermute | solution.py:235
  116.9 3.0 %collective-permute-start.9 = (bf16[2,2,64,896]{3,2,1,0:T(8,128)(2,1)S(1)}, bf16[2,2,64,896]{3,2,1,0:T(8,128)(2,1)S(1)}, u32[]{:S(2)}, u32[]{:S(2)}) collective-permute-start(bf16[2,2,64,896]{3,2,1,0:T(8,128)(2,1)S(1)} %dynamic-slice_bitcast_fusion), channel_id=1, source_target_pairs={{0,1},{1,0},{2,3},{3,2},{4,5},{5,4},{6,7},{7,6},{8,9},{9,8},{10,11... | collective-permute-start | bytes 1376264 | tf_op jit(solution)/shard_map/ppermute | solution.py:279
  120.1 7.7 %collective-permute-start.10 = (bf16[64,896]{1,0:T(8,128)(2,1)S(1)}, bf16[64,896]{1,0:T(8,128)(2,1)S(1)}, u32[]{:S(2)}, u32[]{:S(2)}) collective-permute-start(bf16[64,896]{1,0:T(8,128)(2,1)S(1)} %get-tuple-element.28), channel_id=1, source_target_pairs={{0,0},{1,64},{2,128},{3,192},{32,32},{33,96},{34,160},{35,224},{64... | collective-permute-start | bytes 344072 | tf_op jit(solution)/shard_map/ppermute | solution.py:294
  122.0 7.4 %collective-permute-start.11 = (bf16[64,896]{1,0:T(8,128)(2,1)S(1)}, bf16[64,896]{1,0:T(8,128)(2,1)S(1)}, u32[]{:S(2)}, u32[]{:S(2)}) collective-permute-start(bf16[64,896]{1,0:T(8,128)(2,1)S(1)} %get-tuple-element.27), channel_id=1, source_target_pairs={{0,32},{1,96},{2,160},{3,224},{32,0},{33,64},{34,128},{35,192},{64... | collective-permute-start | bytes 344072 | tf_op jit(solution)/shard_map/ppermute | solution.py:294
  125.2 6.1 %collective-permute-start.12 = (bf16[64,896]{1,0:T(8,128)(2,1)S(1)}, bf16[64,896]{1,0:T(8,128)(2,1)S(1)}, u32[]{:S(2)}, u32[]{:S(2)}) collective-permute-start(bf16[64,896]{1,0:T(8,128)(2,1)S(1)} %get-tuple-element.26), channel_id=1, source_target_pairs={{0,128},{1,192},{2,0},{3,64},{32,160},{33,224},{34,32},{35,96},{64... | collective-permute-start | bytes 344072 | tf_op jit(solution)/shard_map/ppermute | solution.py:294
  127.1 6.4 %collective-permute-start.13 = (bf16[64,896]{1,0:T(8,128)(2,1)S(1)}, bf16[64,896]{1,0:T(8,128)(2,1)S(1)}, u32[]{:S(2)}, u32[]{:S(2)}) collective-permute-start(bf16[64,896]{1,0:T(8,128)(2,1)S(1)} %get-tuple-element.25), channel_id=1, source_target_pairs={{0,160},{1,224},{2,32},{3,96},{32,128},{33,192},{34,0},{35,64},{64... | collective-permute-start | bytes 344072 | tf_op jit(solution)/shard_map/ppermute | solution.py:294

commit v6 on v5

--- a/solution.py
+++ b/solution.py
@@ -45,9 +45,10 @@
             lo = jnp.maximum(lo, jnp.where(starts[d] <= pos, starts[d], 0))
         return lo
 
-    lane = lax.broadcasted_iota(jnp.int32, (1, KEYS), 1)
-    key_half = jnp.where(lane < KEYS // 2, core, 1 - core)
-    key_place = ((lane & (KEYS // 2 - 1)) >> 4) * SPAN + key_half * HALF + (lane & (HALF - 1))
+    def key_places(keys):
+        lane = lax.broadcasted_iota(jnp.int32, (1, keys), 1)
+        key_half = jnp.where(lane < keys // 2, core, 1 - core)
+        return ((lane & (keys // 2 - 1)) >> 4) * SPAN + key_half * HALF + (lane & (HALF - 1))
 
     for t in range(2):
         last = slot[t]
@@ -55,7 +56,10 @@
         for d in range(DOCS):
             lo = jnp.maximum(lo, jnp.where(starts[d] <= last * SPAN, starts[d], 0))
         first = lo // SPAN
-        blocks = (last - first + GROUP) // GROUP
+        spans = last - first + 1
+        left = spans & (GROUP - 1)
+        blocks = (spans + GROUP // 2 - 1) // GROUP
+        tail = (left > 0) & (left <= GROUP // 2)
         row_token = lax.broadcasted_iota(jnp.int32, (rows, 1), 0) // heads
         q_pos = last * SPAN + row_token
         q_lo = doc_start(q_pos) - first * SPAN
@@ -68,13 +72,14 @@
         sum_buf[...] = jnp.zeros(sum_buf.shape, jnp.float32)
         acc[...] = jnp.zeros(acc.shape, jnp.float32)
 
-        def score(b, carry):
-            for g in range(GROUP):
+        def score(b, group):
+            keys = group * SPAN
+            for g in range(group):
                 code = place[jnp.minimum(first + b * GROUP + g, span_total - 1)]
                 block = lax.shift_right_logical(code, 3)
                 z = code & 7
                 for i, ref in enumerate((own_ref, oth_ref)):
-                    row = i * KEYS // 2 + g * HALF
+                    row = i * keys // 2 + g * HALF
                     for j in range(value_cols // 128):
                         src = pl.multiple_of(j * line_rows + z * HALF, HALF)
                         k_buf[b, row : row + HALF, j * 128 : (j + 1) * 128] = ref[
@@ -86,32 +91,42 @@
                         low_lanes == (z < 4), rope, jnp.zeros_like(rope)
                     )
             s = lax.dot_general(
-                q, k_buf[b], (((1,), (1,)), ((), ())), preferred_element_type=jnp.float32
+                q, k_buf[b, :keys], (((1,), (1,)), ((), ())), preferred_element_type=jnp.float32
             )
-            k_pos = b * KEYS + key_place
+            k_pos = b * KEYS + key_places(keys)
             s = jnp.where((k_pos >= q_lo) & (k_pos <= q_hi), s, NEG)
-            s_buf[b] = s
+            s_buf[b, :, :keys] = s
             top = top_buf[...]
-            for j in range(KEYS // 128):
+            for j in range(keys // 128):
                 top = jnp.maximum(top, s[:, j * 128 : (j + 1) * 128])
             top_buf[...] = top
-            return carry
-
-        lax.fori_loop(0, blocks, score, 0)
+
+        def each(step):
+            def whole(b, carry):
+                step(b, GROUP)
+                return carry
+
+            lax.fori_loop(0, blocks, whole, 0)
+
+            @pl.when(tail)
+            def _():
+                step(blocks, GROUP // 2)
+
+        each(score)
         top = jnp.max(top_buf[...], axis=1, keepdims=True)
 
-        def mix(b, carry):
-            w = jnp.exp2((s_buf[b] - top) * scale)
+        def mix(b, group):
+            keys = group * SPAN
+            w = jnp.exp2((s_buf[b, :, :keys] - top) * scale)
             part = sum_buf[...]
-            for j in range(KEYS // 128):
+            for j in range(keys // 128):
                 part = part + w[:, j * 128 : (j + 1) * 128]
             sum_buf[...] = part
             acc[...] += jnp.dot(
-                w.astype(jnp.bfloat16), k_buf[b, :, :value_cols], preferred_element_type=jnp.float32
+                w.astype(jnp.bfloat16), k_buf[b, :keys, :value_cols], preferred_element_type=jnp.float32
             )
-            return carry
-
-        lax.fori_loop(0, blocks, mix, 0)
+
+        each(mix)
         total = jnp.sum(sum_buf[...], axis=1, keepdims=True)
         scaled = acc[...] * (1.0 / total)
         for j in range(value_cols // 128):

time: 135 us -> 135 us (level)
  starting transfers between devices: 40.7 us -> 38.5 us
    all_to_all x1, starting transfers between devices: 7.56 us -> 5.86 us  [shards(): lax.all_to_all(head_out, row_axes, 0, 0)]
  transfers between devices with their start and end apart: 16 -> 16, of which waited for: 12 -> 11; matrix products, arithmetic and copies ran while one was open for 5% -> 5% of each run, Pallas kernels for 7% -> 8%
where the time goes in v6:
time: 135 us; the launch traced here: 133 us
  waiting for transfers between devices  52.2 us (39%)
  starting transfers between devices  38.5 us (29%)
  blocking collectives  17 us (13%)
  Pallas kernels  11.7 us (9%)
  local copies, waits for them, and re-layouts  6.94 us (5%)
  matrix products  4.4 us (3%)
  other arithmetic  2.11 us (2%)
    ppermute x8, waiting for transfers between devices, shift(): return lax.ppermute(v, 'z', [(i, (i + k) % 8) for i in range(8)])  18 us
    all_to_all x1, waiting for transfers between devices, shards(): lax.all_to_all(head_out, row_axes, 0, 0)  18 us
    all_to_all x1, blocking collectives, gather_rows(): lax.all_to_all(jnp.broadcast_to(v[None], (count,) + v.shape), axes, 0, 0)  17 us
    ppermute x8, starting transfers between devices, shift(): return lax.ppermute(v, 'z', [(i, (i + k) % 8) for i in range(8)])  11 us
    pallas_call x1, Pallas kernels, attention(): pl.pallas_call(attention_kernel, out_shape=pltpu.HBM((COPIES, tokens, hea...  10.1 us
    all_to_all x1, waiting for transfers between devices, shards(): own = lax.all_to_all(pack(line, 16), ('x', 'yh', 'yl'), 0, 0)  7.63 us
    ppermute x4, starting transfers between devices, shards(): got = lax.ppermute(block, ('x', 'yh', 'yl', 'c'), pairs).astype(jnp.float32)  7.38 us
    all_to_all x1, starting transfers between devices, shards(): own = lax.all_to_all(pack(line, 16), ('x', 'yh', 'yl'), 0, 0)  6.77 us
  transfers between devices with their start and end apart: 16, of which 11 were waited for; matrix products, arithmetic and copies ran while one was open for 5% of the time, Pallas kernels for 8%

profile of v6, /device:TPU:1, one launch (start us, length us, event | category | flops | bytes accessed | tf_op | source)
XLA Modules:
  0.0 133.1 jit_solution(17878822854887910945)
XLA Ops:
  0.0 0.0 copy-start
  0.0 0.9 copy-done
  0.9 17.0 %all_to_all.15.line_ref = bf16[8,16,576]{2,1,0:T(8,128)(2,1)S(1)} all-to-all(bf16[8,16,576]{2,1,0:T(8,128)(2,1)S(1)} %broadcast_in_dim.69), channel_id=1, replica_groups=mesh['x'=4,'yh'=2,'z'=8,'yl'=2,'c'=2] {'z'}, dimensions={0} | all-to-all | bytes 294912 | tf_op jit(solution)/shard_map/all_to_all | solution.py:239
  17.9 0.0 copy-start.2
  17.9 1.6 %shard_map.64 = bf16[16,576,128]{2,1,0:T(8,128)(2,1)} custom-call(bf16[8,16,576]{2,1,0:T(8,128)(2,1)S(1)} %all_to_all.15.line_ref), custom_call_target="tpu_custom_call" | custom-call | bytes 3000000 | tf_op jit(solution)/shard_map/pallas_call | solution.py:224
  19.5 6.8 %all-to-all-start.1 = ((bf16[16,576,128]{2,1,0:T(8,128)(2,1)}), bf16[16,576,128]{2,1,0:T(8,128)(2,1)S(1)}, u32[]{:S(2)}, u32[]{:S(2)}) async-start(bf16[16,576,128]{2,1,0:T(8,128)(2,1)} %shard_map.64), calls=%async_computation.1 | async-start | bytes 4718592 | tf_op jit(solution)/shard_map/all_to_all | solution.py:260
  26.3 0.0 copy-start.4
  26.3 0.0 copy-start.3
  26.3 0.0 copy-done.2
  26.4 0.7 collective-permute-start
  27.0 2.1 %collective-permute-start.2 = (bf16[112,2048]{1,0:T(8,128)(2,1)S(1)}, bf16[112,2048]{1,0:T(8,128)(2,1)S(1)}, u32[]{:S(2)}, u32[]{:S(2)}) collective-permute-start(bf16[112,2048]{1,0:T(8,128)(2,1)S(1)} %bitcast.45), channel_id=1, source_target_pairs={{0,28},{4,0},{8,4},{12,8},{16,12},{20,16},{24,20},{28,24},{1,29},{... | collective-permute-start | bytes 1376264 | tf_op jit(solution)/shard_map/ppermute | solution.py:250
  29.1 0.4 broadcast_in_dim.70
  29.6 7.2 %collective-permute-done = bf16[112,2048]{1,0:T(8,128)(2,1)S(1)} collective-permute-done((bf16[112,2048]{1,0:T(8,128)(2,1)S(1)}, bf16[112,2048]{1,0:T(8,128)(2,1)S(1)}, u32[]{:S(2)}, u32[]{:S(2)}) %collective-permute-start) | collective-permute-done | bytes 458784 | tf_op jit(solution)/shard_map/ppermute | solution.py:250
  36.8 0.0 collective-permute-start.1
  36.8 0.0 collective-permute-done.2
  36.8 2.7 %collective-permute-start.3 = (bf16[112,2048]{1,0:T(8,128)(2,1)S(1)}, bf16[112,2048]{1,0:T(8,128)(2,1)}, u32[]{:S(2)}, u32[]{:S(2)}) collective-permute-start(bf16[112,2048]{1,0:T(8,128)(2,1)S(1)} %collective-permute-done.2), channel_id=1, source_target_pairs={{0,28},{4,0},{8,4},{12,8},{16,12},{20,16},{24,20},{28,24},{1,29},{... | collective-permute-start | bytes 1376264 | tf_op jit(solution)/shard_map/ppermute | solution.py:250
  39.6 0.0 copy-start.1
  39.6 6.8 %collective-permute-done.1 = bf16[112,2048]{1,0:T(8,128)(2,1)} collective-permute-done((bf16[112,2048]{1,0:T(8,128)(2,1)S(1)}, bf16[112,2048]{1,0:T(8,128)(2,1)}, u32[]{:S(2)}, u32[]{:S(2)}) %collective-permute-start.1) | collective-permute-done | bytes 458784 | tf_op jit(solution)/shard_map/ppermute | solution.py:250
  46.3 0.0 copy-done.1
  46.4 0.0 collective-permute-done.3
  46.4 7.6 %all-to-all-done.1.own_ref = bf16[16,576,128]{2,1,0:T(8,128)(2,1)S(1)} async-done(((bf16[16,576,128]{2,1,0:T(8,128)(2,1)}), bf16[16,576,128]{2,1,0:T(8,128)(2,1)S(1)}, u32[]{:S(2)}, u32[]{:S(2)}) %all-to-all-start.1) | async-done | bytes 2359328 | tf_op jit(solution)/shard_map/all_to_all | solution.py:260
  54.0 6.0 %collective-permute-start.4 = (bf16[16,576,128]{2,1,0:T(8,128)(2,1)S(1)}, bf16[16,576,128]{2,1,0:T(8,128)(2,1)}, u32[]{:S(2)}, u32[]{:S(2)}) collective-permute-start(bf16[16,576,128]{2,1,0:T(8,128)(2,1)S(1)} %all-to-all-done.1.own_ref), channel_id=1, source_target_pairs={{0,1},{1,0},{2,3},{3,2},{4,5},{5,4},{6,7},{7,6},{8,9},{9,8},{10,11... | collective-permute-start | bytes 7077896 | tf_op jit(solution)/shard_map/ppermute | solution.py:267
  59.9 0.0 copy-done.4
  59.9 0.1 dynamic_slice.26
  60.0 0.1 pad_add_fusion.slot
  60.1 0.1 select_reduce_fusion.place
  60.2 0.0 copy-done.3
  60.2 0.1 convert_reduce_fusion.starts
  60.4 0.7 collective-permute-start.5
  61.0 2.1 %collective-permute-start.6 = (bf16[112,2048]{1,0:T(8,128)(2,1)}, bf16[112,2048]{1,0:T(8,128)(2,1)S(1)}, u32[]{:S(2)}, u32[]{:S(2)}) collective-permute-start(bf16[112,2048]{1,0:T(8,128)(2,1)} %collective-permute-done.3), channel_id=1, source_target_pairs={{0,28},{4,0},{8,4},{12,8},{16,12},{20,16},{24,20},{28,24},{1,29},{... | collective-permute-start | bytes 1376264 | tf_op jit(solution)/shard_map/ppermute | solution.py:250
  63.1 1.1 collective-permute-done.4.oth_ref
  64.2 10.1 %shard_map.65 = bf16[8,64,2048]{2,1,0:T(8,128)(2,1)} custom-call(s32[6]{0:T(128)S(1)} %convert_reduce_fusion.starts, s32[128]{0:T(128)S(1)} %select_reduce_fusion.place, s32[3]{0:T(128)S(1)} %pad_add_fusion.slot, bf16[64,16,576]{2,1,0:T(8,128)(2,1)} %q_hbm.1, bf16[16,512,128]{2,1,0:T(8,128)(2,1)} %w_hbm.1, bf16[16,576,128]{2,1,0:T(8,128)(2,1)S(1)} %all-to-all-done.1.own_ref, ...), custom_call_target="tpu_custom_call" | custom-call | flops 5000000000 | bytes 8000000 | tf_op jit(solution)/shard_map/pallas_call | solution.py:176
  74.3 0.0 collective-permute-done.5
  74.3 0.0 collective-permute-done.6
  74.4 5.9 %all-to-all-start.2 = ((bf16[8,64,2048]{2,1,0:T(8,128)(2,1)}), bf16[8,64,2048]{2,1,0:T(8,128)(2,1)S(1)}, u32[]{:S(2)}, u32[]{:S(2)}) async-start(bf16[8,64,2048]{2,1,0:T(8,128)(2,1)} %shard_map.65), calls=%async_computation.2 | async-start | bytes 4194304 | tf_op jit(solution)/shard_map/all_to_all | solution.py:282
  80.2 1.8 %bitcast_dynamic-update-slice_fusion.3 = bf16[8,112,2048]{2,1,0:T(8,128)(2,1)} fusion(bf16[8,112,2048]{2,1,0:T(8,128)(2,1)} %copy-done.1, s32[]{:T(128)S(6)} %select_n.179, bf16[112,2048]{1,0:T(8,128)(2,1)} %collective-permute-done.1), kind=kLoop, calls=%fused_computation.8 | loop fusion | bytes 917508 | tf_op jit(solution)/shard_map/jit(dynamic_update_index_in_dim)/dynamic_update_slice | solution.py:284
  82.0 1.8 %bitcast_dynamic-update-slice_fusion.2 = bf16[8,112,2048]{2,1,0:T(8,128)(2,1)} fusion(bf16[8,112,2048]{2,1,0:T(8,128)(2,1)} %bitcast_dynamic-update-slice_fusion.3, s32[]{:T(128)S(6)} %select_n.181, bf16[112,2048]{1,0:T(8,128)(2,1)} %collective-permute-done.3), kind=kLoop, calls=%fused_computation.7 | loop fusion | bytes 917508 | tf_op jit(solution)/shard_map/jit(dynamic_update_index_in_dim)/dynamic_update_slice | solution.py:284
  83.9 1.1 collective-permute-start.7
  85.0 1.8 %collective-permute-start.8 = (bf16[48,2048]{1,0:T(8,128)(2,1)S(1)}, bf16[48,2048]{1,0:T(8,128)(2,1)S(1)}, u32[]{:S(2)}, u32[]{:S(2)}) collective-permute-start(bf16[48,2048]{1,0:T(8,128)(2,1)S(1)} %slice.7), channel_id=1, source_target_pairs={{0,28},{4,0},{8,4},{12,8},{16,12},{20,16},{24,20},{28,24},{1,29},{... | collective-permute-start | bytes 589832 | tf_op jit(solution)/shard_map/ppermute | solution.py:250
  86.7 0.8 bitcast_dynamic-update-slice_fusion.1
  87.5 0.8 bitcast_dynamic-update-slice_fusion
  88.3 2.2 %collective-permute-done.8 = bf16[48,2048]{1,0:T(8,128)(2,1)S(1)} collective-permute-done((bf16[48,2048]{1,0:T(8,128)(2,1)S(1)}, bf16[48,2048]{1,0:T(8,128)(2,1)S(1)}, u32[]{:S(2)}, u32[]{:S(2)}) %collective-permute-start.8) | collective-permute-done | bytes 196640 | tf_op jit(solution)/shard_map/ppermute | solution.py:250
  90.5 1.9 %collective-permute-done.7 = bf16[64,2048]{1,0:T(8,128)(2,1)S(1)} collective-permute-done((bf16[64,2048]{1,0:T(8,128)(2,1)S(1)}, bf16[64,2048]{1,0:T(8,128)(2,1)S(1)}, u32[]{:S(2)}, u32[]{:S(2)}) %collective-permute-start.7) | collective-permute-done | bytes 262176 | tf_op jit(solution)/shard_map/ppermute | solution.py:250
  92.4 0.8 fusion.1
  93.2 18.0 %all-to-all-done.2 = bf16[8,64,2048]{2,1,0:T(8,128)(2,1)S(1)} async-done(((bf16[8,64,2048]{2,1,0:T(8,128)(2,1)}), bf16[8,64,2048]{2,1,0:T(8,128)(2,1)S(1)}, u32[]{:S(2)}, u32[]{:S(2)}) %all-to-all-start.2) | async-done | bytes 2097184 | tf_op jit(solution)/shard_map/all_to_all | solution.py:282
  111.1 4.4 %convolution_convert_fusion = bf16[512,896]{1,0:T(8,128)(2,1)S(1)} fusion(bf16[512,2048]{1,0:T(8,128)(2,1)S(1)} %bitcast.40, bf16[896,2048]{1,0:T(8,128)(2,1)} %bitcast.39), kind=kOutput, calls=%fused_computation | convolution fusion | flops 1879506944 | bytes 6684672 | tf_op jit(solution)/shard_map/dot_general | solution.py:286
  115.6 1.5 %collective-permute-start.9 = (bf16[2,2,64,896]{3,2,1,0:T(8,128)(2,1)S(1)}, bf16[2,2,64,896]{3,2,1,0:T(8,128)(2,1)S(1)}, u32[]{:S(2)}, u32[]{:S(2)}) collective-permute-start(bf16[2,2,64,896]{3,2,1,0:T(8,128)(2,1)S(1)} %dynamic-slice_bitcast_fusion), channel_id=1, source_target_pairs={{0,1},{1,0},{2,3},{3,2},{4,5},{5,4},{6,7},{7,6},{8,9},{9,8},{10,11... | collective-permute-start | bytes 1376264 | tf_op jit(solution)/shard_map/ppermute | solution.py:294
  117.1 1.4 %collective-permute-done.9 = bf16[2,2,64,896]{3,2,1,0:T(8,128)(2,1)S(1)} collective-permute-done((bf16[2,2,64,896]{3,2,1,0:T(8,128)(2,1)S(1)}, bf16[2,2,64,896]{3,2,1,0:T(8,128)(2,1)S(1)}, u32[]{:S(2)}, u32[]{:S(2)}) %collective-permute-start.9) | collective-permute-done | bytes 458784 | tf_op jit(solution)/shard_map/ppermute | solution.py:294
  118.6 0.1 fusion
  118.8 1.9 %collective-permute-start.10 = (bf16[64,896]{1,0:T(8,128)(2,1)S(1)}, bf16[64,896]{1,0:T(8,128)(2,1)S(1)}, u32[]{:S(2)}, u32[]{:S(2)}) collective-permute-start(bf16[64,896]{1,0:T(8,128)(2,1)S(1)} %get-tuple-element.28), channel_id=1, source_target_pairs={{0,0},{1,64},{2,128},{3,192},{32,32},{33,96},{34,160},{35,224},{64... | collective-permute-start | bytes 344072 | tf_op jit(solution)/shard_map/ppermute | solution.py:309
  120.7 3.2 %collective-permute-start.11 = (bf16[64,896]{1,0:T(8,128)(2,1)S(1)}, bf16[64,896]{1,0:T(8,128)(2,1)S(1)}, u32[]{:S(2)}, u32[]{:S(2)}) collective-permute-start(bf16[64,896]{1,0:T(8,128)(2,1)S(1)} %get-tuple-element.27), channel_id=1, source_target_pairs={{0,32},{1,96},{2,160},{3,224},{32,0},{33,64},{34,128},{35,192},{64... | collective-permute-start | bytes 344072 | tf_op jit(solution)/shard_map/ppermute | solution.py:309
  123.9 1.9 %collective-permute-start.12 = (bf16[64,896]{1,0:T(8,128)(2,1)S(1)}, bf16[64,896]{1,0:T(8,128)(2,1)S(1)}, u32[]{:S(2)}, u32[]{:S(2)}) collective-permute-start(bf16[64,896]{1,0:T(8,128)(2,1)S(1)} %get-tuple-element.26), channel_id=1, source_target_pairs={{0,128},{1,192},{2,0},{3,64},{32,160},{33,224},{34,32},{35,96},{64... | collective-permute-start | bytes 344072 | tf_op jit(solution)/shard_map/ppermute | solution.py:309
  125.8 0.3 collective-permute-start.13
  126.1 0.0 collective-permute-done.10
  126.2 2.4 %collective-permute-done.11 = bf16[64,896]{1,0:T(8,128)(2,1)S(1)} collective-permute-done((bf16[64,896]{1,0:T(8,128)(2,1)S(1)}, bf16[64,896]{1,0:T(8,128)(2,1)S(1)}, u32[]{:S(2)}, u32[]{:S(2)}) %collective-permute-start.11) | collective-permute-done | bytes 114720 | tf_op jit(solution)/shard_map/ppermute | solution.py:309
  128.5 1.5 %collective-permute-done.12 = bf16[64,896]{1,0:T(8,128)(2,1)S(1)} collective-permute-done((bf16[64,896]{1,0:T(8,128)(2,1)S(1)}, bf16[64,896]{1,0:T(8,128)(2,1)S(1)}, u32[]{:S(2)}, u32[]{:S(2)}) %collective-permute-start.12) | collective-permute-done | bytes 114720 | tf_op jit(solution)/shard_map/ppermute | solution.py:309
  130.0 2.2 %collective-permute-done.13 = bf16[64,896]{1,0:T(8,128)(2,1)S(1)} collective-permute-done((bf16[64,896]{1,0:T(8,128)(2,1)S(1)}, bf16[64,896]{1,0:T(8,128)(2,1)S(1)}, u32[]{:S(2)}, u32[]{:S(2)}) %collective-permute-start.13) | collective-permute-done | bytes 114720 | tf_op jit(solution)/shard_map/ppermute | solution.py:309
  132.2 0.1 fusion.5
  132.4 0.7 pad_maximum_fusion
  (10 shorter events, 0.3 us)
Async XLA Ops:
  0.0 0.9 copy-start
  17.9 8.5 %copy-start.2 = (bf16[2048,112]{0,1:T(8,128)(2,1)S(1)}, bf16[2048,112]{0,1:T(8,128)(2,1)}, u32[]{:S(2)}) copy-start(bf16[2048,112]{0,1:T(8,128)(2,1)} %param.11) | copy-start | bytes 1376260
  19.5 34.5 %all-to-all-start.1 = ((bf16[16,576,128]{2,1,0:T(8,128)(2,1)}), bf16[16,576,128]{2,1,0:T(8,128)(2,1)S(1)}, u32[]{:S(2)}, u32[]{:S(2)}) async-start(bf16[16,576,128]{2,1,0:T(8,128)(2,1)} %shard_map.64), calls=%async_computation.1 | async-start | bytes 4718592 | tf_op jit(solution)/shard_map/all_to_all | solution.py:260
  26.3 33.7 %copy-start.4 = (s32[128]{0:T(128)S(1)}, s32[128]{0:T(128)}, u32[]{:S(2)}) copy-start(s32[128]{0:T(128)} %param.9) | copy-start | bytes 1540
  26.3 33.9 %copy-start.3 = (s32[4096]{0:T(1024)S(1)}, s32[4096]{0:T(1024)}, u32[]{:S(2)}) copy-start(s32[4096]{0:T(1024)} %param.8) | copy-start | bytes 49156
  26.4 10.4 %collective-permute-start = (bf16[112,2048]{1,0:T(8,128)(2,1)S(1)}, bf16[112,2048]{1,0:T(8,128)(2,1)S(1)}, u32[]{:S(2)}, u32[]{:S(2)}) collective-permute-start(bf16[112,2048]{1,0:T(8,128)(2,1)S(1)} %bitcast.44), channel_id=1, source_target_pairs={{0,4},{4,8},{8,12},{12,16},{16,20},{20,24},{24,28},{28,0},{1,5},{5... | collective-permute-start | bytes 1376264 | tf_op jit(solution)/shard_map/ppermute | solution.py:250
  27.0 9.8 %collective-permute-start.2 = (bf16[112,2048]{1,0:T(8,128)(2,1)S(1)}, bf16[112,2048]{1,0:T(8,128)(2,1)S(1)}, u32[]{:S(2)}, u32[]{:S(2)}) collective-permute-start(bf16[112,2048]{1,0:T(8,128)(2,1)S(1)} %bitcast.45), channel_id=1, source_target_pairs={{0,28},{4,0},{8,4},{12,8},{16,12},{20,16},{24,20},{28,24},{1,29},{... | collective-permute-start | bytes 1376264 | tf_op jit(solution)/shard_map/ppermute | solution.py:250
  36.8 9.5 %collective-permute-start.1 = (bf16[112,2048]{1,0:T(8,128)(2,1)S(1)}, bf16[112,2048]{1,0:T(8,128)(2,1)}, u32[]{:S(2)}, u32[]{:S(2)}) collective-permute-start(bf16[112,2048]{1,0:T(8,128)(2,1)S(1)} %collective-permute-done), channel_id=1, source_target_pairs={{0,4},{4,8},{8,12},{12,16},{16,20},{20,24},{24,28},{28,0},{1,5},{5... | collective-permute-start | bytes 1376264 | tf_op jit(solution)/shard_map/ppermute | solution.py:250
  36.8 9.5 %collective-permute-start.3 = (bf16[112,2048]{1,0:T(8,128)(2,1)S(1)}, bf16[112,2048]{1,0:T(8,128)(2,1)}, u32[]{:S(2)}, u32[]{:S(2)}) collective-permute-start(bf16[112,2048]{1,0:T(8,128)(2,1)S(1)} %collective-permute-done.2), channel_id=1, source_target_pairs={{0,28},{4,0},{8,4},{12,8},{16,12},{20,16},{24,20},{28,24},{1,29},{... | collective-permute-start | bytes 1376264 | tf_op jit(solution)/shard_map/ppermute | solution.py:250
  39.6 6.8 %copy-start.1 = (bf16[8,112,2048]{2,1,0:T(8,128)(2,1)}, bf16[8,112,2048]{2,1,0:T(8,128)(2,1)S(1)}, u32[]{:S(2)}) copy-start(bf16[8,112,2048]{2,1,0:T(8,128)(2,1)S(1)} %bitcast_dynamic-update-slice_fusion.4) | copy-start | bytes 11010052
  54.0 10.3 %collective-permute-start.4 = (bf16[16,576,128]{2,1,0:T(8,128)(2,1)S(1)}, bf16[16,576,128]{2,1,0:T(8,128)(2,1)}, u32[]{:S(2)}, u32[]{:S(2)}) collective-permute-start(bf16[16,576,128]{2,1,0:T(8,128)(2,1)S(1)} %all-to-all-done.1.own_ref), channel_id=1, source_target_pairs={{0,1},{1,0},{2,3},{3,2},{4,5},{5,4},{6,7},{7,6},{8,9},{9,8},{10,11... | collective-permute-start | bytes 7077896 | tf_op jit(solution)/shard_map/ppermute | solution.py:267
  60.4 14.0 %collective-permute-start.5 = (bf16[112,2048]{1,0:T(8,128)(2,1)}, bf16[112,2048]{1,0:T(8,128)(2,1)S(1)}, u32[]{:S(2)}, u32[]{:S(2)}) collective-permute-start(bf16[112,2048]{1,0:T(8,128)(2,1)} %collective-permute-done.1), channel_id=1, source_target_pairs={{0,4},{4,8},{8,12},{12,16},{16,20},{20,24},{24,28},{28,0},{1,5},{5... | collective-permute-start | bytes 1376264 | tf_op jit(solution)/shard_map/ppermute | solution.py:250
  61.0 13.3 %collective-permute-start.6 = (bf16[112,2048]{1,0:T(8,128)(2,1)}, bf16[112,2048]{1,0:T(8,128)(2,1)S(1)}, u32[]{:S(2)}, u32[]{:S(2)}) collective-permute-start(bf16[112,2048]{1,0:T(8,128)(2,1)} %collective-permute-done.3), channel_id=1, source_target_pairs={{0,28},{4,0},{8,4},{12,8},{16,12},{20,16},{24,20},{28,24},{1,29},{... | collective-permute-start | bytes 1376264 | tf_op jit(solution)/shard_map/ppermute | solution.py:250
  74.4 36.8 %all-to-all-start.2 = ((bf16[8,64,2048]{2,1,0:T(8,128)(2,1)}), bf16[8,64,2048]{2,1,0:T(8,128)(2,1)S(1)}, u32[]{:S(2)}, u32[]{:S(2)}) async-start(bf16[8,64,2048]{2,1,0:T(8,128)(2,1)} %shard_map.65), calls=%async_computation.2 | async-start | bytes 4194304 | tf_op jit(solution)/shard_map/all_to_all | solution.py:282
  83.9 8.5 %collective-permute-start.7 = (bf16[64,2048]{1,0:T(8,128)(2,1)S(1)}, bf16[64,2048]{1,0:T(8,128)(2,1)S(1)}, u32[]{:S(2)}, u32[]{:S(2)}) collective-permute-start(bf16[64,2048]{1,0:T(8,128)(2,1)S(1)} %slice.6), channel_id=1, source_target_pairs={{0,4},{4,8},{8,12},{12,16},{16,20},{20,24},{24,28},{28,0},{1,5},{5... | collective-permute-start | bytes 786440 | tf_op jit(solution)/shard_map/ppermute | solution.py:250
  85.0 5.5 %collective-permute-start.8 = (bf16[48,2048]{1,0:T(8,128)(2,1)S(1)}, bf16[48,2048]{1,0:T(8,128)(2,1)S(1)}, u32[]{:S(2)}, u32[]{:S(2)}) collective-permute-start(bf16[48,2048]{1,0:T(8,128)(2,1)S(1)} %slice.7), channel_id=1, source_target_pairs={{0,28},{4,0},{8,4},{12,8},{16,12},{20,16},{24,20},{28,24},{1,29},{... | collective-permute-start | bytes 589832 | tf_op jit(solution)/shard_map/ppermute | solution.py:250
  115.6 3.0 %collective-permute-start.9 = (bf16[2,2,64,896]{3,2,1,0:T(8,128)(2,1)S(1)}, bf16[2,2,64,896]{3,2,1,0:T(8,128)(2,1)S(1)}, u32[]{:S(2)}, u32[]{:S(2)}) collective-permute-start(bf16[2,2,64,896]{3,2,1,0:T(8,128)(2,1)S(1)} %dynamic-slice_bitcast_fusion), channel_id=1, source_target_pairs={{0,1},{1,0},{2,3},{3,2},{4,5},{5,4},{6,7},{7,6},{8,9},{9,8},{10,11... | collective-permute-start | bytes 1376264 | tf_op jit(solution)/shard_map/ppermute | solution.py:294
  118.8 7.4 %collective-permute-start.10 = (bf16[64,896]{1,0:T(8,128)(2,1)S(1)}, bf16[64,896]{1,0:T(8,128)(2,1)S(1)}, u32[]{:S(2)}, u32[]{:S(2)}) collective-permute-start(bf16[64,896]{1,0:T(8,128)(2,1)S(1)} %get-tuple-element.28), channel_id=1, source_target_pairs={{0,0},{1,64},{2,128},{3,192},{32,32},{33,96},{34,160},{35,224},{64... | collective-permute-start | bytes 344072 | tf_op jit(solution)/shard_map/ppermute | solution.py:309
  120.7 7.8 %collective-permute-start.11 = (bf16[64,896]{1,0:T(8,128)(2,1)S(1)}, bf16[64,896]{1,0:T(8,128)(2,1)S(1)}, u32[]{:S(2)}, u32[]{:S(2)}) collective-permute-start(bf16[64,896]{1,0:T(8,128)(2,1)S(1)} %get-tuple-element.27), channel_id=1, source_target_pairs={{0,32},{1,96},{2,160},{3,224},{32,0},{33,64},{34,128},{35,192},{64... | collective-permute-start | bytes 344072 | tf_op jit(solution)/shard_map/ppermute | solution.py:309
  123.9 6.1 %collective-permute-start.12 = (bf16[64,896]{1,0:T(8,128)(2,1)S(1)}, bf16[64,896]{1,0:T(8,128)(2,1)S(1)}, u32[]{:S(2)}, u32[]{:S(2)}) collective-permute-start(bf16[64,896]{1,0:T(8,128)(2,1)S(1)} %get-tuple-element.26), channel_id=1, source_target_pairs={{0,128},{1,192},{2,0},{3,64},{32,160},{33,224},{34,32},{35,96},{64... | collective-permute-start | bytes 344072 | tf_op jit(solution)/shard_map/ppermute | solution.py:309
  125.8 6.4 %collective-permute-start.13 = (bf16[64,896]{1,0:T(8,128)(2,1)S(1)}, bf16[64,896]{1,0:T(8,128)(2,1)S(1)}, u32[]{:S(2)}, u32[]{:S(2)}) collective-permute-start(bf16[64,896]{1,0:T(8,128)(2,1)S(1)} %get-tuple-element.25), channel_id=1, source_target_pairs={{0,160},{1,224},{2,32},{3,96},{32,128},{33,192},{34,0},{35,64},{64... | collective-permute-start | bytes 344072 | tf_op jit(solution)/shard_map/ppermute | solution.py:309
